TPU v7x, 128 devices: a whole 4x4x4 slice. The times are simulated.
128 devices in a mesh: dom: 128 (over z, x, y, core).
Axes of the slice: x: 4, y: 4, z: 4, core: 2. Of those that a mesh axis runs over, the one named last changes fastest.
Arguments:
- adjoint: float32 [9, 512, 16384], P(None, None, 'dom'), may hold values from -6 to 6
- snapshots: float32 [2, 3, 512, 16384], P(None, None, None, 'dom'), may hold values from -6 to 6
- density: float32 [16384], P('dom'), may hold values from 1 to 3
- lame_lambda: float32 [16384], P('dom'), may hold values from 0.5 to 2
- lame_mu: float32 [16384], P('dom'), may hold values from 0.5 to 2
- element_order: int32 [16384], P('dom'), may hold values from 3 to 7
- orient: int32 [16384], P('dom'), may hold values from 0 to 3
- new_owner: int32 [16384], P('dom'), may hold values from 0 to 127, as said below
- new_slot: int32 [16384], P('dom'), may hold values from 0 to 127
Outputs:
- adjoint_out: float32 [9, 512, 16384], P(None, None, 'dom')
- gradients: float32 [2, 16384], P(None, 'dom')
Inputs may be any that keep to these rules, and one draw needn't show every extreme that they name: (new_owner, new_slot) is a one-to-one map of all elements onto all (device, slot) pairs; an element whose new owner is its present device keeps its slot; each device sends away exactly 96 elements and receives exactly 96; at most 2 go from one device to any one other device, and exactly 2 to some.
All inputs are finite; a program needn't handle non-finite values.
Results may differ from a plain program's by a relative error of at most 0.0003.
Values sent between devices are 32-bit elements; how exact they have to be, the bound alone decides.
No kernel may reach another device: no remote copies, remote signals or barrier semaphores. Data moves between devices by JAX's collectives and lax.ppermute only.
A program may use at most 256 MiB of HBM per device.

v0:
```python
import jax
import jax.numpy as jnp
from jax import lax
from jax.sharding import PartitionSpec as P

NP = 8
EX = 8
CAP = 2
STEPS = 2


precise = lax.Precision.HIGHEST
step_dt = 0.01
voigt_index = ((3, 8, 7), (8, 4, 6), (7, 6, 5))
stress_pairs = ((0, 0), (1, 1), (2, 2), (1, 2), (0, 2), (0, 1))
trace_forms = ("i,fijke->fjke", "j,fijke->fike", "k,fijke->fije")
lift_forms = ("i,fjke->fijke", "j,fike->fijke", "k,fije->fijke")
slope_forms = ("mi,fijke->fmjke", "mj,fijke->fimke", "mk,fijke->fijme")


def padded(x, sides, width):
    for axis, dim in sides:
        size, length = (lax.axis_size(axis), x.shape[dim])
        up = [(i, (i + 1) % size) for i in range(size - 1)]
        down = [(j, i) for i, j in up]
        last = lax.slice_in_dim(x, length - width, length, axis=dim)
        first = lax.slice_in_dim(x, 0, width, axis=dim)
        before = lax.ppermute(last, axis, up)
        after = lax.ppermute(first, axis, down)
        x = jnp.concatenate([before, x, after], axis=dim)
    return x


def basis_tables(modes_count):
    mode_ranks = jnp.arange(modes_count)
    lower_rank = mode_ranks[:, None]
    higher_rank = mode_ranks[None, :]
    derivative = jnp.where(
        (higher_rank > lower_rank) & ((higher_rank + lower_rank) % 2 == 1),
        2.0 * lower_rank + 1.0,
        0.0,
    ).astype(jnp.float32)
    all_ones = jnp.ones((modes_count,), jnp.float32)
    alternating = jnp.where(mode_ranks % 2 == 0, 1.0, -1.0).astype(jnp.float32)
    lift_scale = mode_ranks.astype(jnp.float32) + 0.5
    mass_weight = 2.0 / (2.0 * mode_ranks.astype(jnp.float32) + 1.0)
    return (derivative, all_ones, alternating, lift_scale, mass_weight)


def frame_tables(element_order, orient, modes_count):
    mode_ranks = jnp.arange(modes_count)
    odd_mode = (mode_ranks % 2 == 1)[:, None]
    sign_x = jnp.where(odd_mode & (orient % 2 == 1)[None, :], -1.0, 1.0).astype(jnp.float32)
    sign_y = jnp.where(odd_mode & (orient // 2 == 1)[None, :], -1.0, 1.0).astype(jnp.float32)
    frame_sign = sign_x[:, None, None, :] * sign_y[None, :, None, :]
    keep_mode = jnp.where(mode_ranks[:, None] <= element_order[None, :], 1.0, 0.0).astype(
        jnp.float32
    )
    order_mask = (
        keep_mode[:, None, None, :] * keep_mode[None, :, None, :] * keep_mode[None, None, :, :]
    )
    return (frame_sign, order_mask)


def apply_flux(values, direction, density, lame_lambda, lame_mu):
    velocity_part = [values[voigt_index[component][direction]] / density for component in range(3)]
    stress_part = []
    for index_b, index_c in stress_pairs:
        summed = jnp.zeros_like(values[0])
        if index_b == index_c:
            summed = lame_lambda * values[direction]
        if index_b == direction:
            summed = summed + lame_mu * values[index_c]
        if index_c == direction:
            summed = summed + lame_mu * values[index_b]
        stress_part.append(summed)
    return jnp.stack(velocity_part + stress_part)


def shifted(values, offset):
    padding = jnp.zeros(values.shape[:-1] + (abs(offset),), values.dtype)
    if offset > 0:
        return jnp.concatenate([values[..., offset:], padding], axis=-1)
    return jnp.concatenate([padding, values[..., :offset]], axis=-1)


def volume_part(wavefield, density, lame_lambda, lame_mu):
    derivative = basis_tables(wavefield.shape[1])[0]
    summed = jnp.zeros_like(wavefield)
    for direction in range(3):
        derived = jnp.einsum(slope_forms[direction], derivative, wavefield, precision=precise)
        summed = summed + apply_flux(derived, direction, density, lame_lambda, lame_mu)
    return summed


def surface_part(
    wavefield, z_upper, z_lower, from_below, from_above, density, lame_lambda, lame_mu
):
    tables = basis_tables(wavefield.shape[1])
    wave_speed = jnp.sqrt((lame_lambda + 2.0 * lame_mu) / density)
    column = jnp.arange(wavefield.shape[-1]) % EX
    keep_right = jnp.where(column != EX - 1, 1.0, 0.0).astype(wavefield.dtype)
    keep_left = jnp.where(column != 0, 1.0, 0.0).astype(wavefield.dtype)
    summed = jnp.zeros_like(wavefield)
    for direction in range(3):
        if direction < 2:
            face_upper = jnp.einsum(trace_forms[direction], tables[1], wavefield, precision=precise)
            face_lower = jnp.einsum(trace_forms[direction], tables[2], wavefield, precision=precise)
        else:
            face_upper = z_upper
            face_lower = z_lower
        if direction == 0:
            outer_upper = shifted(face_lower, 1) * keep_right
            outer_lower = shifted(face_upper, -1) * keep_left
        elif direction == 1:
            outer_upper = shifted(face_lower, EX)
            outer_lower = shifted(face_upper, -EX)
        else:
            outer_upper = from_above
            outer_lower = from_below
        jump_upper = face_upper - outer_upper
        jump_lower = face_lower - outer_lower
        flux_upper = -0.5 * (
            apply_flux(jump_upper, direction, density, lame_lambda, lame_mu)
            + wave_speed * jump_upper
        )
        flux_lower = -0.5 * (
            -apply_flux(jump_lower, direction, density, lame_lambda, lame_mu)
            + wave_speed * jump_lower
        )
        summed = summed + jnp.einsum(
            lift_forms[direction], tables[3], flux_upper, precision=precise
        )
        summed = summed + jnp.einsum(
            lift_forms[direction], tables[3] * tables[2], flux_lower, precision=precise
        )
    return summed


def gradient_terms(wavefield, velocity):
    tables = basis_tables(wavefield.shape[1])
    weight_vec = tables[4]
    mass_cube = (
        weight_vec[:, None, None, None]
        * weight_vec[None, :, None, None]
        * weight_vec[None, None, :, None]
    )
    slopes = [jnp.einsum(slope_forms[d], tables[0], velocity, precision=precise) for d in range(3)]
    divergence = slopes[0][0] + slopes[1][1] + slopes[2][2]
    trace_stress = wavefield[3] + wavefield[4] + wavefield[5]
    lambda_part = jnp.sum(mass_cube * trace_stress * divergence, axis=(0, 1, 2))
    shear_sum = jnp.zeros_like(divergence)
    for position, (index_b, index_c) in enumerate(stress_pairs):
        shear_sum = shear_sum + wavefield[3 + position] * (
            slopes[index_b][index_c] + slopes[index_c][index_b]
        )
    shear_part = jnp.sum(mass_cube * shear_sum, axis=(0, 1, 2))
    return jnp.stack([lambda_part, shear_part])


def layer_rhs(wavefield, volume, density, lame_lambda, lame_mu, order_mask):
    tables = basis_tables(NP)
    volume = volume_part(wavefield, density, lame_lambda, lame_mu)
    z_upper = jnp.einsum(trace_forms[2], tables[1], wavefield, precision=precise)
    z_lower = jnp.einsum(trace_forms[2], tables[2], wavefield, precision=precise)
    rim_traces = padded(jnp.stack([z_lower, z_upper]), (("dom", 0),), 1)
    surface = surface_part(
        wavefield, z_upper, z_lower, rim_traces[0], rim_traces[3], density, lame_lambda, lame_mu
    )
    return (volume + surface) * order_mask


def body(
    adjoint, snapshots, density, lame_lambda, lame_mu, element_order, orient, new_owner, new_slot
):
    devices = lax.axis_size("dom")
    myself = lax.axis_index("dom")
    elements = adjoint.shape[-1]
    columns = devices * CAP
    leaving = new_owner != myself
    dest_hits = (leaving[:, None] & (new_owner[:, None] == jnp.arange(devices)[None, :])).astype(
        jnp.float32
    )
    positions = jnp.arange(elements)
    before_me = (positions[:, None] > positions[None, :]).astype(jnp.float32)
    ranks_to = jnp.dot(before_me, dest_hits, precision=precise)
    own_rank = jnp.sum(ranks_to * dest_hits, axis=1).astype(jnp.int32)
    slot_out = jnp.where(leaving, new_owner * CAP + own_rank, columns)
    source_of = jnp.full((columns,), elements, jnp.int32).at[slot_out].set(positions, mode="drop")
    filled = source_of < elements
    safe_source = jnp.minimum(source_of, elements - 1)
    metadata = jnp.stack(
        [
            density,
            lame_lambda,
            lame_mu,
            element_order.astype(jnp.float32),
            orient.astype(jnp.float32),
            new_slot.astype(jnp.float32),
            jnp.ones_like(density),
        ]
    )
    flat_state = adjoint.reshape(9 * NP * NP * NP, elements)
    flat_snap = snapshots.reshape(STEPS * 3 * NP * NP * NP, elements)

    def outgoing(values):
        return jnp.where(filled[None, :], jnp.take(values, safe_source, axis=1), 0.0)

    send_state = outgoing(flat_state)
    send_snap = outgoing(flat_snap)
    send_meta = outgoing(metadata)
    got_state, got_snap, got_meta = (
        lax.all_to_all(send_state, "dom", split_axis=1, concat_axis=1, tiled=True),
        lax.all_to_all(send_snap, "dom", split_axis=1, concat_axis=1, tiled=True),
        lax.all_to_all(send_meta, "dom", split_axis=1, concat_axis=1, tiled=True),
    )
    got_valid = got_meta[6] > 0.5
    got_slot = got_meta[5].astype(jnp.int32)
    fill_from = (
        jnp.full((elements,), columns, jnp.int32)
        .at[jnp.where(got_valid, got_slot, elements)]
        .set(jnp.arange(columns, dtype=jnp.int32), mode="drop")
    )
    incoming = fill_from < columns
    pick_column = jnp.minimum(fill_from, columns - 1)

    def settle(local_values, received_values):
        return jnp.where(
            incoming[None, :], jnp.take(received_values, pick_column, axis=1), local_values
        )

    settled_meta = settle(metadata, got_meta)
    settled_state = settle(flat_state, got_state).reshape(9, NP, NP, NP, elements)
    here_density = settled_meta[0]
    here_lambda = settled_meta[1]
    here_mu = settled_meta[2]
    here_order = settled_meta[3].astype(jnp.int32)
    here_orient = settled_meta[4].astype(jnp.int32)
    frame_sign, order_mask = frame_tables(here_order, here_orient, NP)
    wavefield = frame_sign * order_mask * settled_state
    settled_snap = settle(flat_snap, got_snap).reshape(STEPS, 3, NP, NP, NP, elements)
    velocity = frame_sign * order_mask * settled_snap
    first_volume = None
    gradient_sum = jnp.zeros((2, elements), jnp.float32)
    for step_index in range(STEPS):
        given = first_volume if step_index == 0 else None
        section_one = wavefield + step_dt * layer_rhs(
            wavefield, given, here_density, here_lambda, here_mu, order_mask
        )
        section_two = section_one + step_dt * layer_rhs(
            section_one, None, here_density, here_lambda, here_mu, order_mask
        )
        wavefield = 0.5 * (wavefield + section_two)
        gradient_sum = gradient_sum + step_dt * gradient_terms(wavefield, velocity[step_index])
    adjoint_out = (frame_sign * wavefield).reshape(9, NP * NP * NP, elements)
    return (adjoint_out, gradient_sum)


def solution(mesh):
    in_specs = (
        P(None, None, "dom"),
        P(None, None, None, "dom"),
        P("dom"),
        P("dom"),
        P("dom"),
        P("dom"),
        P("dom"),
        P("dom"),
        P("dom"),
    )
    out_specs = (P(None, None, "dom"), P(None, "dom"))
    return jax.shard_map(body, mesh=mesh, in_specs=in_specs, out_specs=out_specs, check_vma=False)
```

profile of v0, /device:TPU:32, one launch (start us, length us, event | category | flops | bytes accessed | tf_op | source)
XLA Modules:
  0.0 350.8 jit_solution(1924552606292518073)
XLA Ops:
  8.1 10.2 %all-to-all-start = ((f32[7,128,2]{0,2,1:T(2,128)}), f32[7,128,2]{0,2,1:T(2,128)S(1)}, u32[]{:S(2)}, u32[]{:S(2)}) async-start(f32[7,128,2]{0,2,1:T(2,128)} %select_select_fusion.2), calls=%async_computation | async-start | bytes 262144 | tf_op jit(solution)/shard_map/all_to_all | solution.py:215
  20.2 3.3 gather_fusion.4
  23.5 3.7 %gather.42 = f32[3072,128,2]{0,2,1:T(2,128)S(1)} reshape(f32[3072,256]{0,1:T(8,128)} %bitcast.420) | data formatting | bytes 6291456 | tf_op jit(solution)/shard_map/jit(_take)/gather | solution.py:207
  27.2 4.5 %select_select_fusion.1 = f32[3072,128,2]{0,2,1:T(2,128)} fusion(f32[3072,128,2]{0,2,1:T(2,128)S(1)} %gather.42, pred[128,2]{1,0:T(8,128)(4,1)S(1)} %broadcast_in_dim.339, pred[128,2]{1,0:T(8,128)(4,1)S(1)} %broadcast_in_dim.337), kind=kLoop, calls=%fused_computation.9 | loop fusion | flops 1572864 | bytes 6291968 | tf_op jit(solution)/shard_map/jit(_where)/select_n | solution.py:207
  31.7 10.5 %all-to-all-start.2 = ((f32[3072,128,2]{0,2,1:T(2,128)}), f32[3072,128,2]{0,2,1:T(2,128)}, u32[]{:S(2)}, u32[]{:S(2)}) async-start(f32[3072,128,2]{0,2,1:T(2,128)} %select_select_fusion.1), calls=%async_computation.2 | async-start | bytes 6291456 | tf_op jit(solution)/shard_map/all_to_all | solution.py:214
  44.3 4.3 %gather_fusion.2 = f32[256,4608]{1,0:T(8,128)} fusion(f32[4608,128]{0,1:T(8,128)S(1)} %copy.212, s32[1024]{0:T(1024)S(1)} %pad_clamp_fusion.1), kind=kCustom, calls=%fused_computation.2 | custom fusion | bytes 9438208 | tf_op jit(solution)/shard_map/jit(_take)/gather | solution.py:207
  48.6 6.2 %gather.38 = f32[4608,128,2]{0,2,1:T(2,128)} reshape(f32[4608,256]{0,1:T(8,128)} %bitcast.419) | data formatting | bytes 9437184 | tf_op jit(solution)/shard_map/jit(_take)/gather | solution.py:207
  55.0 10.3 %select_select_fusion = f32[4608,128,2]{0,2,1:T(2,128)} fusion(f32[4608,128,2]{0,2,1:T(2,128)} %gather.38, pred[128,2]{1,0:T(8,128)(4,1)S(1)} %broadcast_in_dim.339, pred[128,2]{1,0:T(8,128)(4,1)S(1)} %broadcast_in_dim.337), kind=kLoop, calls=%fused_computation.8 | loop fusion | flops 2359296 | bytes 9437696 | tf_op jit(solution)/shard_map/jit(_where)/select_n | solution.py:207
  65.4 2.5 fusion.110
  68.1 15.0 %all-to-all-done.2 = f32[3072,128,2]{0,2,1:T(2,128)} async-done(((f32[3072,128,2]{0,2,1:T(2,128)}), f32[3072,128,2]{0,2,1:T(2,128)}, u32[]{:S(2)}, u32[]{:S(2)}) %all-to-all-start.2) | async-done | bytes 3145760 | tf_op jit(solution)/shard_map/all_to_all | solution.py:214
  83.0 6.8 %all-to-all-start.1 = ((f32[4608,128,2]{0,2,1:T(2,128)}), f32[4608,128,2]{0,2,1:T(2,128)}, u32[]{:S(2)}, u32[]{:S(2)}) async-start(f32[4608,128,2]{0,2,1:T(2,128)} %select_select_fusion), calls=%async_computation.1 | async-start | bytes 9437184 | tf_op jit(solution)/shard_map/all_to_all | solution.py:213
  93.5 3.9 %all_to_all.23 = f32[3072,256]{0,1:T(8,128)S(1)} reshape(f32[3072,128,2]{0,2,1:T(2,128)} %all-to-all-done.2) | data formatting | bytes 6291456 | tf_op jit(solution)/shard_map/all_to_all | solution.py:214
  97.4 2.2 gather_fusion.5
  101.7 3.3 fusion.80
  117.3 30.0 %all-to-all-done.1 = f32[4608,128,2]{0,2,1:T(2,128)} async-done(((f32[4608,128,2]{0,2,1:T(2,128)}), f32[4608,128,2]{0,2,1:T(2,128)}, u32[]{:S(2)}, u32[]{:S(2)}) %all-to-all-start.1) | async-done | bytes 4718624 | tf_op jit(solution)/shard_map/all_to_all | solution.py:213
  147.3 6.7 %all_to_all.21 = f32[4608,256]{0,1:T(8,128)} reshape(f32[4608,128,2]{0,2,1:T(2,128)} %all-to-all-done.1) | data formatting | bytes 9437184 | tf_op jit(solution)/shard_map/all_to_all | solution.py:213
  154.0 4.8 %gather_fusion.3 = f32[128,4608]{1,0:T(8,128)S(1)} fusion(f32[4608,256]{0,1:T(8,128)} %all_to_all.21, s32[1024]{0:T(1024)S(1)} %pad_clamp_fusion), kind=kCustom, calls=%fused_computation.3 | custom fusion | bytes 4719104 | tf_op jit(solution)/shard_map/jit(_take)/gather | solution.py:229
  160.7 6.3 %fusion.22 = f32[9,8,8,8,128]{4,1,3,2,0:T(8,128)S(1)} fusion(f32[9,8,8,8,128]{4,3,2,1,0:T(8,128)} %bitcast.423, f32[9,8,8,8,128]{4,3,2,1,0:T(8,128)} %bitcast.424, f32[8,8,8,128]{3,0,2,1:T(8,128)} %get-tuple-element.23, pred[128]{0:T(512)(128)(4,1)S(1)} %get-tuple-element.11, pred[128]{0:T(512)(128)(4,1)S(1)} %get-tuple-element.287), kind=kLoop, calls=%fused_computation.62 | loop fusion | flops 1769472 | bytes 7340288 | tf_op jit(solution)/shard_map/mul | solution.py:240
  167.1 2.2 convolution_bitcast_fusion
  169.3 3.5 %fusion.69 = f32[9,8,8,128,8]{3,4,2,1,0:T(8,128)S(1)} fusion(f32[9,8,8,8,128]{4,1,3,2,0:T(8,128)S(1)} %fusion.22, f32[8]{0:T(128)S(1)} %multiply_add_fusion), kind=kOutput, calls=%fused_computation.111 | convolution fusion | flops 56624128 | bytes 4718624 | tf_op jit(solution)/shard_map/mj,fijke->fimke/dot_general | solution.py:91
  172.9 2.7 fusion.63
  175.6 2.1 fusion.216
  177.7 2.1 fusion.197
  179.8 3.2 fusion.67
  183.0 3.2 fusion.65
  186.2 2.6 fusion.61
  188.8 2.2 fusion.59
  195.6 2.1 collective-permute-start
  197.7 2.4 collective-permute-start.1
  201.9 8.0 %collective-permute-done.1 = f32[1,9,8,8,128]{4,3,2,1,0:T(8,128)S(1)} collective-permute-done((f32[1,9,8,8,128]{4,3,2,1,0:T(8,128)S(1)}, f32[1,9,8,8,128]{4,3,2,1,0:T(8,128)S(1)}, u32[]{:S(2)}, u32[]{:S(2)}) %collective-permute-start.1) | collective-permute-done | bytes 294944 | tf_op jit(solution)/shard_map/ppermute | solution.py:28
  212.9 3.5 %fusion.57 = f32[9,8,8,128,8]{3,4,2,1,0:T(8,128)S(1)} fusion(f32[9,8,8,8,128]{4,1,3,2,0:T(8,128)S(1)} %fusion.21, f32[8]{0:T(128)S(1)} %multiply_add_fusion), kind=kOutput, calls=%fused_computation.99 | convolution fusion | flops 56624128 | bytes 4718624 | tf_op jit(solution)/shard_map/mj,fijke->fimke/dot_general | solution.py:91
  216.4 2.2 fusion.71
  218.7 2.5 fusion.51
  221.2 2.3 fusion.214
  223.5 2.1 fusion.195
  225.6 3.2 fusion.55
  228.8 3.2 fusion.53
  232.1 2.6 fusion.49
  234.7 2.2 fusion.47
  243.1 2.4 collective-permute-start.3
  247.3 8.0 %collective-permute-done.3 = f32[1,9,8,8,128]{4,3,2,1,0:T(8,128)S(1)} collective-permute-done((f32[1,9,8,8,128]{4,3,2,1,0:T(8,128)S(1)}, f32[1,9,8,8,128]{4,3,2,1,0:T(8,128)S(1)}, u32[]{:S(2)}, u32[]{:S(2)}) %collective-permute-start.3) | collective-permute-done | bytes 294944 | tf_op jit(solution)/shard_map/ppermute | solution.py:28
  256.5 2.4 fusion.18
  258.9 3.5 %fusion.45 = f32[9,8,8,128,8]{3,4,2,1,0:T(8,128)S(1)} fusion(f32[9,8,8,8,128]{4,1,3,2,0:T(8,128)S(1)} %fusion.18, f32[8]{0:T(128)S(1)} %multiply_add_fusion), kind=kOutput, calls=%fused_computation.87 | convolution fusion | flops 56624128 | bytes 4718624 | tf_op jit(solution)/shard_map/mj,fijke->fimke/dot_general | solution.py:91
  262.5 2.3 fusion.74
  264.8 2.5 fusion.39
  267.2 2.1 fusion.212
  269.3 2.5 fusion.193
  271.9 3.2 fusion.43
  275.1 3.2 fusion.41
  278.3 2.2 fusion.37
  280.5 2.2 fusion.35
  289.2 2.4 collective-permute-start.5
  293.5 8.0 %collective-permute-done.5 = f32[1,9,8,8,128]{4,3,2,1,0:T(8,128)S(1)} collective-permute-done((f32[1,9,8,8,128]{4,3,2,1,0:T(8,128)S(1)}, f32[1,9,8,8,128]{4,3,2,1,0:T(8,128)S(1)}, u32[]{:S(2)}, u32[]{:S(2)}) %collective-permute-start.5) | collective-permute-done | bytes 294944 | tf_op jit(solution)/shard_map/ppermute | solution.py:28
  304.9 3.2 fusion.29
  308.1 3.2 fusion.31
  311.3 2.5 fusion.210
  315.9 2.2 fusion.25
  318.1 2.2 fusion.23
  320.3 3.5 %fusion.33 = f32[9,8,8,128,8]{3,4,2,1,0:T(8,128)S(1)} fusion(f32[9,8,8,8,128]{4,1,3,2,0:T(8,128)S(1)} %fusion.16, f32[8]{0:T(128)S(1)} %multiply_add_fusion), kind=kOutput, calls=%fused_computation.75 | convolution fusion | flops 56624128 | bytes 4718624 | tf_op jit(solution)/shard_map/mj,fijke->fimke/dot_general | solution.py:91
  323.9 2.3 fusion.77
  326.2 2.5 fusion.27
  331.3 2.4 collective-permute-start.7
  337.5 6.0 %collective-permute-done.7 = f32[1,9,8,8,128]{4,3,2,1,0:T(8,128)S(1)} collective-permute-done((f32[1,9,8,8,128]{4,3,2,1,0:T(8,128)S(1)}, f32[1,9,8,8,128]{4,3,2,1,0:T(8,128)S(1)}, u32[]{:S(2)}, u32[]{:S(2)}) %collective-permute-start.7) | collective-permute-done | bytes 294944 | tf_op jit(solution)/shard_map/ppermute | solution.py:28
  344.7 2.4 broadcast_multiply_fusion.1
  (311 shorter events, 73.2 us)
Async XLA Ops:
  8.1 23.6 %all-to-all-start = ((f32[7,128,2]{0,2,1:T(2,128)}), f32[7,128,2]{0,2,1:T(2,128)S(1)}, u32[]{:S(2)}, u32[]{:S(2)}) async-start(f32[7,128,2]{0,2,1:T(2,128)} %select_select_fusion.2), calls=%async_computation | async-start | bytes 262144 | tf_op jit(solution)/shard_map/all_to_all | solution.py:215
  31.7 51.3 %all-to-all-start.2 = ((f32[3072,128,2]{0,2,1:T(2,128)}), f32[3072,128,2]{0,2,1:T(2,128)}, u32[]{:S(2)}, u32[]{:S(2)}) async-start(f32[3072,128,2]{0,2,1:T(2,128)} %select_select_fusion.1), calls=%async_computation.2 | async-start | bytes 6291456 | tf_op jit(solution)/shard_map/all_to_all | solution.py:214
  83.0 64.3 %all-to-all-start.1 = ((f32[4608,128,2]{0,2,1:T(2,128)}), f32[4608,128,2]{0,2,1:T(2,128)}, u32[]{:S(2)}, u32[]{:S(2)}) async-start(f32[4608,128,2]{0,2,1:T(2,128)} %select_select_fusion), calls=%async_computation.1 | async-start | bytes 9437184 | tf_op jit(solution)/shard_map/all_to_all | solution.py:213
  99.7 2.0 copy-start
  195.6 6.3 %collective-permute-start = (f32[1,9,8,8,128]{4,3,2,1,0:T(8,128)S(1)}, f32[1,9,8,8,128]{4,3,2,1,0:T(8,128)S(1)}, u32[]{:S(2)}, u32[]{:S(2)}) collective-permute-start(f32[1,9,8,8,128]{4,3,2,1,0:T(8,128)S(1)} %bitcast.535), channel_id=1, source_target_pairs={{1,0},{2,1},{3,2},{4,3},{5,4},{6,5},{7,6},{8,7},{9,8},{10,9},{11,1... | collective-permute-start | bytes 884744 | tf_op jit(solution)/shard_map/ppermute | solution.py:29
  197.7 12.3 %collective-permute-start.1 = (f32[1,9,8,8,128]{4,3,2,1,0:T(8,128)S(1)}, f32[1,9,8,8,128]{4,3,2,1,0:T(8,128)S(1)}, u32[]{:S(2)}, u32[]{:S(2)}) collective-permute-start(f32[1,9,8,8,128]{4,3,2,1,0:T(8,128)S(1)} %bitcast.537), channel_id=1, source_target_pairs={{0,1},{1,2},{2,3},{3,4},{4,5},{5,6},{6,7},{7,8},{8,9},{9,10},{10,1... | collective-permute-start | bytes 884744 | tf_op jit(solution)/shard_map/ppermute | solution.py:28
  241.2 6.1 %collective-permute-start.2 = (f32[1,9,8,8,128]{4,3,2,1,0:T(8,128)S(1)}, f32[1,9,8,8,128]{4,3,2,1,0:T(8,128)S(1)}, u32[]{:S(2)}, u32[]{:S(2)}) collective-permute-start(f32[1,9,8,8,128]{4,3,2,1,0:T(8,128)S(1)} %bitcast.545), channel_id=1, source_target_pairs={{1,0},{2,1},{3,2},{4,3},{5,4},{6,5},{7,6},{8,7},{9,8},{10,9},{11,1... | collective-permute-start | bytes 884744 | tf_op jit(solution)/shard_map/ppermute | solution.py:29
  243.1 12.3 %collective-permute-start.3 = (f32[1,9,8,8,128]{4,3,2,1,0:T(8,128)S(1)}, f32[1,9,8,8,128]{4,3,2,1,0:T(8,128)S(1)}, u32[]{:S(2)}, u32[]{:S(2)}) collective-permute-start(f32[1,9,8,8,128]{4,3,2,1,0:T(8,128)S(1)} %bitcast.549), channel_id=1, source_target_pairs={{0,1},{1,2},{2,3},{3,4},{4,5},{5,6},{6,7},{7,8},{8,9},{9,10},{10,1... | collective-permute-start | bytes 884744 | tf_op jit(solution)/shard_map/ppermute | solution.py:28
  286.8 5.0 %copy-start.2 = (f32[3,8,8,128,8]{3,1,4,2,0:T(8,128)S(1)}, f32[3,8,8,128,8]{3,1,4,2,0:T(8,128)}, u32[]{:S(2)}) copy-start(f32[3,8,8,128,8]{3,1,4,2,0:T(8,128)} %copy.530) | copy-start | bytes 2359300
  286.8 5.0 %copy-start.5 = (f32[3,8,8,8,128]{4,1,3,2,0:T(8,128)S(1)}, f32[3,8,8,8,128]{4,1,3,2,0:T(8,128)}, u32[]{:S(2)}) copy-start(f32[3,8,8,8,128]{4,1,3,2,0:T(8,128)} %convolution_bitcast_fusion.2) | copy-start | bytes 2359300
  287.2 6.3 %collective-permute-start.4 = (f32[1,9,8,8,128]{4,3,2,1,0:T(8,128)S(1)}, f32[1,9,8,8,128]{4,3,2,1,0:T(8,128)S(1)}, u32[]{:S(2)}, u32[]{:S(2)}) collective-permute-start(f32[1,9,8,8,128]{4,3,2,1,0:T(8,128)S(1)} %bitcast.543), channel_id=1, source_target_pairs={{1,0},{2,1},{3,2},{4,3},{5,4},{6,5},{7,6},{8,7},{9,8},{10,9},{11,1... | collective-permute-start | bytes 884744 | tf_op jit(solution)/shard_map/ppermute | solution.py:29
  289.2 12.3 %collective-permute-start.5 = (f32[1,9,8,8,128]{4,3,2,1,0:T(8,128)S(1)}, f32[1,9,8,8,128]{4,3,2,1,0:T(8,128)S(1)}, u32[]{:S(2)}, u32[]{:S(2)}) collective-permute-start(f32[1,9,8,8,128]{4,3,2,1,0:T(8,128)S(1)} %bitcast.547), channel_id=1, source_target_pairs={{0,1},{1,2},{2,3},{3,4},{4,5},{5,6},{6,7},{7,8},{8,9},{9,10},{10,1... | collective-permute-start | bytes 884744 | tf_op jit(solution)/shard_map/ppermute | solution.py:28
  329.4 8.1 %collective-permute-start.6 = (f32[1,9,8,8,128]{4,3,2,1,0:T(8,128)S(1)}, f32[1,9,8,8,128]{4,3,2,1,0:T(8,128)S(1)}, u32[]{:S(2)}, u32[]{:S(2)}) collective-permute-start(f32[1,9,8,8,128]{4,3,2,1,0:T(8,128)S(1)} %bitcast.539), channel_id=1, source_target_pairs={{1,0},{2,1},{3,2},{4,3},{5,4},{6,5},{7,6},{8,7},{9,8},{10,9},{11,1... | collective-permute-start | bytes 884744 | tf_op jit(solution)/shard_map/ppermute | solution.py:29
  331.3 12.3 %collective-permute-start.7 = (f32[1,9,8,8,128]{4,3,2,1,0:T(8,128)S(1)}, f32[1,9,8,8,128]{4,3,2,1,0:T(8,128)S(1)}, u32[]{:S(2)}, u32[]{:S(2)}) collective-permute-start(f32[1,9,8,8,128]{4,3,2,1,0:T(8,128)S(1)} %bitcast.541), channel_id=1, source_target_pairs={{0,1},{1,2},{2,3},{3,4},{4,5},{5,6},{6,7},{7,8},{8,9},{9,10},{10,1... | collective-permute-start | bytes 884744 | tf_op jit(solution)/shard_map/ppermute | solution.py:28
  344.7 2.4 copy-start.1
  344.7 2.4 copy-start.3
  344.7 2.4 copy-start.4
where the time goes:
time: 357 us; the launch traced here: 351 us
  matrix products  104 us (29%)
  waiting for transfers between devices  79.4 us (22%)
  local copies, waits for them, and re-layouts  69.1 us (19%)
  other arithmetic  50.1 us (14%)
  starting transfers between devices  45.1 us (13%)
    dot_general x12, matrix products, volume_part(): jnp.einsum(slope_forms[direction], derivative, wavefield, precision=precise)  33.3 us
    ppermute x4, waiting for transfers between devices, padded(): before = lax.ppermute(last, axis, up)  30 us
    all_to_all x1, waiting for transfers between devices, body(): lax.all_to_all(send_state, 'dom', split_axis=1, concat_axis=1, tiled=True)  30 us
    gather x5, local copies, waits for them, and re-layouts, outgoing(): jnp.take(values, safe_source, axis=1)  18.3 us
    unnamed x8, matrix products  17.8 us
    select_n x3, other arithmetic, outgoing(): jnp.where(filled[None, :], jnp.take(values, safe_source, axis=1), 0.0)  15.8 us
    all_to_all x1, waiting for transfers between devices, body(): lax.all_to_all(send_snap, 'dom', split_axis=1, concat_axis=1, tiled=True)  15 us
    dot_general x4, matrix products, surface_part(): jnp.einsum(trace_forms[direction], tables[2], wavefield, precision=precise)  12.8 us
  transfers between devices with their start and end apart: 11, of which 9 were waited for; matrix products, arithmetic and copies ran while one was open for 19% of the time, Pallas kernels for 0%

commit v1 on v0

v1 whole, which is shorter than its diff:
```python
import jax
import jax.numpy as jnp
from jax import lax
from jax.experimental import pallas as pl
from jax.experimental.pallas import tpu as pltpu
from jax.sharding import PartitionSpec as P

NP = 8
NM = 512
EX = 8
NE = 128
STEPS = 2
DEV = 128
FIELDS = 9
SNAPS = 6
BLOCK_A = 10
BLOCK_B = 5
DT = 0.01
VMEM_LIMIT = 16 * 1024 * 1024
f32 = jnp.float32
bf16 = jnp.bfloat16

VOIGT = ((3, 8, 7), (8, 4, 6), (7, 6, 5))
ACTIVE = tuple((0, 1, 2) + VOIGT[a] for a in range(3))


def split3(x):
    high = x.astype(bf16)
    rest = x - high.astype(f32)
    middle = rest.astype(bf16)
    low = (rest - middle.astype(f32)).astype(bf16)
    return high, middle, low


def call(kernel, operands, out_shape, scratch_shapes=(), flops=0, nbytes=0):
    return pl.pallas_call(
        kernel,
        in_specs=[
            pl.BlockSpec(memory_space=pltpu.SMEM if x.shape == (1,) else pltpu.VMEM)
            for x in operands
        ],
        out_specs=[pl.BlockSpec(memory_space=pltpu.VMEM) for _ in out_shape],
        out_shape=out_shape,
        scratch_shapes=list(scratch_shapes),
        compiler_params=pltpu.CompilerParams(vmem_limit_bytes=VMEM_LIMIT),
        cost_estimate=pl.CostEstimate(flops=flops, bytes_accessed=nbytes, transcendentals=0),
    )(*operands)


def array(*shape, dtype=f32):
    return jax.ShapeDtypeStruct(shape, dtype)


def scatter_rows(hot, x, out_ref, row):
    parts = jnp.concatenate(split3(x), axis=1)
    hots = jnp.concatenate([hot, hot, hot], axis=1)
    rows = lax.dot_general(hots, parts, (((1,), (1,)), ((), ())), preferred_element_type=f32)
    for r in range(2):
        for q in range(4):
            out_ref[:, row + r * 4 + q, :] = rows[r * DEV : (r + 1) * DEV, q * 128 : (q + 1) * 128]


def pack_a_kernel(me_ref, owner_ref, meta_ref, adj_ref, snap_ref, out_ref, hot_ref):
    owner_row = owner_ref[...]
    owner_all = jnp.broadcast_to(owner_row, (NE, NE))
    owner_col = jnp.transpose(owner_all)
    at0 = lax.broadcasted_iota(jnp.int32, (NE, NE), 0)
    at1 = lax.broadcasted_iota(jnp.int32, (NE, NE), 1)
    earlier = jnp.where((owner_col == owner_all) & (at0 < at1), 1.0, 0.0)
    rank = jnp.sum(earlier, axis=0, keepdims=True)
    dest = jnp.where(owner_row != me_ref[0], owner_row, -1)
    for r in range(2):
        chosen = (at0 == dest) & (rank == float(r))
        hot_ref[r * DEV : (r + 1) * DEV, :] = jnp.where(chosen, 1.0, 0.0).astype(bf16)

    @pl.loop(0, FIELDS)
    def _(g):
        scatter_rows(hot_ref[...], adj_ref[g], out_ref, pl.multiple_of(g * 8, 8))

    first = jnp.where(
        lax.broadcasted_iota(jnp.int32, (8, NE), 0) < 6, meta_ref[...], snap_ref[0, 0:8, :]
    )
    block = jnp.concatenate([first, snap_ref[0, 8:, :]], axis=0)
    scatter_rows(hot_ref[...], block, out_ref, FIELDS * 8)


def pack_b_kernel(hot_ref, snap_ref, out_ref):
    row0 = lax.broadcasted_iota(jnp.int32, (8, NE), 0) == 0

    @pl.loop(0, BLOCK_B)
    def _(g):
        moved = snap_ref[0, pl.ds(g + 1, 1), :]
        first = jnp.where(row0, jnp.broadcast_to(moved, (8, NE)), snap_ref[g + 1, 0:8, :])
        block = jnp.concatenate([first, snap_ref[g + 1, 8:, :]], axis=0)
        scatter_rows(hot_ref[...], block, out_ref, pl.multiple_of(g * 8, 8))


def pack(me, owner, meta, adjoint, snaps):
    send_a, hot = call(
        pack_a_kernel,
        (me, owner, meta, adjoint, snaps),
        [array(DEV, BLOCK_A * 8, 128), array(2 * DEV, NE, dtype=bf16)],
    )
    (send_b,) = call(pack_b_kernel, (hot, snaps), [array(DEV, BLOCK_B * 8, 128)])
    return send_a, send_b


def gather_elements(pick, got_ref, row):
    slots = [
        jnp.concatenate([got_ref[:, row + r * 4 + q, :] for q in range(4)], axis=1) for r in range(2)
    ]
    parts = jnp.concatenate(split3(jnp.concatenate(slots, axis=0)), axis=0)
    picks = jnp.concatenate([pick, pick, pick], axis=1)
    placed = lax.dot_general(picks, parts, (((1,), (0,)), ((), ())), preferred_element_type=f32)
    return jnp.transpose(placed)


def mode_indices(shape):
    mode = lax.broadcasted_iota(jnp.int32, shape, 0)
    return mode // 64, (mode // 8) % 8, mode % 8


def mask_and_sign(order, orient):
    i, j, k = mode_indices((NM, NE))
    highest = jnp.maximum(jnp.maximum(i, j), k).astype(f32)
    flip_x = (orient == 1.0) | (orient == 3.0)
    flip_y = orient >= 2.0
    sign_x = jnp.where(i % 2 == 1, jnp.where(flip_x, -1.0, 1.0), 1.0)
    sign_y = jnp.where(j % 2 == 1, jnp.where(flip_y, -1.0, 1.0), 1.0)
    return jnp.where(highest <= order, sign_x * sign_y, 0.0)


def face_traces(modes, row):
    low4, low2, even = row < 4, row % 4 < 2, row % 2 == 0
    fours = []
    for j in range(4):
        first, second = modes[j], modes[j + 4]
        other = jnp.where(low4, second, first)
        fours.append(jnp.where(low4, first, second) + pltpu.roll(other, 4, 0))
    twos = []
    for j in range(2):
        first, second = fours[j], fours[j + 2]
        twos.append(
            jnp.where(low2, first + pltpu.roll(first, 6, 0), second + pltpu.roll(second, 2, 0))
        )
    first, second = twos
    next_first, next_second = pltpu.roll(first, 7, 0), pltpu.roll(second, 1, 0)
    upper = jnp.where(even, first + next_first, second + next_second)
    lower = jnp.where(even, first - next_first, next_second - second)
    return upper, lower


def place_kernel(
    me_ref, owner_ref, meta_ref, got_ref, adj_ref,
    wave_ref, upper_ref, lower_ref, rows_ref, pick_ref, head_ref, frame_ref,
):
    keep = owner_ref[...] == me_ref[0]
    at1 = lax.broadcasted_iota(jnp.int32, (DEV, NE), 1).astype(f32)
    for r in range(2):
        slot = got_ref[:, FIELDS * 8 + r * 4, 5:6]
        chosen = jnp.where(slot == at1 + 1.0, 1.0, 0.0)
        pick_ref[:, r * DEV : (r + 1) * DEV] = jnp.transpose(chosen).astype(bf16)
    block = gather_elements(pick_ref[...], got_ref, FIELDS * 8)
    head_ref[...] = block
    meta = jnp.where(keep, meta_ref[...], block[0:8])
    density, lam, mu = meta[0:1], meta[1:2], meta[2:3]
    order, orient = meta[3:4], meta[4:5]
    rows_ref[0:1, :] = 1.0 / density
    rows_ref[1:2, :] = lam
    rows_ref[2:3, :] = mu
    rows_ref[3:4, :] = jnp.sqrt((lam + 2.0 * mu) / density)
    rows_ref[4:5, :] = order
    rows_ref[5:6, :] = orient
    rows_ref[6:8, :] = jnp.zeros((2, NE), f32)
    frame_ref[...] = mask_and_sign(order, orient)

    @pl.loop(0, FIELDS)
    def _(f):
        block = gather_elements(pick_ref[...], got_ref, pl.multiple_of(f * 8, 8))
        wave = jnp.where(keep, adj_ref[f], block) * frame_ref[...]
        wave = wave.reshape(64, NP, NE)
        wave_ref[f] = wave
        row = lax.broadcasted_iota(jnp.int32, (NP, NE), 0)
        for i in range(NP):
            upper, lower = face_traces([wave[i * NP + j] for j in range(NP)], row)
            upper_ref[f, i * NP : (i + 1) * NP, :] = upper
            lower_ref[f, i * NP : (i + 1) * NP, :] = lower


def place(me, owner, meta, got, adjoint):
    return call(
        place_kernel,
        (me, owner, meta, got, adjoint),
        [
            array(FIELDS, 64, NP, NE),
            array(FIELDS, 64, NE),
            array(FIELDS, 64, NE),
            array(8, NE),
            array(NE, 2 * DEV, dtype=bf16),
            array(NM, NE),
        ],
        [pltpu.VMEM((NM, NE), f32)],
    )


def materials(rows_ref):
    full = lambda r: jnp.broadcast_to(rows_ref[r : r + 1, :], (NP, NE))
    return full(0), full(1), full(2), full(3)


def apply_b(values, direction, rinv, lam, mu):
    out = [None] * FIELDS
    for c in range(3):
        out[c] = values[VOIGT[c][direction]] * rinv
    spread = lam * values[direction]
    for b in range(3):
        out[3 + b] = spread
    out[3 + direction] = spread + 2.0 * mu * values[direction]
    for c in range(3):
        if c != direction:
            out[VOIGT[c][direction]] = mu * values[c]
    return out


def face_flux(total, difference, direction, rinv, lam, mu, speed):
    even_b = apply_b(difference, direction, rinv, lam, mu)
    odd_b = apply_b(total, direction, rinv, lam, mu)
    even, odd = [], []
    for f in range(FIELDS):
        pen_even, pen_odd = speed * total[f], speed * difference[f]
        if even_b[f] is not None:
            pen_even, pen_odd = pen_even + even_b[f], pen_odd + odd_b[f]
        even.append(-0.25 * pen_even)
        odd.append(-0.25 * pen_odd)
    return even, odd


def local_flux(evens, odds, direction, offset, keep_up, keep_down, rinv, lam, mu, speed):
    total, difference = [], []
    for f in range(FIELDS):
        upper, lower = evens[f] + odds[f], evens[f] - odds[f]
        above = pltpu.roll(lower, NE - offset, 1) * keep_up
        below = pltpu.roll(upper, offset, 1) * keep_down
        total.append((upper - above) + (lower - below))
        difference.append((upper - above) - (lower - below))
    return face_flux(total, difference, direction, rinv, lam, mu, speed)


def lane_keeps():
    lane = lax.broadcasted_iota(jnp.int32, (NP, NE), 1)
    one = lambda cond: jnp.where(cond, 1.0, 0.0)
    column = lane % EX
    return (
        (one(column != EX - 1), one(column != 0)),
        (one(lane < NE - EX), one(lane >= EX)),
    )


def mode_rows():
    k = lax.broadcasted_iota(jnp.int32, (NP, NE), 0)
    one = lambda cond: jnp.where(cond, 1.0, 0.0)
    return one(k < 7), one(k < 6), one(k < 4), (2 * k + 1).astype(f32)


def sums_above(x, keep1, keep2, keep4):
    x = pltpu.roll(x, 7, 0) * keep1
    x = x + pltpu.roll(x, 6, 0) * keep2
    return x + pltpu.roll(x, 4, 0) * keep4


def inner_kernel(wave_ref, rows_ref, out_ref, flux_ref, run_ref, fluxy_ref):
    rinv, lam, mu, speed = materials(rows_ref)
    keeps_x, keeps_y = lane_keeps()
    keep1, keep2, keep4, factor_z = mode_rows()
    run_ref[...] = jnp.zeros_like(run_ref)

    @pl.loop(0, NP)
    def _(g):
        i = NP - 1 - g
        parity = lax.rem(i, 2)
        factor_x = (2 * i + 1).astype(f32)

        evens, odds = [], []
        for f in range(FIELDS):
            col = [wave_ref[f, i * NP + j] for j in range(NP)]
            evens.append((col[0] + col[2]) + (col[4] + col[6]))
            odds.append((col[1] + col[3]) + (col[5] + col[7]))
        even, odd = local_flux(evens, odds, 1, EX, *keeps_y, rinv, lam, mu, speed)
        for f in range(FIELDS):
            fluxy_ref[0, f] = even[f]
            fluxy_ref[1, f] = odd[f]

        sums_y = {f: [None, None] for f in ACTIVE[1]}
        for j in range(NP - 1, -1, -1):
            here = [wave_ref[f, i * NP + j] for f in range(FIELDS)]
            slope = [{}, {}, {}]
            for f in ACTIVE[0]:
                slope[0][f] = factor_x * run_ref[parity, f, j]
            for f in ACTIVE[1]:
                if sums_y[f][j % 2] is not None:
                    slope[1][f] = (2.0 * j + 1.0) * sums_y[f][j % 2]
            for f in ACTIVE[2]:
                slope[2][f] = factor_z * sums_above(here[f], keep1, keep2, keep4)

            def total(pairs):
                found = [slope[a][f] for a, f in pairs if f in slope[a]]
                result = found[0]
                for item in found[1:]:
                    result = result + item
                return result

            result = [None] * FIELDS
            for c in range(3):
                result[c] = rinv * total([(a, VOIGT[c][a]) for a in range(3)])
            spread = lam * total([(a, a) for a in range(3)])
            for b in range(3):
                if b in slope[b]:
                    result[3 + b] = spread + 2.0 * mu * slope[b][b]
                else:
                    result[3 + b] = spread
            for b, c in ((1, 2), (0, 2), (0, 1)):
                result[VOIGT[b][c]] = mu * total([(b, c), (c, b)])
            for f in range(FIELDS):
                out_ref[f, i * NP + j] = result[f] + (2.0 * j + 1.0) * fluxy_ref[j % 2, f]

            for f in ACTIVE[1]:
                before = sums_y[f][1 - j % 2]
                sums_y[f][1 - j % 2] = here[f] if before is None else before + here[f]
            for f in range(FIELDS):
                run_ref[1 - parity, f, j] += here[f]

    @pl.loop(0, NP)
    def _(j):
        even_x, odd_x = local_flux(
            [run_ref[1, f, j] for f in range(FIELDS)],
            [run_ref[0, f, j] for f in range(FIELDS)],
            0, 1, *keeps_x, rinv, lam, mu, speed,
        )
        for f in range(FIELDS):
            flux_ref[0, f, j] = even_x[f]
            flux_ref[1, f, j] = odd_x[f]


def inner(wave, rows):
    return call(
        inner_kernel,
        (wave, rows),
        [array(FIELDS, 64, NP, NE), array(2, FIELDS, NP, NP, NE)],
        [pltpu.VMEM((2, FIELDS, NP, NP, NE), f32), pltpu.VMEM((2, FIELDS, NP, NE), f32)],
    )


def update_kernel(last, half, *refs):
    refs = list(refs)
    base_ref = refs.pop(0) if half else None
    (wave_ref, part_ref, flux_ref, upper_ref, lower_ref, below_ref, above_ref, rows_ref,
     *outs, fluxz_ref) = refs
    rinv, lam, mu, speed = materials(rows_ref)
    order = jnp.broadcast_to(rows_ref[4:5, :], (NP, NE))
    orient = jnp.broadcast_to(rows_ref[5:6, :], (NP, NE))
    k = lax.broadcasted_iota(jnp.int32, (NP, NE), 0)
    k_even = k % 2 == 0
    factor_z = (2 * k + 1).astype(f32)
    step = 0.5 * DT if half else DT

    @pl.loop(0, NP)
    def _(i):
        parity = lax.rem(i, 2)
        factor_x = (2 * i + 1).astype(f32)
        at = pl.multiple_of(i * NP, NP)
        rows = pl.ds(at, NP)
        total, difference = [], []
        for f in range(FIELDS):
            jump_upper = upper_ref[f, rows] - above_ref[f, rows]
            jump_lower = lower_ref[f, rows] - below_ref[f, rows]
            total.append(jump_upper + jump_lower)
            difference.append(jump_upper - jump_lower)
        even, odd = face_flux(total, difference, 2, rinv, lam, mu, speed)
        for f in range(FIELDS):
            fluxz_ref[0, f] = even[f]
            fluxz_ref[1, f] = odd[f]

        masks = []
        for j in range(NP):
            highest = jnp.maximum(k, jnp.maximum(i, j)).astype(f32)
            masks.append(jnp.where(highest <= order, step, 0.0))
        if last:
            flip_x = ((orient == 1.0) | (orient == 3.0)) & (parity == 1)
            sign_x = jnp.where(flip_x, -1.0, 1.0)
            sign_y = jnp.where(orient >= 2.0, -1.0, 1.0)
            signs = [sign_x, sign_x * sign_y]

        for f in range(FIELDS):
            fresh = []
            for j in range(NP):
                lifted = jnp.where(
                    k_even,
                    jnp.broadcast_to(fluxz_ref[0, f, j : j + 1, :], (NP, NE)),
                    jnp.broadcast_to(fluxz_ref[1, f, j : j + 1, :], (NP, NE)),
                )
                slope = part_ref[f, at + j] + factor_x * flux_ref[parity, f, j] + factor_z * lifted
                start = wave_ref[f, at + j]
                if half:
                    start = 0.5 * (base_ref[f, at + j] + start)
                new = start + masks[j] * slope
                if last:
                    outs[1][f, at + j] = new * signs[j % 2]
                    if f >= 3:
                        outs[0][0, f - 3, at + j] = base_ref[f, at + j]
                        outs[0][1, f - 3, at + j] = new
                else:
                    outs[0][f, at + j] = new
                fresh.append(new)
            if not last:
                outs[1][f, rows], outs[2][f, rows] = face_traces(fresh, k)


def update(base, wave, part, flux, upper, lower, below, above, rows, last):
    half = base is not None
    whole, trace = array(FIELDS, 64, NP, NE), array(FIELDS, 64, NE)
    operands = (wave, part, flux, upper, lower, below, above, rows)
    both = array(STEPS, 6, 64, NP, NE)

    def kernel(*refs):
        update_kernel(last, half, *refs)

    return call(
        kernel,
        (base,) + operands if half else operands,
        [both, whole] if last else [whole, trace, trace],
        [pltpu.VMEM((2, FIELDS, NP, NE), f32)],
    )


def gradient_kernel(
    me_ref, owner_ref, rows_ref, pick_ref, head_ref, snap_ref, got_ref, stress_ref,
    out_ref, vel_ref, moved_ref, frame_ref,
):
    keep = owner_ref[...] == me_ref[0]
    row = lax.broadcasted_iota(jnp.int32, (8, NE), 0)
    out_ref[...] = jnp.zeros_like(out_ref)
    frame_ref[...] = mask_and_sign(rows_ref[4:5, :], rows_ref[5:6, :])

    @pl.loop(0, SNAPS)
    def _(g):
        index = jnp.where(g < BLOCK_B, g + 1, 0)
        step, c = index // 3, lax.rem(index, 3)

        def settle(block):
            velocity = jnp.where(keep, snap_ref[index], block) * frame_ref[...]
            vel_ref[...] = velocity.reshape(64, NP, NE)

        @pl.when(g < BLOCK_B)
        def _():
            block = gather_elements(pick_ref[...], got_ref, pl.multiple_of(g * 8, 8))
            moved_ref[pl.ds(g + 1, 1), :] = block[0:1]
            first = jnp.where(row == 0, 0.0, block[0:8])
            settle(jnp.concatenate([first, block[8:]], axis=0))

        @pl.when(g == BLOCK_B)
        def _():
            first = jnp.where(
                row == 0, 0.0, jnp.where(row < 6, moved_ref[...], head_ref[0:8, :])
            )
            settle(jnp.concatenate([first, head_ref[8:, :]], axis=0))

        keep1, keep2, keep4, factor_z = mode_rows()
        weight_z = 2.0 / factor_z
        is_x, is_y, is_z = c == 0, c == 1, c == 2

        def pick3(x, y, z):
            return jnp.where(is_x, x, jnp.where(is_y, y, z))

        sum_lambda = jnp.zeros((NP, NE), f32)
        sum_shear = jnp.zeros((NP, NE), f32)
        runs = [[None] * NP, [None] * NP]
        for i in range(NP - 1, -1, -1):
            run_y = [None, None]
            for j in range(NP - 1, -1, -1):
                at = i * NP + j
                here = vel_ref[at]
                weight_x, weight_y = 2.0 / (2.0 * i + 1.0), 2.0 / (2.0 * j + 1.0)
                zero = jnp.zeros((NP, NE), f32)
                slope_x = zero if runs[i % 2][j] is None else runs[i % 2][j]
                slope_y = zero if run_y[j % 2] is None else run_y[j % 2]
                slope_x = (2.0 * weight_y) * (weight_z * slope_x)
                slope_y = (2.0 * weight_x) * (weight_z * slope_y)
                slope_z = (2.0 * weight_x * weight_y) * sums_above(here, keep1, keep2, keep4)
                sxx, syy, szz = (stress_ref[step, f, at] for f in range(3))
                syz, sxz, sxy = (stress_ref[step, f, at] for f in range(3, 6))
                own = pick3(slope_x, slope_y, slope_z)
                sum_lambda = sum_lambda + own * (sxx + syy + szz)
                sum_shear = (
                    sum_shear
                    + slope_x * pick3(2.0 * sxx, sxy, sxz)
                    + slope_y * pick3(sxy, 2.0 * syy, syz)
                    + slope_z * pick3(sxz, syz, 2.0 * szz)
                )
                for store, spot in ((run_y, 1 - j % 2), (runs[1 - i % 2], j)):
                    store[spot] = here if store[spot] is None else store[spot] + here
        out_ref[0:1, :] += DT * jnp.sum(sum_lambda, axis=0, keepdims=True)
        out_ref[1:2, :] += DT * jnp.sum(sum_shear, axis=0, keepdims=True)


def gradient(me, owner, rows, pick, head, snaps, got, stress):
    (result,) = call(
        gradient_kernel,
        (me, owner, rows, pick, head, snaps, got, stress),
        [array(2, NE)],
        [pltpu.VMEM((64, NP, NE), f32), pltpu.VMEM((8, NE), f32), pltpu.VMEM((NM, NE), f32)],
    )
    return result


def exchange(send):
    return lax.all_to_all(send, "dom", split_axis=0, concat_axis=0, tiled=True)


def traces_of_neighbours(upper, lower):
    up = [(d, d + 1) for d in range(DEV - 1)]
    down = [(d + 1, d) for d in range(DEV - 1)]
    return lax.ppermute(upper, "dom", up), lax.ppermute(lower, "dom", down)


def body(
    adjoint, snapshots, density, lame_lambda, lame_mu, element_order, orient, new_owner, new_slot
):
    me = jnp.reshape(lax.axis_index("dom"), (1,)).astype(jnp.int32)
    owner = new_owner.reshape(1, NE)
    nothing = jnp.zeros_like(density)
    meta = jnp.stack(
        [
            density,
            lame_lambda,
            lame_mu,
            element_order.astype(f32),
            orient.astype(f32),
            new_slot.astype(f32) + 1.0,
            nothing,
            nothing,
        ]
    )
    snaps = snapshots.reshape(SNAPS, NM, NE)
    send_a, send_b = pack(me, owner, meta, adjoint, snaps)
    got_a = exchange(send_a)
    got_b = exchange(send_b)
    wave, upper, lower, rows, pick, head = place(me, owner, meta, got_a, adjoint)
    for step in range(STEPS):
        start = wave
        for half in (False, True):
            below, above = traces_of_neighbours(upper, lower)
            part, flux = inner(wave, rows)
            last = half and step == STEPS - 1
            base = start if half else None
            results = update(base, wave, part, flux, upper, lower, below, above, rows, last)
            if last:
                stress, signed = results
            else:
                wave, upper, lower = results
    gradients = gradient(me, owner, rows, pick, head, snaps, got_b, stress)
    return signed.reshape(FIELDS, NM, NE), gradients


def solution(mesh):
    shard = P("dom")
    in_specs = (P(None, None, "dom"), P(None, None, None, "dom")) + (shard,) * 7
    out_specs = (P(None, None, "dom"), P(None, "dom"))
    return jax.shard_map(body, mesh=mesh, in_specs=in_specs, out_specs=out_specs, check_vma=False)
```

time: 357 us -> 193 us (0.54); the launches traced: 351 us -> 191 us
  matrix products: 104 us -> 0 us
  local copies, waits for them, and re-layouts: 69.1 us -> 13.6 us
  other arithmetic: 50.1 us -> 1.33 us
  Pallas kernels: 0 us -> 43 us
  starting transfers between devices: 45.1 us -> 56.5 us
  waiting for transfers between devices: 79.4 us -> 75.6 us
    dot_general x35 -> x0, matrix products: 86 us -> none  [the longest x12 33.3 us: volume_part(): jnp.einsum(slope_forms[direction], derivative, wavefield, precision=precise)]
    pallas_call x0 -> x12, Pallas kernels: none -> 43 us  [call(): pl.pallas_call(kernel, in_specs=[pl.BlockSpec(memory_space=pltpu.SMEM if...]
    gather x10 -> x0, local copies, waits for them, and re-layouts: 29.9 us -> none  [the longest x5 18.3 us: outgoing(): jnp.take(values, safe_source, axis=1)]
    ppermute x8, starting transfers between devices: 17.6 us -> 39.5 us  [traces_of_neighbours(): return (lax.ppermute(upper, 'dom', up), lax.ppermute(lower, 'dom', down))]
    select_n x12 -> x0, other arithmetic: 19.2 us -> none  [the longest x3 15.8 us: outgoing(): jnp.where(filled[None, :], jnp.take(values, safe_source, axis=1), 0.0)]
    unnamed x8 -> x0, matrix products: 17.8 us -> none
    ppermute x8, waiting for transfers between devices: 34.5 us -> 16.7 us  [traces_of_neighbours(): return (lax.ppermute(upper, 'dom', up), lax.ppermute(lower, 'dom', down))]
    mul x15 -> x0, other arithmetic: 17.5 us -> none  [the longest x1 6.34 us: body(): wavefield = frame_sign * order_mask * settled_state]
  transfers between devices with their start and end apart: 11 -> 10, of which waited for: 9 -> 5; matrix products, arithmetic and copies ran while one was open for 19% -> 0% of each run, Pallas kernels for 0% -> 16%
where the time goes in v1:
time: 193 us; the launch traced here: 191 us
  waiting for transfers between devices  75.6 us (39%)
  starting transfers between devices  56.5 us (29%)
  Pallas kernels  43 us (22%)
  local copies, waits for them, and re-layouts  13.6 us (7%)
    all_to_all x2, waiting for transfers between devices, exchange(): return lax.all_to_all(send, 'dom', split_axis=0, concat_axis=0, tiled=True)  58.8 us
    pallas_call x12, Pallas kernels, call(): pl.pallas_call(kernel, in_specs=[pl.BlockSpec(memory_space=pltpu.SMEM if...  43 us
    ppermute x8, starting transfers between devices, traces_of_neighbours(): return (lax.ppermute(upper, 'dom', up), lax.ppermute(lower, 'dom', down))  39.5 us
    all_to_all x2, starting transfers between devices, exchange(): return lax.all_to_all(send, 'dom', split_axis=0, concat_axis=0, tiled=True)  17 us
    ppermute x8, waiting for transfers between devices, traces_of_neighbours(): return (lax.ppermute(upper, 'dom', up), lax.ppermute(lower, 'dom', down))  16.7 us
    unnamed x20, local copies, waits for them, and re-layouts  12.9 us
  transfers between devices with their start and end apart: 10, of which 5 were waited for; matrix products, arithmetic and copies ran while one was open for 0% of the time, Pallas kernels for 16%

profile of v1, /device:TPU:32, one launch (start us, length us, event | category | flops | bytes accessed | tf_op | source)
XLA Modules:
  0.0 190.8 jit_solution(3342829355585146204)
XLA Ops:
  0.6 0.7 add_bitcast_fusion
  1.3 0.7 convert_bitcast_fusion
  2.0 0.7 stack.31.meta_ref
  2.7 0.0 copy-start
  2.7 1.4 copy-done
  4.1 0.0 copy-start.3
  4.1 1.7 copy-done.3
  5.7 0.0 copy-start.8
  5.8 0.7 copy-done.8
  6.4 5.7 %shard_map.104 = (f32[128,80,128]{2,1,0:T(8,128)S(1)}, bf16[256,128]{1,0:T(8,128)(2,1)S(1)}) custom-call(s32[1]{0:T(128)} %bitcast.me_ref, s32[1,128]{1,0:T(1,128)S(1)} %bitcast.16, f32[8,128]{1,0:T(8,128)S(1)} %stack.31.meta_ref, f32[9,512,128]{2,1,0:T(8,128)S(1)} %copy-done.3, f32[6,512,128]{2,1,0:T(8,128)S(1)} %bitcast.13), custom_call_target="tpu_custom_call" | custom-call | tf_op jit(solution)/shard_map/pallas_call | solution.py:36
  12.1 0.0 copy-start.5
  12.1 2.4 %copy-done.5 = f32[128,80,128]{2,1,0:T(8,128)} copy-done((f32[128,80,128]{2,1,0:T(8,128)}, f32[128,80,128]{2,1,0:T(8,128)S(1)}, u32[]{:S(2)}) %copy-start.5) | copy-done | bytes 5242904
  14.5 0.0 copy-start.1
  14.5 10.6 %all-to-all-start = ((f32[128,80,128]{2,1,0:T(8,128)}), f32[128,80,128]{2,1,0:T(8,128)}, u32[]{:S(2)}, u32[]{:S(2)}) async-start(f32[128,80,128]{2,1,0:T(8,128)} %copy-done.5), calls=%async_computation | async-start | bytes 10485760 | tf_op jit(solution)/shard_map/all_to_all | solution.py:516
  25.1 0.0 copy-done.1
  25.1 2.8 %shard_map.114 = f32[128,40,128]{2,1,0:T(8,128)S(1)} custom-call(bf16[256,128]{1,0:T(8,128)(2,1)S(1)} %get-tuple-element.54.hot_ref, f32[6,512,128]{2,1,0:T(8,128)S(1)} %bitcast.14), custom_call_target="tpu_custom_call" | custom-call | tf_op jit(solution)/shard_map/pallas_call | solution.py:36
  27.9 0.0 copy-start.2
  27.9 1.6 copy-done.2
  29.5 0.0 copy-start.9
  29.5 58.8 %all-to-all-done.got_ref = f32[128,80,128]{2,1,0:T(8,128)} async-done(((f32[128,80,128]{2,1,0:T(8,128)}), f32[128,80,128]{2,1,0:T(8,128)}, u32[]{:S(2)}, u32[]{:S(2)}) %all-to-all-start) | async-done | bytes 5242912 | tf_op jit(solution)/shard_map/all_to_all | solution.py:516
  88.3 6.4 %all-to-all-start.1 = ((f32[128,40,128]{2,1,0:T(8,128)}), f32[128,40,128]{2,1,0:T(8,128)}, u32[]{:S(2)}, u32[]{:S(2)}) async-start(f32[128,40,128]{2,1,0:T(8,128)} %copy-done.2), calls=%async_computation.1 | async-start | bytes 5242880 | tf_op jit(solution)/shard_map/all_to_all | solution.py:516
  94.7 0.0 copy-done.9
  94.7 0.0 copy-start.4
  94.8 1.7 copy-done.4
  96.4 10.7 %shard_map.105 = (f32[9,64,8,128]{3,2,1,0:T(8,128)S(1)}, f32[9,64,128]{2,1,0:T(8,128)S(1)}, f32[9,64,128]{2,1,0:T(8,128)S(1)}, f32[8,128]{1,0:T(8,128)S(1)}, bf1...) custom-call(s32[1]{0:T(128)} %bitcast.me_ref, s32[1,128]{1,0:T(1,128)S(1)} %bitcast.17, f32[8,128]{1,0:T(8,128)S(1)} %stack.31.meta_ref, ...), custom_call_target="tpu_custom_call" | custom-call | tf_op jit(solution)/shard_map/pallas_call | solution.py:36
  107.2 2.1 %collective-permute-start = (f32[9,64,128]{2,1,0:T(8,128)S(1)}, f32[9,64,128]{2,1,0:T(8,128)S(1)}, u32[]{:S(2)}, u32[]{:S(2)}) collective-permute-start(f32[9,64,128]{2,1,0:T(8,128)S(1)} %get-tuple-element.34.refs_3_), channel_id=1, source_target_pairs={{0,1},{1,2},{2,3},{3,4},{4,5},{5,6},{6,7},{7,8},{8,9},{9,10},{10,1... | collective-permute-start | bytes 884744 | tf_op jit(solution)/shard_map/ppermute | solution.py:522
  109.2 7.7 %collective-permute-start.1 = (f32[9,64,128]{2,1,0:T(8,128)S(1)}, f32[9,64,128]{2,1,0:T(8,128)S(1)}, u32[]{:S(2)}, u32[]{:S(2)}) collective-permute-start(f32[9,64,128]{2,1,0:T(8,128)S(1)} %get-tuple-element.35.refs_4_), channel_id=1, source_target_pairs={{1,0},{2,1},{3,2},{4,3},{5,4},{6,5},{7,6},{8,7},{9,8},{10,9},{11,1... | collective-permute-start | bytes 884744 | tf_op jit(solution)/shard_map/ppermute | solution.py:522
  117.0 2.4 %shard_map.106 = (f32[9,64,8,128]{3,2,1,0:T(8,128)S(1)}, f32[2,9,8,8,128]{4,3,2,1,0:T(8,128)S(1)}) custom-call(f32[9,64,8,128]{3,2,1,0:T(8,128)S(1)} %get-tuple-element.30.wave_ref.refs_0_, f32[8,128]{1,0:T(8,128)S(1)} %get-tuple-element.31.rows_ref.refs_7_.refs_8_), custom_call_target="tpu_custom_call" | custom-call | tf_op jit(solution)/shard_map/pallas_call | solution.py:36
  119.4 11.4 %collective-permute-done.refs_5_ = f32[9,64,128]{2,1,0:T(8,128)S(1)} collective-permute-done((f32[9,64,128]{2,1,0:T(8,128)S(1)}, f32[9,64,128]{2,1,0:T(8,128)S(1)}, u32[]{:S(2)}, u32[]{:S(2)}) %collective-permute-start) | collective-permute-done | bytes 294944 | tf_op jit(solution)/shard_map/ppermute | solution.py:522
  130.8 0.0 collective-permute-done.1.refs_6_
  130.8 1.2 shard_map.107
  132.0 1.9 %collective-permute-start.2 = (f32[9,64,128]{2,1,0:T(8,128)S(1)}, f32[9,64,128]{2,1,0:T(8,128)S(1)}, u32[]{:S(2)}, u32[]{:S(2)}) collective-permute-start(f32[9,64,128]{2,1,0:T(8,128)S(1)} %get-tuple-element.39.refs_4_), channel_id=1, source_target_pairs={{0,1},{1,2},{2,3},{3,4},{4,5},{5,6},{6,7},{7,8},{8,9},{9,10},{10,1... | collective-permute-start | bytes 884744 | tf_op jit(solution)/shard_map/ppermute | solution.py:522
  133.9 7.9 %collective-permute-start.3 = (f32[9,64,128]{2,1,0:T(8,128)S(1)}, f32[9,64,128]{2,1,0:T(8,128)S(1)}, u32[]{:S(2)}, u32[]{:S(2)}) collective-permute-start(f32[9,64,128]{2,1,0:T(8,128)S(1)} %get-tuple-element.40.refs_5_), channel_id=1, source_target_pairs={{1,0},{2,1},{3,2},{4,3},{5,4},{6,5},{7,6},{8,7},{9,8},{10,9},{11,1... | collective-permute-start | bytes 884744 | tf_op jit(solution)/shard_map/ppermute | solution.py:522
  141.8 2.4 %shard_map.108 = (f32[9,64,8,128]{3,2,1,0:T(8,128)S(1)}, f32[2,9,8,8,128]{4,3,2,1,0:T(8,128)S(1)}) custom-call(f32[9,64,8,128]{3,2,1,0:T(8,128)S(1)} %get-tuple-element.36.wave_ref.refs_1_, f32[8,128]{1,0:T(8,128)S(1)} %get-tuple-element.31.rows_ref.refs_7_.refs_8_), custom_call_target="tpu_custom_call" | custom-call | tf_op jit(solution)/shard_map/pallas_call | solution.py:36
  144.2 0.0 collective-permute-done.2.refs_6_
  144.3 1.8 collective-permute-done.3.refs_7_
  146.0 1.4 shard_map.109
  147.4 1.9 %collective-permute-start.4 = (f32[9,64,128]{2,1,0:T(8,128)S(1)}, f32[9,64,128]{2,1,0:T(8,128)S(1)}, u32[]{:S(2)}, u32[]{:S(2)}) collective-permute-start(f32[9,64,128]{2,1,0:T(8,128)S(1)} %get-tuple-element.44.refs_3_), channel_id=1, source_target_pairs={{0,1},{1,2},{2,3},{3,4},{4,5},{5,6},{6,7},{7,8},{8,9},{9,10},{10,1... | collective-permute-start | bytes 884744 | tf_op jit(solution)/shard_map/ppermute | solution.py:522
  149.3 8.0 %collective-permute-start.5 = (f32[9,64,128]{2,1,0:T(8,128)S(1)}, f32[9,64,128]{2,1,0:T(8,128)S(1)}, u32[]{:S(2)}, u32[]{:S(2)}) collective-permute-start(f32[9,64,128]{2,1,0:T(8,128)S(1)} %get-tuple-element.45.refs_4_), channel_id=1, source_target_pairs={{1,0},{2,1},{3,2},{4,3},{5,4},{6,5},{7,6},{8,7},{9,8},{10,9},{11,1... | collective-permute-start | bytes 884744 | tf_op jit(solution)/shard_map/ppermute | solution.py:522
  157.4 2.4 %shard_map.110 = (f32[9,64,8,128]{3,2,1,0:T(8,128)S(1)}, f32[2,9,8,8,128]{4,3,2,1,0:T(8,128)S(1)}) custom-call(f32[9,64,8,128]{3,2,1,0:T(8,128)S(1)} %get-tuple-element.41.wave_ref.refs_0_, f32[8,128]{1,0:T(8,128)S(1)} %get-tuple-element.31.rows_ref.refs_7_.refs_8_), custom_call_target="tpu_custom_call" | custom-call | tf_op jit(solution)/shard_map/pallas_call | solution.py:36
  159.8 0.0 collective-permute-done.4.refs_5_
  159.9 1.8 collective-permute-done.5.refs_6_
  161.6 1.3 shard_map.111
  163.0 1.9 %collective-permute-start.6 = (f32[9,64,128]{2,1,0:T(8,128)S(1)}, f32[9,64,128]{2,1,0:T(8,128)S(1)}, u32[]{:S(2)}, u32[]{:S(2)}) collective-permute-start(f32[9,64,128]{2,1,0:T(8,128)S(1)} %get-tuple-element.49.refs_4_), channel_id=1, source_target_pairs={{0,1},{1,2},{2,3},{3,4},{4,5},{5,6},{6,7},{7,8},{8,9},{9,10},{10,1... | collective-permute-start | bytes 884744 | tf_op jit(solution)/shard_map/ppermute | solution.py:522
  164.9 8.0 %collective-permute-start.7 = (f32[9,64,128]{2,1,0:T(8,128)S(1)}, f32[9,64,128]{2,1,0:T(8,128)S(1)}, u32[]{:S(2)}, u32[]{:S(2)}) collective-permute-start(f32[9,64,128]{2,1,0:T(8,128)S(1)} %get-tuple-element.50.refs_5_), channel_id=1, source_target_pairs={{1,0},{2,1},{3,2},{4,3},{5,4},{6,5},{7,6},{8,7},{9,8},{10,9},{11,1... | collective-permute-start | bytes 884744 | tf_op jit(solution)/shard_map/ppermute | solution.py:522
  172.9 2.4 %shard_map.112 = (f32[9,64,8,128]{3,2,1,0:T(8,128)S(1)}, f32[2,9,8,8,128]{4,3,2,1,0:T(8,128)S(1)}) custom-call(f32[9,64,8,128]{3,2,1,0:T(8,128)S(1)} %get-tuple-element.46.wave_ref.refs_1_, f32[8,128]{1,0:T(8,128)S(1)} %get-tuple-element.31.rows_ref.refs_7_.refs_8_), custom_call_target="tpu_custom_call" | custom-call | tf_op jit(solution)/shard_map/pallas_call | solution.py:36
  175.4 0.0 collective-permute-done.6.refs_6_
  175.4 1.8 collective-permute-done.7.refs_7_
  177.1 2.5 %shard_map.113 = (f32[2,6,64,8,128]{4,3,2,1,0:T(8,128)S(1)}, f32[9,64,8,128]{3,2,1,0:T(8,128)}) custom-call(f32[9,64,8,128]{3,2,1,0:T(8,128)S(1)} %get-tuple-element.41.wave_ref.refs_0_, f32[9,64,8,128]{3,2,1,0:T(8,128)S(1)} %get-tuple-element.46.wave_ref.refs_1_, f32[9,64,8,128]{3,2,1,0:T(8,128)S(1)} %get-tuple-element.47.refs_2_, ...), custom_call_target="tpu_custom_call" | custom-call | tf_op jit(solution)/shard_map/pallas_call | solution.py:36
  179.6 0.0 copy-start.6
  179.6 1.6 copy-done.6
  181.3 0.0 all-to-all-done.1.got_ref
  181.3 0.0 copy-start.7
  181.3 1.9 copy-done.7
  183.2 7.6 %shard_map.115 = f32[2,128]{1,0:T(2,128)} custom-call(s32[1]{0:T(128)} %bitcast.me_ref, s32[1,128]{1,0:T(1,128)S(1)} %bitcast.18, f32[8,128]{1,0:T(8,128)S(1)} %get-tuple-element.31.rows_ref.refs_7_.refs_8_, bf16[128,256]{1,0:T(8,128)(2,1)S(1)} %get-tuple-element.52.pick_ref, f32[512,128]{1,0:T(8,128)S(1)} %get-tuple-element.53.head_ref, ...), custom_call_target="tpu_custom_call" | custom-call | tf_op jit(solution)/shard_map/pallas_call | solution.py:36
  (1 shorter events, 0.0 us)
Async XLA Ops:
  2.7 1.4 copy-start
  4.1 1.7 copy-start.3
  5.7 0.7 copy-start.8
  12.1 2.4 %copy-start.5 = (f32[128,80,128]{2,1,0:T(8,128)}, f32[128,80,128]{2,1,0:T(8,128)S(1)}, u32[]{:S(2)}) copy-start(f32[128,80,128]{2,1,0:T(8,128)S(1)} %get-tuple-element.29) | copy-start | bytes 15728644
  14.5 10.6 %copy-start.1 = (f32[2,3,512,128]{3,2,1,0:T(8,128)S(1)}, f32[2,3,512,128]{3,2,1,0:T(8,128)}, u32[]{:S(2)}) copy-start(f32[2,3,512,128]{3,2,1,0:T(8,128)} %param.10) | copy-start | bytes 4718596
  14.5 73.9 %all-to-all-start = ((f32[128,80,128]{2,1,0:T(8,128)}), f32[128,80,128]{2,1,0:T(8,128)}, u32[]{:S(2)}, u32[]{:S(2)}) async-start(f32[128,80,128]{2,1,0:T(8,128)} %copy-done.5), calls=%async_computation | async-start | bytes 10485760 | tf_op jit(solution)/shard_map/all_to_all | solution.py:516
  27.9 1.6 copy-start.2
  29.5 65.3 %copy-start.9 = (s32[128]{0:T(128)S(1)}, s32[128]{0:T(128)}, u32[]{:S(2)}) copy-start(s32[128]{0:T(128)} %param.16) | copy-start | bytes 1540
  88.3 92.9 %all-to-all-start.1 = ((f32[128,40,128]{2,1,0:T(8,128)}), f32[128,40,128]{2,1,0:T(8,128)}, u32[]{:S(2)}, u32[]{:S(2)}) async-start(f32[128,40,128]{2,1,0:T(8,128)} %copy-done.2), calls=%async_computation.1 | async-start | bytes 5242880 | tf_op jit(solution)/shard_map/all_to_all | solution.py:516
  94.7 1.7 copy-start.4
  107.2 23.7 %collective-permute-start = (f32[9,64,128]{2,1,0:T(8,128)S(1)}, f32[9,64,128]{2,1,0:T(8,128)S(1)}, u32[]{:S(2)}, u32[]{:S(2)}) collective-permute-start(f32[9,64,128]{2,1,0:T(8,128)S(1)} %get-tuple-element.34.refs_3_), channel_id=1, source_target_pairs={{0,1},{1,2},{2,3},{3,4},{4,5},{5,6},{6,7},{7,8},{8,9},{9,10},{10,1... | collective-permute-start | bytes 884744 | tf_op jit(solution)/shard_map/ppermute | solution.py:522
  109.2 21.6 %collective-permute-start.1 = (f32[9,64,128]{2,1,0:T(8,128)S(1)}, f32[9,64,128]{2,1,0:T(8,128)S(1)}, u32[]{:S(2)}, u32[]{:S(2)}) collective-permute-start(f32[9,64,128]{2,1,0:T(8,128)S(1)} %get-tuple-element.35.refs_4_), channel_id=1, source_target_pairs={{1,0},{2,1},{3,2},{4,3},{5,4},{6,5},{7,6},{8,7},{9,8},{10,9},{11,1... | collective-permute-start | bytes 884744 | tf_op jit(solution)/shard_map/ppermute | solution.py:522
  132.0 12.3 %collective-permute-start.2 = (f32[9,64,128]{2,1,0:T(8,128)S(1)}, f32[9,64,128]{2,1,0:T(8,128)S(1)}, u32[]{:S(2)}, u32[]{:S(2)}) collective-permute-start(f32[9,64,128]{2,1,0:T(8,128)S(1)} %get-tuple-element.39.refs_4_), channel_id=1, source_target_pairs={{0,1},{1,2},{2,3},{3,4},{4,5},{5,6},{6,7},{7,8},{8,9},{9,10},{10,1... | collective-permute-start | bytes 884744 | tf_op jit(solution)/shard_map/ppermute | solution.py:522
  133.9 12.1 %collective-permute-start.3 = (f32[9,64,128]{2,1,0:T(8,128)S(1)}, f32[9,64,128]{2,1,0:T(8,128)S(1)}, u32[]{:S(2)}, u32[]{:S(2)}) collective-permute-start(f32[9,64,128]{2,1,0:T(8,128)S(1)} %get-tuple-element.40.refs_5_), channel_id=1, source_target_pairs={{1,0},{2,1},{3,2},{4,3},{5,4},{6,5},{7,6},{8,7},{9,8},{10,9},{11,1... | collective-permute-start | bytes 884744 | tf_op jit(solution)/shard_map/ppermute | solution.py:522
  147.4 12.4 %collective-permute-start.4 = (f32[9,64,128]{2,1,0:T(8,128)S(1)}, f32[9,64,128]{2,1,0:T(8,128)S(1)}, u32[]{:S(2)}, u32[]{:S(2)}) collective-permute-start(f32[9,64,128]{2,1,0:T(8,128)S(1)} %get-tuple-element.44.refs_3_), channel_id=1, source_target_pairs={{0,1},{1,2},{2,3},{3,4},{4,5},{5,6},{6,7},{7,8},{8,9},{9,10},{10,1... | collective-permute-start | bytes 884744 | tf_op jit(solution)/shard_map/ppermute | solution.py:522
  149.3 12.3 %collective-permute-start.5 = (f32[9,64,128]{2,1,0:T(8,128)S(1)}, f32[9,64,128]{2,1,0:T(8,128)S(1)}, u32[]{:S(2)}, u32[]{:S(2)}) collective-permute-start(f32[9,64,128]{2,1,0:T(8,128)S(1)} %get-tuple-element.45.refs_4_), channel_id=1, source_target_pairs={{1,0},{2,1},{3,2},{4,3},{5,4},{6,5},{7,6},{8,7},{9,8},{10,9},{11,1... | collective-permute-start | bytes 884744 | tf_op jit(solution)/shard_map/ppermute | solution.py:522
  163.0 12.4 %collective-permute-start.6 = (f32[9,64,128]{2,1,0:T(8,128)S(1)}, f32[9,64,128]{2,1,0:T(8,128)S(1)}, u32[]{:S(2)}, u32[]{:S(2)}) collective-permute-start(f32[9,64,128]{2,1,0:T(8,128)S(1)} %get-tuple-element.49.refs_4_), channel_id=1, source_target_pairs={{0,1},{1,2},{2,3},{3,4},{4,5},{5,6},{6,7},{7,8},{8,9},{9,10},{10,1... | collective-permute-start | bytes 884744 | tf_op jit(solution)/shard_map/ppermute | solution.py:522
  164.9 12.3 %collective-permute-start.7 = (f32[9,64,128]{2,1,0:T(8,128)S(1)}, f32[9,64,128]{2,1,0:T(8,128)S(1)}, u32[]{:S(2)}, u32[]{:S(2)}) collective-permute-start(f32[9,64,128]{2,1,0:T(8,128)S(1)} %get-tuple-element.50.refs_5_), channel_id=1, source_target_pairs={{1,0},{2,1},{3,2},{4,3},{5,4},{6,5},{7,6},{8,7},{9,8},{10,9},{11,1... | collective-permute-start | bytes 884744 | tf_op jit(solution)/shard_map/ppermute | solution.py:522
  179.6 1.6 copy-start.6
  181.3 1.9 copy-start.7

commit v2 on v1

v2 whole, which is shorter than its diff:
```python
import jax
import jax.numpy as jnp
from jax import lax
from jax.experimental import pallas as pl
from jax.experimental.pallas import tpu as pltpu
from jax.sharding import PartitionSpec as P

NP = 8
NM = 512
EX = 8
NE = 128
STEPS = 2
DEV = 128
FIELDS = 9
SNAPS = 6
BLOCKS = FIELDS + SNAPS
DT = 0.01
f32 = jnp.float32
bf16 = jnp.bfloat16

VOIGT = ((3, 8, 7), (8, 4, 6), (7, 6, 5))
ACTIVE = tuple((0, 1, 2) + VOIGT[a] for a in range(3))


def split3(x):
    high = x.astype(bf16)
    rest = x - high.astype(f32)
    middle = rest.astype(bf16)
    low = (rest - middle.astype(f32)).astype(bf16)
    return high, middle, low


def call(kernel, operands, out_shape, scratch_shapes=(), hbm=(), hbm_out=(), limit=16):
    def space(position, x):
        return pltpu.HBM if position in hbm else pltpu.VMEM

    return pl.pallas_call(
        kernel,
        in_specs=[pl.BlockSpec(memory_space=space(n, x)) for n, x in enumerate(operands)],
        out_specs=[
            pl.BlockSpec(memory_space=pltpu.HBM if n in hbm_out else pltpu.VMEM)
            for n in range(len(out_shape))
        ],
        out_shape=out_shape,
        scratch_shapes=list(scratch_shapes),
        compiler_params=pltpu.CompilerParams(vmem_limit_bytes=limit * 1024 * 1024),
        cost_estimate=pl.CostEstimate(flops=0, bytes_accessed=0, transcendentals=0),
    )(*operands)


def array(*shape, dtype=f32):
    return jax.ShapeDtypeStruct(shape, dtype)


def scatter_rows(hot, x, out_ref, row):
    parts = jnp.concatenate(split3(x), axis=1)
    hots = jnp.concatenate([hot, hot, hot], axis=1)
    rows = lax.dot_general(hots, parts, (((1,), (1,)), ((), ())), preferred_element_type=f32)
    for r in range(2):
        for q in range(4):
            out_ref[:, row + r * 4 + q, :] = rows[r * DEV : (r + 1) * DEV, q * 128 : (q + 1) * 128]


def pack_kernel(*refs):
    (owner_hbm, density_hbm, lambda_hbm, mu_hbm, order_hbm, orient_hbm, slot_hbm, adj_hbm,
     snap_hbm, out_hbm, meta_ref, owner_ref, floats_ref, ints_ref, hot_ref, block_ref, out_ref,
     row_sem, in_sem, out_sem) = refs
    small = [pltpu.make_async_copy(owner_hbm, owner_ref, row_sem.at[0])]
    for n, source in enumerate((density_hbm, lambda_hbm, mu_hbm)):
        small.append(pltpu.make_async_copy(source, floats_ref.at[n], row_sem.at[1 + n]))
    for n, source in enumerate((order_hbm, orient_hbm, slot_hbm)):
        small.append(pltpu.make_async_copy(source, ints_ref.at[n], row_sem.at[4 + n]))
    arrive = []
    for b in range(BLOCKS):
        source = adj_hbm.at[b] if b < FIELDS else snap_hbm.at[b - FIELDS]
        arrive.append(pltpu.make_async_copy(source, block_ref.at[b], in_sem.at[b]))
    for copy in small + arrive:
        copy.start()
    for copy in small:
        copy.wait()
    for n in range(3):
        meta_ref[n : n + 1, :] = floats_ref[n]
        meta_ref[3 + n : 4 + n, :] = ints_ref[n].astype(f32)
    meta_ref[5:6, :] += 1.0
    meta_ref[6:7, :] = jnp.where(owner_ref[...] == lax.axis_index("dom"), 1.0, 0.0)
    meta_ref[7:8, :] = jnp.zeros((1, NE), f32)
    owner_row = owner_ref[...]
    owner_all = jnp.broadcast_to(owner_row, (NE, NE))
    owner_col = jnp.transpose(owner_all)
    at0 = lax.broadcasted_iota(jnp.int32, (NE, NE), 0)
    at1 = lax.broadcasted_iota(jnp.int32, (NE, NE), 1)
    earlier = jnp.where((owner_col == owner_all) & (at0 < at1), 1.0, 0.0)
    rank = jnp.sum(earlier, axis=0, keepdims=True)
    dest = jnp.where(owner_row != lax.axis_index("dom"), owner_row, -1)
    for r in range(2):
        chosen = (at0 == dest) & (rank == float(r))
        hot_ref[r * DEV : (r + 1) * DEV, :] = jnp.where(chosen, 1.0, 0.0).astype(bf16)

    first_row = lax.broadcasted_iota(jnp.int32, (8, NE), 0) == 0
    leave = []
    for b in range(BLOCKS):
        arrive[b].wait()
        block = block_ref[b]
        if b >= FIELDS:
            n = b - FIELDS
            row = jnp.broadcast_to(meta_ref[n : n + 1, :], (8, NE))
            block = jnp.concatenate([jnp.where(first_row, row, block[0:8]), block[8:]], axis=0)
        scatter_rows(hot_ref[...], block, out_ref, b * 8)
        rows = pl.ds(b * 8, 8)
        leave.append(
            pltpu.make_async_copy(out_ref.at[:, rows, :], out_hbm.at[:, rows, :], out_sem.at[b])
        )
        leave[b].start()
    for copy in leave:
        copy.wait()


def pack(rows, adjoint, snaps):
    return call(
        pack_kernel,
        (*rows, adjoint, snaps),
        [array(DEV, BLOCKS * 8, 128), array(8, NE)],
        [
            pltpu.VMEM((1, NE), jnp.int32),
            pltpu.VMEM((3, 1, NE), f32),
            pltpu.VMEM((3, 1, NE), jnp.int32),
            pltpu.VMEM((2 * DEV, NE), bf16),
            pltpu.VMEM((BLOCKS, NM, NE), f32),
            pltpu.VMEM((DEV, BLOCKS * 8, 128), f32),
            pltpu.SemaphoreType.DMA((7,)),
            pltpu.SemaphoreType.DMA((BLOCKS,)),
            pltpu.SemaphoreType.DMA((BLOCKS,)),
        ],
        hbm=tuple(range(9)),
        hbm_out=(0,),
        limit=63,
    )


def select_slots(pick, slots):
    parts = jnp.concatenate(split3(slots), axis=0)
    picks = jnp.concatenate([pick, pick, pick], axis=1)
    placed = lax.dot_general(picks, parts, (((1,), (0,)), ((), ())), preferred_element_type=f32)
    return jnp.transpose(placed)


def gather_elements(pick, got_ref, row):
    slots = [
        jnp.concatenate([got_ref[:, row + r * 4 + q, :] for q in range(4)], axis=1) for r in range(2)
    ]
    return select_slots(pick, jnp.concatenate(slots, axis=0))


def mode_indices(shape):
    mode = lax.broadcasted_iota(jnp.int32, shape, 0)
    return mode // 64, (mode // 8) % 8, mode % 8


def mask_and_sign(order, orient):
    i, j, k = mode_indices((NM, NE))
    highest = jnp.maximum(jnp.maximum(i, j), k).astype(f32)
    flip_x = (orient == 1.0) | (orient == 3.0)
    flip_y = orient >= 2.0
    sign_x = jnp.where(i % 2 == 1, jnp.where(flip_x, -1.0, 1.0), 1.0)
    sign_y = jnp.where(j % 2 == 1, jnp.where(flip_y, -1.0, 1.0), 1.0)
    return jnp.where(highest <= order, sign_x * sign_y, 0.0)


def odd_device():
    return jnp.full((NP, NE), lax.axis_index("dom"), jnp.int32) % 2 == 1


def face_traces(modes, row):
    low4, low2, even = row < 4, row % 4 < 2, row % 2 == 0
    fours = []
    for j in range(4):
        first, second = modes[j], modes[j + 4]
        other = jnp.where(low4, second, first)
        fours.append(jnp.where(low4, first, second) + pltpu.roll(other, 4, 0))
    twos = []
    for j in range(2):
        first, second = fours[j], fours[j + 2]
        twos.append(
            jnp.where(low2, first + pltpu.roll(first, 6, 0), second + pltpu.roll(second, 2, 0))
        )
    first, second = twos
    next_first, next_second = pltpu.roll(first, 7, 0), pltpu.roll(second, 1, 0)
    upper = jnp.where(even, first + next_first, second + next_second)
    lower = jnp.where(even, first - next_first, next_second - second)
    return upper, lower


def place_kernel(
    meta_ref, got_ref, adj_ref, wave_ref, cross_ref, paired_ref, rows_ref, pick_ref, frame_ref
):
    keep = meta_ref[6:7, :] > 0.5
    odd = odd_device()
    lane = lax.broadcasted_iota(jnp.int32, (DEV, NE), 1)
    columns = []
    for r in range(2):
        column = jnp.zeros((DEV, NE), f32)
        for n in range(SNAPS):
            value = got_ref[:, (FIELDS + n) * 8 + r * 4, 0:1]
            column = jnp.where(lane == n, value, column)
        columns.append(column)
        chosen = jnp.where(column[:, 5:6] == lane.astype(f32) + 1.0, 1.0, 0.0)
        pick_ref[:, r * DEV : (r + 1) * DEV] = jnp.transpose(chosen).astype(bf16)
    arrived = select_slots(pick_ref[...], jnp.concatenate(columns, axis=0))
    meta = jnp.where(keep, meta_ref[...], arrived[0:8])
    density, lam, mu = meta[0:1], meta[1:2], meta[2:3]
    order, orient = meta[3:4], meta[4:5]
    rows_ref[0:1, :] = 1.0 / density
    rows_ref[1:2, :] = lam
    rows_ref[2:3, :] = mu
    rows_ref[3:4, :] = jnp.sqrt((lam + 2.0 * mu) / density)
    rows_ref[4:5, :] = order
    rows_ref[5:6, :] = orient
    rows_ref[6:8, :] = jnp.zeros((2, NE), f32)
    frame_ref[...] = mask_and_sign(order, orient)

    row = lax.broadcasted_iota(jnp.int32, (NP, NE), 0)
    for f in range(FIELDS):
        block = gather_elements(pick_ref[...], got_ref, f * 8)
        wave = jnp.where(keep, adj_ref[f], block) * frame_ref[...]
        wave = wave.reshape(64, NP, NE)
        wave_ref[f] = wave
        for i in range(NP):
            upper, lower = face_traces([wave[i * NP + j] for j in range(NP)], row)
            cross_ref[f, i * NP : (i + 1) * NP, :] = jnp.where(odd, upper, lower)
            paired_ref[f, i * NP : (i + 1) * NP, :] = jnp.where(odd, lower, upper)


def place(meta, got, adjoint):
    return call(
        place_kernel,
        (meta, got, adjoint),
        [
            array(FIELDS, 64, NP, NE),
            array(FIELDS, 64, NE),
            array(FIELDS, 64, NE),
            array(8, NE),
            array(NE, 2 * DEV, dtype=bf16),
            array(NM, NE),
        ],
    )


def materials(rows_ref):
    full = lambda r: jnp.broadcast_to(rows_ref[r : r + 1, :], (NP, NE))
    return full(0), full(1), full(2), full(3)


def apply_b(values, direction, rinv, lam, mu):
    out = [None] * FIELDS
    for c in range(3):
        out[c] = values[VOIGT[c][direction]] * rinv
    spread = lam * values[direction]
    for b in range(3):
        out[3 + b] = spread
    out[3 + direction] = spread + 2.0 * mu * values[direction]
    for c in range(3):
        if c != direction:
            out[VOIGT[c][direction]] = mu * values[c]
    return out


def face_flux(total, difference, direction, rinv, lam, mu, speed):
    even_b = apply_b(difference, direction, rinv, lam, mu)
    odd_b = apply_b(total, direction, rinv, lam, mu)
    even, odd = [], []
    for f in range(FIELDS):
        pen_even, pen_odd = speed * total[f], speed * difference[f]
        if even_b[f] is not None:
            pen_even, pen_odd = pen_even + even_b[f], pen_odd + odd_b[f]
        even.append(-0.25 * pen_even)
        odd.append(-0.25 * pen_odd)
    return even, odd


def local_flux(evens, odds, direction, offset, keep_up, keep_down, rinv, lam, mu, speed):
    total, difference = [], []
    for f in range(FIELDS):
        upper, lower = evens[f] + odds[f], evens[f] - odds[f]
        above = pltpu.roll(lower, NE - offset, 1) * keep_up
        below = pltpu.roll(upper, offset, 1) * keep_down
        total.append((upper - above) + (lower - below))
        difference.append((upper - above) - (lower - below))
    return face_flux(total, difference, direction, rinv, lam, mu, speed)


def lane_keeps():
    lane = lax.broadcasted_iota(jnp.int32, (NP, NE), 1)
    one = lambda cond: jnp.where(cond, 1.0, 0.0)
    column = lane % EX
    return (
        (one(column != EX - 1), one(column != 0)),
        (one(lane < NE - EX), one(lane >= EX)),
    )


def mode_rows():
    k = lax.broadcasted_iota(jnp.int32, (NP, NE), 0)
    one = lambda cond: jnp.where(cond, 1.0, 0.0)
    return one(k < 7), one(k < 6), one(k < 4), (2 * k + 1).astype(f32)


def sums_above(x, keep1, keep2, keep4):
    x = pltpu.roll(x, 7, 0) * keep1
    x = x + pltpu.roll(x, 6, 0) * keep2
    return x + pltpu.roll(x, 4, 0) * keep4


def inner_kernel(wave_ref, rows_ref, out_ref, flux_ref, run_ref, fluxy_ref):
    rinv, lam, mu, speed = materials(rows_ref)
    keeps_x, keeps_y = lane_keeps()
    keep1, keep2, keep4, factor_z = mode_rows()
    run_ref[...] = jnp.zeros_like(run_ref)

    @pl.loop(0, NP)
    def _(g):
        i = NP - 1 - g
        parity = lax.rem(i, 2)
        factor_x = (2 * i + 1).astype(f32)

        evens, odds = [], []
        for f in range(FIELDS):
            col = [wave_ref[f, i * NP + j] for j in range(NP)]
            evens.append((col[0] + col[2]) + (col[4] + col[6]))
            odds.append((col[1] + col[3]) + (col[5] + col[7]))
        even, odd = local_flux(evens, odds, 1, EX, *keeps_y, rinv, lam, mu, speed)
        for f in range(FIELDS):
            fluxy_ref[0, f] = even[f]
            fluxy_ref[1, f] = odd[f]

        sums_y = {f: [None, None] for f in ACTIVE[1]}
        for j in range(NP - 1, -1, -1):
            here = [wave_ref[f, i * NP + j] for f in range(FIELDS)]
            slope = [{}, {}, {}]
            for f in ACTIVE[0]:
                slope[0][f] = factor_x * run_ref[parity, f, j]
            for f in ACTIVE[1]:
                if sums_y[f][j % 2] is not None:
                    slope[1][f] = (2.0 * j + 1.0) * sums_y[f][j % 2]
            for f in ACTIVE[2]:
                slope[2][f] = factor_z * sums_above(here[f], keep1, keep2, keep4)

            def total(pairs):
                found = [slope[a][f] for a, f in pairs if f in slope[a]]
                result = found[0]
                for item in found[1:]:
                    result = result + item
                return result

            result = [None] * FIELDS
            for c in range(3):
                result[c] = rinv * total([(a, VOIGT[c][a]) for a in range(3)])
            spread = lam * total([(a, a) for a in range(3)])
            for b in range(3):
                if b in slope[b]:
                    result[3 + b] = spread + 2.0 * mu * slope[b][b]
                else:
                    result[3 + b] = spread
            for b, c in ((1, 2), (0, 2), (0, 1)):
                result[VOIGT[b][c]] = mu * total([(b, c), (c, b)])
            for f in range(FIELDS):
                out_ref[f, i * NP + j] = result[f] + (2.0 * j + 1.0) * fluxy_ref[j % 2, f]

            for f in ACTIVE[1]:
                before = sums_y[f][1 - j % 2]
                sums_y[f][1 - j % 2] = here[f] if before is None else before + here[f]
            for f in range(FIELDS):
                run_ref[1 - parity, f, j] += here[f]

    @pl.loop(0, NP)
    def _(j):
        even_x, odd_x = local_flux(
            [run_ref[1, f, j] for f in range(FIELDS)],
            [run_ref[0, f, j] for f in range(FIELDS)],
            0, 1, *keeps_x, rinv, lam, mu, speed,
        )
        for f in range(FIELDS):
            flux_ref[0, f, j] = even_x[f]
            flux_ref[1, f, j] = odd_x[f]


def inner(wave, rows):
    return call(
        inner_kernel,
        (wave, rows),
        [array(FIELDS, 64, NP, NE), array(2, FIELDS, NP, NP, NE)],
        [pltpu.VMEM((2, FIELDS, NP, NP, NE), f32), pltpu.VMEM((2, FIELDS, NP, NE), f32)],
    )


def update_kernel(last, half, *refs):
    refs = list(refs)
    base_ref = refs.pop(0) if half else None
    (wave_ref, part_ref, flux_ref, cross_ref, paired_ref, got_cross_ref, got_paired_ref,
     rows_ref, *rest) = refs
    if last:
        strain_ref, first_ref, out_ref, gradient_ref, fluxz_ref, sums_ref = rest
        sums_ref[...] = jnp.zeros_like(sums_ref)
    else:
        out_ref, out_cross_ref, out_paired_ref, fluxz_ref = rest
    rinv, lam, mu, speed = materials(rows_ref)
    order = jnp.broadcast_to(rows_ref[4:5, :], (NP, NE))
    orient = jnp.broadcast_to(rows_ref[5:6, :], (NP, NE))
    odd = odd_device()
    side = jnp.where(odd, 1.0, -1.0)
    k = lax.broadcasted_iota(jnp.int32, (NP, NE), 0)
    k_even = k % 2 == 0
    factor_z = (2 * k + 1).astype(f32)
    step = 0.5 * DT if half else DT

    @pl.loop(0, NP)
    def _(i):
        parity = lax.rem(i, 2)
        factor_x = (2 * i + 1).astype(f32)
        at = pl.multiple_of(i * NP, NP)
        rows = pl.ds(at, NP)
        total, difference = [], []
        for f in range(FIELDS):
            jump_cross = cross_ref[f, rows] - got_cross_ref[f, rows]
            jump_paired = paired_ref[f, rows] - got_paired_ref[f, rows]
            total.append(jump_cross + jump_paired)
            difference.append(side * (jump_cross - jump_paired))
        even, odds = face_flux(total, difference, 2, rinv, lam, mu, speed)
        for f in range(FIELDS):
            fluxz_ref[0, f] = even[f]
            fluxz_ref[1, f] = odds[f]

        masks = []
        for j in range(NP):
            highest = jnp.maximum(k, jnp.maximum(i, j)).astype(f32)
            masks.append(jnp.where(highest <= order, step, 0.0))
        if last:
            flip_x = ((orient == 1.0) | (orient == 3.0)) & (parity == 1)
            sign_x = jnp.where(flip_x, -1.0, 1.0)
            sign_y = jnp.where(orient >= 2.0, -1.0, 1.0)
            signs = [sign_x, sign_x * sign_y]
            stresses = [[] for _ in range(NP)]

        for f in range(FIELDS):
            fresh = []
            for j in range(NP):
                lifted = jnp.where(
                    k_even,
                    jnp.broadcast_to(fluxz_ref[0, f, j : j + 1, :], (NP, NE)),
                    jnp.broadcast_to(fluxz_ref[1, f, j : j + 1, :], (NP, NE)),
                )
                slope = part_ref[f, at + j] + factor_x * flux_ref[parity, f, j] + factor_z * lifted
                start = wave_ref[f, at + j]
                if half:
                    start = 0.5 * (base_ref[f, at + j] + start)
                new = start + masks[j] * slope
                if last:
                    out_ref[f, at + j] = new * signs[j % 2]
                    if f >= 3:
                        stresses[j].append(new)
                else:
                    out_ref[f, at + j] = new
                fresh.append(new)
            if not last:
                upper, lower = face_traces(fresh, k)
                out_cross_ref[f, rows] = jnp.where(odd, upper, lower)
                out_paired_ref[f, rows] = jnp.where(odd, lower, upper)
        if last:
            for j in range(NP):
                add_gradient(sums_ref, stresses[j], [strain_ref[f, at + j] for f in range(6)])

    if last:
        gradient_ref[...] = first_ref[...] + gradient_rows(sums_ref)


def update(base, wave, part, flux, traces, got, rows, last=None):
    half = base is not None
    whole, trace = array(FIELDS, 64, NP, NE), array(FIELDS, 64, NE)
    operands = ([base] if half else []) + [wave, part, flux, *traces, *got, rows]
    scratch = [pltpu.VMEM((2, FIELDS, NP, NE), f32)]
    out = [whole, trace, trace]
    if last is not None:
        operands += list(last)
        scratch.append(pltpu.VMEM((2, NP, NE), f32))
        out = [whole, array(2, NE)]

    def kernel(*refs):
        update_kernel(last is not None, half, *refs)

    return call(kernel, operands, out, scratch)


def add_gradient(sums_ref, stress, strain):
    normal = (stress[0] + stress[1]) + stress[2]
    sums_ref[0] += normal * ((strain[0] + strain[1]) + strain[2])
    shear = stress[0] * strain[0]
    for f in range(1, 6):
        shear = shear + stress[f] * strain[f]
    sums_ref[1] += shear


def gradient_rows(sums_ref):
    first = (0.5 * DT) * jnp.sum(sums_ref[0], axis=0, keepdims=True)
    second = DT * jnp.sum(sums_ref[1], axis=0, keepdims=True)
    return jnp.concatenate([first, second], axis=0)


def velocity_kernel(second, meta_ref, pick_ref, frame_ref, *refs):
    if second:
        snap_ref, got_ref, strain_ref, *rest = refs
    else:
        wave_ref, snap_ref, got_ref, gradient_ref, *rest = refs
    vel_ref, run_ref, sums_ref = rest
    start = 3 if second else 0
    keep = meta_ref[6:7, :] > 0.5
    row = lax.broadcasted_iota(jnp.int32, (8, NE), 0)
    keep1, keep2, keep4, factor_z = mode_rows()
    weight_z = 2.0 / factor_z
    sums_ref[...] = jnp.zeros_like(sums_ref)

    def settle(c):
        block = gather_elements(pick_ref[...], got_ref, (FIELDS + start + c) * 8)
        block = jnp.concatenate([jnp.where(row == 0, 0.0, block[0:8]), block[8:]], axis=0)
        velocity = jnp.where(keep, snap_ref[start + c], block) * frame_ref[...]
        vel_ref[c] = velocity.reshape(64, NP, NE)

    def strains(use):
        run_ref[...] = jnp.zeros_like(run_ref)

        @pl.loop(0, NP)
        def _(g):
            i = NP - 1 - g
            parity = lax.rem(i, 2)
            at = pl.multiple_of(i * NP, NP)
            weight_x = 2.0 / jnp.full((NP, NE), 2 * i + 1, jnp.int32).astype(f32)
            weight_xz = 2.0 * weight_x * weight_z
            zero = jnp.zeros((NP, NE), f32)
            run_y = [[zero, zero] for _ in range(3)]
            for j in range(NP - 1, -1, -1):
                weight_y = 2.0 / (2.0 * j + 1.0)
                slopes = []
                for c in range(3):
                    here = vel_ref[c, at + j]
                    slopes.append([
                        (2.0 * weight_y) * (weight_z * run_ref[parity, c, j]),
                        weight_xz * run_y[c][j % 2],
                        (2.0 * weight_y) * (weight_x * sums_above(here, keep1, keep2, keep4)),
                    ])
                    run_y[c][1 - j % 2] = run_y[c][1 - j % 2] + here
                    run_ref[1 - parity, c, j] += here
                use(at + j, [
                    2.0 * slopes[0][0], 2.0 * slopes[1][1], 2.0 * slopes[2][2],
                    slopes[2][1] + slopes[1][2], slopes[2][0] + slopes[0][2],
                    slopes[1][0] + slopes[0][1],
                ])

    for c in range(3):
        settle(c)
    if second:

        def keep_strains(at, strain):
            for f in range(6):
                strain_ref[f, at] = strain[f]

        strains(keep_strains)
    else:
        strains(
            lambda at, strain: add_gradient(
                sums_ref, [wave_ref[3 + f, at] for f in range(6)], strain
            )
        )
        gradient_ref[...] = gradient_rows(sums_ref)


def velocities(meta, pick, frame, wave, snaps, got):
    second = wave is None
    operands = [meta, pick, frame] + ([] if second else [wave]) + [snaps, got]

    def kernel(*refs):
        velocity_kernel(second, *refs)

    (result,) = call(
        kernel,
        operands,
        [array(6, 64, NP, NE) if second else array(2, NE)],
        [
            pltpu.VMEM((3, 64, NP, NE), f32),
            pltpu.VMEM((2, 3, NP, NP, NE), f32),
            pltpu.VMEM((2, NP, NE), f32),
        ],
    )
    return result


def exchange(send):
    return lax.all_to_all(send, "dom", split_axis=0, concat_axis=0, tiled=True)


def swap_traces(cross, paired):
    ups = [(d, d + 1) for d in range(1, DEV - 1, 2)]
    pairs = [(d, d + 1) for d in range(0, DEV, 2)]
    both = lambda steps: steps + [(b, a) for a, b in steps]
    return lax.ppermute(cross, "dom", both(ups)), lax.ppermute(paired, "dom", both(pairs))


def body(
    adjoint, snapshots, density, lame_lambda, lame_mu, element_order, orient, new_owner, new_slot
):
    rows = [
        x.reshape(1, NE)
        for x in (new_owner, density, lame_lambda, lame_mu, element_order, orient, new_slot)
    ]
    snaps = snapshots.reshape(SNAPS, NM, NE)
    send, meta = pack(rows, adjoint, snaps)
    got = lax.all_to_all(send, "dom", split_axis=0, concat_axis=0, tiled=True)
    wave, *traces, rows, pick, frame = place(meta, got, adjoint)
    stage = 0
    for step in range(STEPS):
        start = wave
        for half in (False, True):
            outer = swap_traces(*traces)
            part, flux = inner(wave, rows)
            base = start if half else None
            if stage == 2:
                strain = velocities(meta, pick, frame, None, snaps, got)
                part, strain = lax.optimization_barrier((part, strain))
            if stage == 3:
                first = velocities(meta, pick, frame, start, snaps, got)
                signed, gradients = update(
                    base, wave, part, flux, traces, outer, rows, (strain, first)
                )
            else:
                wave, *traces = update(base, wave, part, flux, traces, outer, rows)
            stage += 1
    return signed.reshape(FIELDS, NM, NE), gradients


def solution(mesh):
    shard = P("dom")
    in_specs = (P(None, None, "dom"), P(None, None, None, "dom")) + (shard,) * 7
    out_specs = (P(None, None, "dom"), P(None, "dom"))
    return jax.shard_map(body, mesh=mesh, in_specs=in_specs, out_specs=out_specs, check_vma=False)
```

time: 193 us -> 178 us (0.922)
  blocking collectives: 0 us -> 102 us
  waiting for transfers between devices: 75.6 us -> 25.2 us
  starting transfers between devices: 56.5 us -> 9.4 us
  local copies, waits for them, and re-layouts: 13.6 us -> 0.02 us
  Pallas kernels: 43 us -> 40.3 us
    all_to_all x0 -> x1, blocking collectives: none -> 102 us  [body(): got = lax.all_to_all(send, 'dom', split_axis=0, concat_axis=0, tiled=True)]
    all_to_all x2 -> x0, waiting for transfers between devices: 58.8 us -> none  [exchange(): return lax.all_to_all(send, 'dom', split_axis=0, concat_axis=0, tiled=True)]
    ppermute x8, starting transfers between devices: 39.5 us -> 9.4 us  [the longest x4 9.05 us: swap_traces(): lax.ppermute(cross, 'dom', both(ups))]
    all_to_all x2 -> x0, starting transfers between devices: 17 us -> none  [exchange(): return lax.all_to_all(send, 'dom', split_axis=0, concat_axis=0, tiled=True)]
    unnamed x20 -> x6, local copies, waits for them, and re-layouts: 12.9 us -> 0.02 us
    ppermute x8, waiting for transfers between devices: 16.7 us -> 25.2 us  [the longest x4 25.1 us: swap_traces(): lax.ppermute(cross, 'dom', both(ups))]
    pallas_call x12, Pallas kernels: 43 us -> 40.3 us  [call(): pl.pallas_call(kernel, in_specs=[pl.BlockSpec(memory_space=space(n, x)) f...]
  transfers between devices with their start and end apart: 10 -> 8, of which waited for: 5 -> 4; matrix products, arithmetic and copies ran while one was open for 0% -> 0% of each run, Pallas kernels for 16% -> 8%
where the time goes in v2:
time: 178 us
  blocking collectives  102 us (57%)
  Pallas kernels  40.3 us (23%)
  waiting for transfers between devices  25.2 us (14%)
  starting transfers between devices  9.4 us (5%)
    all_to_all x1, blocking collectives, body(): got = lax.all_to_all(send, 'dom', split_axis=0, concat_axis=0, tiled=True)  102 us
    pallas_call x12, Pallas kernels, call(): pl.pallas_call(kernel, in_specs=[pl.BlockSpec(memory_space=space(n, x)) f...  40.3 us
    ppermute x4, waiting for transfers between devices, swap_traces(): lax.ppermute(cross, 'dom', both(ups))  25.1 us
    ppermute x4, starting transfers between devices, swap_traces(): lax.ppermute(cross, 'dom', both(ups))  9.05 us
  transfers between devices with their start and end apart: 8, of which 4 were waited for; matrix products, arithmetic and copies ran while one was open for 0% of the time, Pallas kernels for 8%

profile of v2, /device:TPU:32, one launch (start us, length us, event | category | flops | bytes accessed | tf_op | source)
XLA Modules:
  0.0 177.6 jit_solution(14495808685192761795)
XLA Ops:
  0.6 12.1 %shard_map.104 = (f32[128,120,128]{2,1,0:T(8,128)}, f32[8,128]{1,0:T(8,128)}) custom-call(s32[1,128]{1,0:T(1,128)} %bitcast.12, f32[1,128]{1,0:T(1,128)} %bitcast.13, f32[1,128]{1,0:T(1,128)} %bitcast.14, f32[1,128]{1,0:T(1,128)} %bitcast.15, s32[1,128]{1,0:T(1,128)} %bitcast.16, s32[1,128]{1,0:T(1,128)} %bitcast.17, s32[1,128]{1,0:T(1,128)} %bitcast.18, ...), custom_call_target="tpu_custom_call" | custom-call | tf_op jit(solution)/shard_map/pallas_call | solution.py:37
  12.7 0.0 copy-start.1
  12.8 0.0 copy-start.2
  12.8 102.0 %all_to_all.5.got_ref.refs_4_.refs_5_ = f32[128,120,128]{2,1,0:T(8,128)S(1)} all-to-all(f32[128,120,128]{2,1,0:T(8,128)} %get-tuple-element.32), channel_id=1, replica_groups=mesh['dom'=128] {'dom'}, dimensions={0} | all-to-all | bytes 15728640 | tf_op jit(solution)/shard_map/all_to_all | solution.py:614
  114.8 0.0 copy-done.1
  114.8 0.0 copy-done.2
  114.8 6.3 %shard_map.105 = (f32[9,64,8,128]{3,2,1,0:T(8,128)S(1)}, f32[9,64,128]{2,1,0:T(8,128)S(1)}, f32[9,64,128]{2,1,0:T(8,128)S(1)}, f32[8,128]{1,0:T(8,128)S(1)}, bf1...) custom-call(f32[8,128]{1,0:T(8,128)S(1)} %copy-done.2, f32[128,120,128]{2,1,0:T(8,128)S(1)} %all_to_all.5.got_ref.refs_4_.refs_5_, ...), custom_call_target="tpu_custom_call" | custom-call | tf_op jit(solution)/shard_map/pallas_call | solution.py:37
  121.1 2.2 %collective-permute-start = (f32[9,64,128]{2,1,0:T(8,128)S(1)}, f32[9,64,128]{2,1,0:T(8,128)S(1)}, u32[]{:S(2)}, u32[]{:S(2)}) collective-permute-start(f32[9,64,128]{2,1,0:T(8,128)S(1)} %get-tuple-element.37.refs_3_), channel_id=1, source_target_pairs={{1,2},{3,4},{5,6},{7,8},{9,10},{11,12},{13,14},{15,16},{17,18},{19... | collective-permute-start | bytes 884744 | tf_op jit(solution)/shard_map/ppermute | solution.py:602
  123.3 0.1 collective-permute-start.1
  123.4 2.5 %shard_map.106 = (f32[9,64,8,128]{3,2,1,0:T(8,128)S(1)}, f32[2,9,8,8,128]{4,3,2,1,0:T(8,128)S(1)}) custom-call(f32[9,64,8,128]{3,2,1,0:T(8,128)S(1)} %get-tuple-element.33.wave_ref.refs_0_, f32[8,128]{1,0:T(8,128)S(1)} %get-tuple-element.34.rows_ref.refs_7_.refs_8_), custom_call_target="tpu_custom_call" | custom-call | tf_op jit(solution)/shard_map/pallas_call | solution.py:37
  125.9 7.5 %collective-permute-done.refs_5_ = f32[9,64,128]{2,1,0:T(8,128)S(1)} collective-permute-done((f32[9,64,128]{2,1,0:T(8,128)S(1)}, f32[9,64,128]{2,1,0:T(8,128)S(1)}, u32[]{:S(2)}, u32[]{:S(2)}) %collective-permute-start) | collective-permute-done | bytes 294944 | tf_op jit(solution)/shard_map/ppermute | solution.py:602
  133.4 0.0 collective-permute-done.1.refs_6_
  133.4 1.3 shard_map.107
  134.7 2.2 %collective-permute-start.2 = (f32[9,64,128]{2,1,0:T(8,128)S(1)}, f32[9,64,128]{2,1,0:T(8,128)S(1)}, u32[]{:S(2)}, u32[]{:S(2)}) collective-permute-start(f32[9,64,128]{2,1,0:T(8,128)S(1)} %get-tuple-element.42.refs_4_), channel_id=1, source_target_pairs={{1,2},{3,4},{5,6},{7,8},{9,10},{11,12},{13,14},{15,16},{17,18},{19... | collective-permute-start | bytes 884744 | tf_op jit(solution)/shard_map/ppermute | solution.py:602
  136.9 0.1 collective-permute-start.3
  137.0 2.5 %shard_map.108 = (f32[9,64,8,128]{3,2,1,0:T(8,128)S(1)}, f32[2,9,8,8,128]{4,3,2,1,0:T(8,128)S(1)}) custom-call(f32[9,64,8,128]{3,2,1,0:T(8,128)S(1)} %get-tuple-element.39.wave_ref.refs_1_, f32[8,128]{1,0:T(8,128)S(1)} %get-tuple-element.34.rows_ref.refs_7_.refs_8_), custom_call_target="tpu_custom_call" | custom-call | tf_op jit(solution)/shard_map/pallas_call | solution.py:37
  139.5 7.5 %collective-permute-done.2.refs_6_ = f32[9,64,128]{2,1,0:T(8,128)S(1)} collective-permute-done((f32[9,64,128]{2,1,0:T(8,128)S(1)}, f32[9,64,128]{2,1,0:T(8,128)S(1)}, u32[]{:S(2)}, u32[]{:S(2)}) %collective-permute-start.2) | collective-permute-done | bytes 294944 | tf_op jit(solution)/shard_map/ppermute | solution.py:602
  147.0 0.0 collective-permute-done.3.refs_7_
  147.0 0.0 copy-start
  147.0 1.7 shard_map.109
  148.7 2.2 %collective-permute-start.4 = (f32[9,64,128]{2,1,0:T(8,128)S(1)}, f32[9,64,128]{2,1,0:T(8,128)S(1)}, u32[]{:S(2)}, u32[]{:S(2)}) collective-permute-start(f32[9,64,128]{2,1,0:T(8,128)S(1)} %get-tuple-element.50.refs_3_), channel_id=1, source_target_pairs={{1,2},{3,4},{5,6},{7,8},{9,10},{11,12},{13,14},{15,16},{17,18},{19... | collective-permute-start | bytes 884744 | tf_op jit(solution)/shard_map/ppermute | solution.py:602
  150.9 0.1 collective-permute-start.5
  151.0 0.0 copy-done
  151.0 2.3 %shard_map.111.refs_9_ = f32[6,64,8,128]{3,2,1,0:T(8,128)S(1)} custom-call(f32[8,128]{1,0:T(8,128)S(1)} %copy-done.2, bf16[128,256]{1,0:T(8,128)(2,1)S(1)} %get-tuple-element.46.refs_1_, f32[512,128]{1,0:T(8,128)S(1)} %get-tuple-element.47.refs_2_, f32[6,512,128]{2,1,0:T(8,128)S(1)} %bitcast.10, f32[128,120,128]{2,1,0:T(8,128)S(1)} %all_to_all.5.got_ref.refs_4_.refs_5_), custom_call_target="tpu_custom_call" | custom-call | tf_op jit(solution)/shard_map/pallas_call | solution.py:37
  153.3 2.5 %shard_map.110 = (f32[9,64,8,128]{3,2,1,0:T(8,128)S(1)}, f32[2,9,8,8,128]{4,3,2,1,0:T(8,128)S(1)}) custom-call(f32[9,64,8,128]{3,2,1,0:T(8,128)S(1)} %get-tuple-element.44.wave_ref.refs_0_.refs_3_, f32[8,128]{1,0:T(8,128)S(1)} %get-tuple-element.34.rows_ref.refs_7_.refs_8_), custom_call_target="tpu_custom_call" | custom-call | tf_op jit(solution)/shard_map/pallas_call | solution.py:37
  155.8 5.2 %collective-permute-done.4.refs_5_ = f32[9,64,128]{2,1,0:T(8,128)S(1)} collective-permute-done((f32[9,64,128]{2,1,0:T(8,128)S(1)}, f32[9,64,128]{2,1,0:T(8,128)S(1)}, u32[]{:S(2)}, u32[]{:S(2)}) %collective-permute-start.4) | collective-permute-done | bytes 294944 | tf_op jit(solution)/shard_map/ppermute | solution.py:602
  160.9 0.0 collective-permute-done.5.refs_6_
  161.0 1.4 shard_map.112
  162.3 2.4 %collective-permute-start.6 = (f32[9,64,128]{2,1,0:T(8,128)S(1)}, f32[9,64,128]{2,1,0:T(8,128)S(1)}, u32[]{:S(2)}, u32[]{:S(2)}) collective-permute-start(f32[9,64,128]{2,1,0:T(8,128)S(1)} %get-tuple-element.55.refs_4_), channel_id=1, source_target_pairs={{1,2},{3,4},{5,6},{7,8},{9,10},{11,12},{13,14},{15,16},{17,18},{19... | collective-permute-start | bytes 884744 | tf_op jit(solution)/shard_map/ppermute | solution.py:602
  164.8 0.1 collective-permute-start.7
  164.8 2.3 %shard_map.114.refs_10_ = f32[2,128]{1,0:T(2,128)S(1)} custom-call(f32[8,128]{1,0:T(8,128)S(1)} %copy-done.2, bf16[128,256]{1,0:T(8,128)(2,1)S(1)} %get-tuple-element.46.refs_1_, f32[512,128]{1,0:T(8,128)S(1)} %get-tuple-element.47.refs_2_, f32[9,64,8,128]{3,2,1,0:T(8,128)S(1)} %get-tuple-element.44.wave_ref.refs_0_.refs_3_, f32[6,512,128]{2,1,0:T(8,128)S(1)} %bitcast.11, ...), custom_call_target="tpu_custom_call" | custom-call | tf_op jit(solution)/shard_map/pallas_call | solution.py:37
  167.1 2.5 %shard_map.113 = (f32[9,64,8,128]{3,2,1,0:T(8,128)S(1)}, f32[2,9,8,8,128]{4,3,2,1,0:T(8,128)S(1)}) custom-call(f32[9,64,8,128]{3,2,1,0:T(8,128)S(1)} %get-tuple-element.52.wave_ref.refs_1_, f32[8,128]{1,0:T(8,128)S(1)} %get-tuple-element.34.rows_ref.refs_7_.refs_8_), custom_call_target="tpu_custom_call" | custom-call | tf_op jit(solution)/shard_map/pallas_call | solution.py:37
  169.6 5.0 %collective-permute-done.6.refs_6_ = f32[9,64,128]{2,1,0:T(8,128)S(1)} collective-permute-done((f32[9,64,128]{2,1,0:T(8,128)S(1)}, f32[9,64,128]{2,1,0:T(8,128)S(1)}, u32[]{:S(2)}, u32[]{:S(2)}) %collective-permute-start.6) | collective-permute-done | bytes 294944 | tf_op jit(solution)/shard_map/ppermute | solution.py:602
  174.6 0.0 collective-permute-done.7.refs_7_
  174.6 3.0 %shard_map.115 = (f32[9,64,8,128]{3,2,1,0:T(8,128)}, f32[2,128]{1,0:T(2,128)}) custom-call(f32[9,64,8,128]{3,2,1,0:T(8,128)S(1)} %get-tuple-element.44.wave_ref.refs_0_.refs_3_, f32[9,64,8,128]{3,2,1,0:T(8,128)S(1)} %get-tuple-element.52.wave_ref.refs_1_, f32[9,64,8,128]{3,2,1,0:T(8,128)S(1)} %get-tuple-element.53.refs_2_, ...), custom_call_target="tpu_custom_call" | custom-call | tf_op jit(solution)/shard_map/pallas_call | solution.py:37
Async XLA Ops:
  12.7 102.0 %copy-start.1 = (f32[9,512,128]{2,1,0:T(8,128)S(1)}, f32[9,512,128]{2,1,0:T(8,128)}, u32[]{:S(2)}) copy-start(f32[9,512,128]{2,1,0:T(8,128)} %adj_ref.1) | copy-start | bytes 7077892
  12.8 102.0 %copy-start.2 = (f32[8,128]{1,0:T(8,128)S(1)}, f32[8,128]{1,0:T(8,128)}, u32[]{:S(2)}) copy-start(f32[8,128]{1,0:T(8,128)} %get-tuple-element.31.meta_ref.refs_0_) | copy-start | bytes 12292
  121.1 12.3 %collective-permute-start = (f32[9,64,128]{2,1,0:T(8,128)S(1)}, f32[9,64,128]{2,1,0:T(8,128)S(1)}, u32[]{:S(2)}, u32[]{:S(2)}) collective-permute-start(f32[9,64,128]{2,1,0:T(8,128)S(1)} %get-tuple-element.37.refs_3_), channel_id=1, source_target_pairs={{1,2},{3,4},{5,6},{7,8},{9,10},{11,12},{13,14},{15,16},{17,18},{19... | collective-permute-start | bytes 884744 | tf_op jit(solution)/shard_map/ppermute | solution.py:602
  123.3 10.0 %collective-permute-start.1 = (f32[9,64,128]{2,1,0:T(8,128)S(1)}, f32[9,64,128]{2,1,0:T(8,128)S(1)}, u32[]{:S(2)}, u32[]{:S(2)}) collective-permute-start(f32[9,64,128]{2,1,0:T(8,128)S(1)} %get-tuple-element.38.refs_4_), channel_id=1, source_target_pairs={{0,1},{2,3},{4,5},{6,7},{8,9},{10,11},{12,13},{14,15},{16,17},{18,... | collective-permute-start | bytes 884744 | tf_op jit(solution)/shard_map/ppermute | solution.py:602
  134.7 12.3 %collective-permute-start.2 = (f32[9,64,128]{2,1,0:T(8,128)S(1)}, f32[9,64,128]{2,1,0:T(8,128)S(1)}, u32[]{:S(2)}, u32[]{:S(2)}) collective-permute-start(f32[9,64,128]{2,1,0:T(8,128)S(1)} %get-tuple-element.42.refs_4_), channel_id=1, source_target_pairs={{1,2},{3,4},{5,6},{7,8},{9,10},{11,12},{13,14},{15,16},{17,18},{19... | collective-permute-start | bytes 884744 | tf_op jit(solution)/shard_map/ppermute | solution.py:602
  136.9 10.0 %collective-permute-start.3 = (f32[9,64,128]{2,1,0:T(8,128)S(1)}, f32[9,64,128]{2,1,0:T(8,128)S(1)}, u32[]{:S(2)}, u32[]{:S(2)}) collective-permute-start(f32[9,64,128]{2,1,0:T(8,128)S(1)} %get-tuple-element.43.refs_5_), channel_id=1, source_target_pairs={{0,1},{2,3},{4,5},{6,7},{8,9},{10,11},{12,13},{14,15},{16,17},{18,... | collective-permute-start | bytes 884744 | tf_op jit(solution)/shard_map/ppermute | solution.py:602
  147.0 4.0 %copy-start = (f32[2,3,512,128]{3,2,1,0:T(8,128)S(1)}, f32[2,3,512,128]{3,2,1,0:T(8,128)}, u32[]{:S(2)}) copy-start(f32[2,3,512,128]{3,2,1,0:T(8,128)} %param.10) | copy-start | bytes 4718596
  148.7 12.3 %collective-permute-start.4 = (f32[9,64,128]{2,1,0:T(8,128)S(1)}, f32[9,64,128]{2,1,0:T(8,128)S(1)}, u32[]{:S(2)}, u32[]{:S(2)}) collective-permute-start(f32[9,64,128]{2,1,0:T(8,128)S(1)} %get-tuple-element.50.refs_3_), channel_id=1, source_target_pairs={{1,2},{3,4},{5,6},{7,8},{9,10},{11,12},{13,14},{15,16},{17,18},{19... | collective-permute-start | bytes 884744 | tf_op jit(solution)/shard_map/ppermute | solution.py:602
  150.9 10.0 %collective-permute-start.5 = (f32[9,64,128]{2,1,0:T(8,128)S(1)}, f32[9,64,128]{2,1,0:T(8,128)S(1)}, u32[]{:S(2)}, u32[]{:S(2)}) collective-permute-start(f32[9,64,128]{2,1,0:T(8,128)S(1)} %get-tuple-element.51.refs_4_), channel_id=1, source_target_pairs={{0,1},{2,3},{4,5},{6,7},{8,9},{10,11},{12,13},{14,15},{16,17},{18,... | collective-permute-start | bytes 884744 | tf_op jit(solution)/shard_map/ppermute | solution.py:602
  162.3 12.3 %collective-permute-start.6 = (f32[9,64,128]{2,1,0:T(8,128)S(1)}, f32[9,64,128]{2,1,0:T(8,128)S(1)}, u32[]{:S(2)}, u32[]{:S(2)}) collective-permute-start(f32[9,64,128]{2,1,0:T(8,128)S(1)} %get-tuple-element.55.refs_4_), channel_id=1, source_target_pairs={{1,2},{3,4},{5,6},{7,8},{9,10},{11,12},{13,14},{15,16},{17,18},{19... | collective-permute-start | bytes 884744 | tf_op jit(solution)/shard_map/ppermute | solution.py:602
  164.8 9.9 %collective-permute-start.7 = (f32[9,64,128]{2,1,0:T(8,128)S(1)}, f32[9,64,128]{2,1,0:T(8,128)S(1)}, u32[]{:S(2)}, u32[]{:S(2)}) collective-permute-start(f32[9,64,128]{2,1,0:T(8,128)S(1)} %get-tuple-element.56.refs_5_), channel_id=1, source_target_pairs={{0,1},{2,3},{4,5},{6,7},{8,9},{10,11},{12,13},{14,15},{16,17},{18,... | collective-permute-start | bytes 884744 | tf_op jit(solution)/shard_map/ppermute | solution.py:602

commit v3 on v2

--- a/solution.py
+++ b/solution.py
@@ -56,9 +56,13 @@
     parts = jnp.concatenate(split3(x), axis=1)
     hots = jnp.concatenate([hot, hot, hot], axis=1)
     rows = lax.dot_general(hots, parts, (((1,), (1,)), ((), ())), preferred_element_type=f32)
-    for r in range(2):
-        for q in range(4):
-            out_ref[:, row + r * 4 + q, :] = rows[r * DEV : (r + 1) * DEV, q * 128 : (q + 1) * 128]
+    groups = [
+        rows[r * DEV : (r + 1) * DEV, q * 128 : (q + 1) * 128].reshape(DEV // 8, 8, 128)
+        for r in range(2)
+        for q in range(4)
+    ]
+    tiles = jnp.swapaxes(jnp.stack(groups, axis=1), 1, 2)
+    out_ref[:, row : row + 8, :] = tiles.reshape(DEV, 8, 128)
 
 
 def pack_kernel(*refs):
@@ -145,9 +149,9 @@
 
 
 def gather_elements(pick, got_ref, row):
-    slots = [
-        jnp.concatenate([got_ref[:, row + r * 4 + q, :] for q in range(4)], axis=1) for r in range(2)
-    ]
+    tiles = jnp.swapaxes(got_ref[:, row : row + 8, :].reshape(DEV // 8, 8, 8, 128), 1, 2)
+    rows = [tiles[:, n].reshape(DEV, 128) for n in range(8)]
+    slots = [jnp.concatenate(rows[4 * r : 4 * r + 4], axis=1) for r in range(2)]
     return select_slots(pick, jnp.concatenate(slots, axis=0))
 
 

time: 178 us -> 173 us (0.972)
  Pallas kernels: 40.3 us -> 34.4 us
    pallas_call x12, Pallas kernels: 40.3 us -> 34.4 us  [call(): pl.pallas_call(kernel, in_specs=[pl.BlockSpec(memory_space=space(n, x)) f...]
where the time goes in v3:
time: 173 us
  blocking collectives  102 us (59%)
  Pallas kernels  34.4 us (20%)
  waiting for transfers between devices  26.5 us (15%)
  starting transfers between devices  9.23 us (5%)
    all_to_all x1, blocking collectives, body(): got = lax.all_to_all(send, 'dom', split_axis=0, concat_axis=0, tiled=True)  102 us
    pallas_call x12, Pallas kernels, call(): pl.pallas_call(kernel, in_specs=[pl.BlockSpec(memory_space=space(n, x)) f...  34.4 us
    ppermute x4, waiting for transfers between devices, swap_traces(): lax.ppermute(cross, 'dom', both(ups))  26.5 us
    ppermute x4, starting transfers between devices, swap_traces(): lax.ppermute(cross, 'dom', both(ups))  8.89 us
  transfers between devices with their start and end apart: 8, of which 4 were waited for; matrix products, arithmetic and copies ran while one was open for 0% of the time, Pallas kernels for 8%

profile of v3, /device:TPU:32, one launch (start us, length us, event | category | flops | bytes accessed | tf_op | source)
XLA Modules:
  0.0 173.0 jit_solution(10400820436561925443)
XLA Ops:
  0.6 9.2 %shard_map.104 = (f32[128,120,128]{2,1,0:T(8,128)}, f32[8,128]{1,0:T(8,128)}) custom-call(s32[1,128]{1,0:T(1,128)} %bitcast.12, f32[1,128]{1,0:T(1,128)} %bitcast.13, f32[1,128]{1,0:T(1,128)} %bitcast.14, f32[1,128]{1,0:T(1,128)} %bitcast.15, s32[1,128]{1,0:T(1,128)} %bitcast.16, s32[1,128]{1,0:T(1,128)} %bitcast.17, s32[1,128]{1,0:T(1,128)} %bitcast.18, ...), custom_call_target="tpu_custom_call" | custom-call | tf_op jit(solution)/shard_map/pallas_call | solution.py:37
  9.9 0.0 copy-start.1
  9.9 0.0 copy-start.2
  9.9 102.0 %all_to_all.5.got_ref.refs_4_.refs_5_ = f32[128,120,128]{2,1,0:T(8,128)S(1)} all-to-all(f32[128,120,128]{2,1,0:T(8,128)} %get-tuple-element.32), channel_id=1, replica_groups=mesh['dom'=128] {'dom'}, dimensions={0} | all-to-all | bytes 15728640 | tf_op jit(solution)/shard_map/all_to_all | solution.py:618
  111.9 0.0 copy-done.1
  111.9 0.0 copy-done.2
  111.9 4.6 %shard_map.105 = (f32[9,64,8,128]{3,2,1,0:T(8,128)S(1)}, f32[9,64,128]{2,1,0:T(8,128)S(1)}, f32[9,64,128]{2,1,0:T(8,128)S(1)}, f32[8,128]{1,0:T(8,128)S(1)}, bf1...) custom-call(f32[8,128]{1,0:T(8,128)S(1)} %copy-done.2, f32[128,120,128]{2,1,0:T(8,128)S(1)} %all_to_all.5.got_ref.refs_4_.refs_5_, ...), custom_call_target="tpu_custom_call" | custom-call | tf_op jit(solution)/shard_map/pallas_call | solution.py:37
  116.5 2.2 %collective-permute-start = (f32[9,64,128]{2,1,0:T(8,128)S(1)}, f32[9,64,128]{2,1,0:T(8,128)S(1)}, u32[]{:S(2)}, u32[]{:S(2)}) collective-permute-start(f32[9,64,128]{2,1,0:T(8,128)S(1)} %get-tuple-element.37.refs_3_), channel_id=1, source_target_pairs={{1,2},{3,4},{5,6},{7,8},{9,10},{11,12},{13,14},{15,16},{17,18},{19... | collective-permute-start | bytes 884744 | tf_op jit(solution)/shard_map/ppermute | solution.py:606
  118.7 0.1 collective-permute-start.1
  118.8 2.5 %shard_map.106 = (f32[9,64,8,128]{3,2,1,0:T(8,128)S(1)}, f32[2,9,8,8,128]{4,3,2,1,0:T(8,128)S(1)}) custom-call(f32[9,64,8,128]{3,2,1,0:T(8,128)S(1)} %get-tuple-element.33.wave_ref.refs_0_, f32[8,128]{1,0:T(8,128)S(1)} %get-tuple-element.34.rows_ref.refs_7_.refs_8_), custom_call_target="tpu_custom_call" | custom-call | tf_op jit(solution)/shard_map/pallas_call | solution.py:37
  121.3 7.5 %collective-permute-done.refs_5_ = f32[9,64,128]{2,1,0:T(8,128)S(1)} collective-permute-done((f32[9,64,128]{2,1,0:T(8,128)S(1)}, f32[9,64,128]{2,1,0:T(8,128)S(1)}, u32[]{:S(2)}, u32[]{:S(2)}) %collective-permute-start) | collective-permute-done | bytes 294944 | tf_op jit(solution)/shard_map/ppermute | solution.py:606
  128.8 0.0 collective-permute-done.1.refs_6_
  128.8 1.3 shard_map.107
  130.1 2.2 %collective-permute-start.2 = (f32[9,64,128]{2,1,0:T(8,128)S(1)}, f32[9,64,128]{2,1,0:T(8,128)S(1)}, u32[]{:S(2)}, u32[]{:S(2)}) collective-permute-start(f32[9,64,128]{2,1,0:T(8,128)S(1)} %get-tuple-element.42.refs_4_), channel_id=1, source_target_pairs={{1,2},{3,4},{5,6},{7,8},{9,10},{11,12},{13,14},{15,16},{17,18},{19... | collective-permute-start | bytes 884744 | tf_op jit(solution)/shard_map/ppermute | solution.py:606
  132.3 0.1 collective-permute-start.3
  132.4 2.5 %shard_map.108 = (f32[9,64,8,128]{3,2,1,0:T(8,128)S(1)}, f32[2,9,8,8,128]{4,3,2,1,0:T(8,128)S(1)}) custom-call(f32[9,64,8,128]{3,2,1,0:T(8,128)S(1)} %get-tuple-element.39.wave_ref.refs_1_, f32[8,128]{1,0:T(8,128)S(1)} %get-tuple-element.34.rows_ref.refs_7_.refs_8_), custom_call_target="tpu_custom_call" | custom-call | tf_op jit(solution)/shard_map/pallas_call | solution.py:37
  134.9 7.5 %collective-permute-done.2.refs_6_ = f32[9,64,128]{2,1,0:T(8,128)S(1)} collective-permute-done((f32[9,64,128]{2,1,0:T(8,128)S(1)}, f32[9,64,128]{2,1,0:T(8,128)S(1)}, u32[]{:S(2)}, u32[]{:S(2)}) %collective-permute-start.2) | collective-permute-done | bytes 294944 | tf_op jit(solution)/shard_map/ppermute | solution.py:606
  142.4 0.0 collective-permute-done.3.refs_7_
  142.4 0.0 copy-start
  142.4 1.7 shard_map.109
  144.1 2.2 %collective-permute-start.4 = (f32[9,64,128]{2,1,0:T(8,128)S(1)}, f32[9,64,128]{2,1,0:T(8,128)S(1)}, u32[]{:S(2)}, u32[]{:S(2)}) collective-permute-start(f32[9,64,128]{2,1,0:T(8,128)S(1)} %get-tuple-element.50.refs_3_), channel_id=1, source_target_pairs={{1,2},{3,4},{5,6},{7,8},{9,10},{11,12},{13,14},{15,16},{17,18},{19... | collective-permute-start | bytes 884744 | tf_op jit(solution)/shard_map/ppermute | solution.py:606
  146.3 0.1 collective-permute-start.5
  146.4 0.0 copy-done
  146.4 1.7 shard_map.111.refs_9_
  148.1 2.5 %shard_map.110 = (f32[9,64,8,128]{3,2,1,0:T(8,128)S(1)}, f32[2,9,8,8,128]{4,3,2,1,0:T(8,128)S(1)}) custom-call(f32[9,64,8,128]{3,2,1,0:T(8,128)S(1)} %get-tuple-element.44.wave_ref.refs_0_.refs_3_, f32[8,128]{1,0:T(8,128)S(1)} %get-tuple-element.34.rows_ref.refs_7_.refs_8_), custom_call_target="tpu_custom_call" | custom-call | tf_op jit(solution)/shard_map/pallas_call | solution.py:37
  150.5 5.8 %collective-permute-done.4.refs_5_ = f32[9,64,128]{2,1,0:T(8,128)S(1)} collective-permute-done((f32[9,64,128]{2,1,0:T(8,128)S(1)}, f32[9,64,128]{2,1,0:T(8,128)S(1)}, u32[]{:S(2)}, u32[]{:S(2)}) %collective-permute-start.4) | collective-permute-done | bytes 294944 | tf_op jit(solution)/shard_map/ppermute | solution.py:606
  156.3 0.0 collective-permute-done.5.refs_6_
  156.3 1.4 shard_map.112
  157.7 2.2 %collective-permute-start.6 = (f32[9,64,128]{2,1,0:T(8,128)S(1)}, f32[9,64,128]{2,1,0:T(8,128)S(1)}, u32[]{:S(2)}, u32[]{:S(2)}) collective-permute-start(f32[9,64,128]{2,1,0:T(8,128)S(1)} %get-tuple-element.55.refs_4_), channel_id=1, source_target_pairs={{1,2},{3,4},{5,6},{7,8},{9,10},{11,12},{13,14},{15,16},{17,18},{19... | collective-permute-start | bytes 884744 | tf_op jit(solution)/shard_map/ppermute | solution.py:606
  160.0 0.1 collective-permute-start.7
  160.0 1.7 shard_map.114.refs_10_
  161.7 2.5 %shard_map.113 = (f32[9,64,8,128]{3,2,1,0:T(8,128)S(1)}, f32[2,9,8,8,128]{4,3,2,1,0:T(8,128)S(1)}) custom-call(f32[9,64,8,128]{3,2,1,0:T(8,128)S(1)} %get-tuple-element.52.wave_ref.refs_1_, f32[8,128]{1,0:T(8,128)S(1)} %get-tuple-element.34.rows_ref.refs_7_.refs_8_), custom_call_target="tpu_custom_call" | custom-call | tf_op jit(solution)/shard_map/pallas_call | solution.py:37
  164.2 5.8 %collective-permute-done.6.refs_6_ = f32[9,64,128]{2,1,0:T(8,128)S(1)} collective-permute-done((f32[9,64,128]{2,1,0:T(8,128)S(1)}, f32[9,64,128]{2,1,0:T(8,128)S(1)}, u32[]{:S(2)}, u32[]{:S(2)}) %collective-permute-start.6) | collective-permute-done | bytes 294944 | tf_op jit(solution)/shard_map/ppermute | solution.py:606
  170.0 0.0 collective-permute-done.7.refs_7_
  170.0 3.0 %shard_map.115 = (f32[9,64,8,128]{3,2,1,0:T(8,128)}, f32[2,128]{1,0:T(2,128)}) custom-call(f32[9,64,8,128]{3,2,1,0:T(8,128)S(1)} %get-tuple-element.44.wave_ref.refs_0_.refs_3_, f32[9,64,8,128]{3,2,1,0:T(8,128)S(1)} %get-tuple-element.52.wave_ref.refs_1_, f32[9,64,8,128]{3,2,1,0:T(8,128)S(1)} %get-tuple-element.53.refs_2_, ...), custom_call_target="tpu_custom_call" | custom-call | tf_op jit(solution)/shard_map/pallas_call | solution.py:37
Async XLA Ops:
  9.9 102.0 %copy-start.1 = (f32[9,512,128]{2,1,0:T(8,128)S(1)}, f32[9,512,128]{2,1,0:T(8,128)}, u32[]{:S(2)}) copy-start(f32[9,512,128]{2,1,0:T(8,128)} %adj_ref.1) | copy-start | bytes 7077892
  9.9 102.0 %copy-start.2 = (f32[8,128]{1,0:T(8,128)S(1)}, f32[8,128]{1,0:T(8,128)}, u32[]{:S(2)}) copy-start(f32[8,128]{1,0:T(8,128)} %get-tuple-element.31.meta_ref.refs_0_) | copy-start | bytes 12292
  116.5 12.3 %collective-permute-start = (f32[9,64,128]{2,1,0:T(8,128)S(1)}, f32[9,64,128]{2,1,0:T(8,128)S(1)}, u32[]{:S(2)}, u32[]{:S(2)}) collective-permute-start(f32[9,64,128]{2,1,0:T(8,128)S(1)} %get-tuple-element.37.refs_3_), channel_id=1, source_target_pairs={{1,2},{3,4},{5,6},{7,8},{9,10},{11,12},{13,14},{15,16},{17,18},{19... | collective-permute-start | bytes 884744 | tf_op jit(solution)/shard_map/ppermute | solution.py:606
  118.7 10.0 %collective-permute-start.1 = (f32[9,64,128]{2,1,0:T(8,128)S(1)}, f32[9,64,128]{2,1,0:T(8,128)S(1)}, u32[]{:S(2)}, u32[]{:S(2)}) collective-permute-start(f32[9,64,128]{2,1,0:T(8,128)S(1)} %get-tuple-element.38.refs_4_), channel_id=1, source_target_pairs={{0,1},{2,3},{4,5},{6,7},{8,9},{10,11},{12,13},{14,15},{16,17},{18,... | collective-permute-start | bytes 884744 | tf_op jit(solution)/shard_map/ppermute | solution.py:606
  130.1 12.3 %collective-permute-start.2 = (f32[9,64,128]{2,1,0:T(8,128)S(1)}, f32[9,64,128]{2,1,0:T(8,128)S(1)}, u32[]{:S(2)}, u32[]{:S(2)}) collective-permute-start(f32[9,64,128]{2,1,0:T(8,128)S(1)} %get-tuple-element.42.refs_4_), channel_id=1, source_target_pairs={{1,2},{3,4},{5,6},{7,8},{9,10},{11,12},{13,14},{15,16},{17,18},{19... | collective-permute-start | bytes 884744 | tf_op jit(solution)/shard_map/ppermute | solution.py:606
  132.3 10.0 %collective-permute-start.3 = (f32[9,64,128]{2,1,0:T(8,128)S(1)}, f32[9,64,128]{2,1,0:T(8,128)S(1)}, u32[]{:S(2)}, u32[]{:S(2)}) collective-permute-start(f32[9,64,128]{2,1,0:T(8,128)S(1)} %get-tuple-element.43.refs_5_), channel_id=1, source_target_pairs={{0,1},{2,3},{4,5},{6,7},{8,9},{10,11},{12,13},{14,15},{16,17},{18,... | collective-permute-start | bytes 884744 | tf_op jit(solution)/shard_map/ppermute | solution.py:606
  142.4 4.0 %copy-start = (f32[2,3,512,128]{3,2,1,0:T(8,128)S(1)}, f32[2,3,512,128]{3,2,1,0:T(8,128)}, u32[]{:S(2)}) copy-start(f32[2,3,512,128]{3,2,1,0:T(8,128)} %param.10) | copy-start | bytes 4718596
  144.1 12.3 %collective-permute-start.4 = (f32[9,64,128]{2,1,0:T(8,128)S(1)}, f32[9,64,128]{2,1,0:T(8,128)S(1)}, u32[]{:S(2)}, u32[]{:S(2)}) collective-permute-start(f32[9,64,128]{2,1,0:T(8,128)S(1)} %get-tuple-element.50.refs_3_), channel_id=1, source_target_pairs={{1,2},{3,4},{5,6},{7,8},{9,10},{11,12},{13,14},{15,16},{17,18},{19... | collective-permute-start | bytes 884744 | tf_op jit(solution)/shard_map/ppermute | solution.py:606
  146.3 10.0 %collective-permute-start.5 = (f32[9,64,128]{2,1,0:T(8,128)S(1)}, f32[9,64,128]{2,1,0:T(8,128)S(1)}, u32[]{:S(2)}, u32[]{:S(2)}) collective-permute-start(f32[9,64,128]{2,1,0:T(8,128)S(1)} %get-tuple-element.51.refs_4_), channel_id=1, source_target_pairs={{0,1},{2,3},{4,5},{6,7},{8,9},{10,11},{12,13},{14,15},{16,17},{18,... | collective-permute-start | bytes 884744 | tf_op jit(solution)/shard_map/ppermute | solution.py:606
  157.7 12.3 %collective-permute-start.6 = (f32[9,64,128]{2,1,0:T(8,128)S(1)}, f32[9,64,128]{2,1,0:T(8,128)S(1)}, u32[]{:S(2)}, u32[]{:S(2)}) collective-permute-start(f32[9,64,128]{2,1,0:T(8,128)S(1)} %get-tuple-element.55.refs_4_), channel_id=1, source_target_pairs={{1,2},{3,4},{5,6},{7,8},{9,10},{11,12},{13,14},{15,16},{17,18},{19... | collective-permute-start | bytes 884744 | tf_op jit(solution)/shard_map/ppermute | solution.py:606
  160.0 10.0 %collective-permute-start.7 = (f32[9,64,128]{2,1,0:T(8,128)S(1)}, f32[9,64,128]{2,1,0:T(8,128)S(1)}, u32[]{:S(2)}, u32[]{:S(2)}) collective-permute-start(f32[9,64,128]{2,1,0:T(8,128)S(1)} %get-tuple-element.56.refs_5_), channel_id=1, source_target_pairs={{0,1},{2,3},{4,5},{6,7},{8,9},{10,11},{12,13},{14,15},{16,17},{18,... | collective-permute-start | bytes 884744 | tf_op jit(solution)/shard_map/ppermute | solution.py:606

commit v4 on v3

--- a/solution.py
+++ b/solution.py
@@ -314,7 +314,14 @@
     return x + pltpu.roll(x, 4, 0) * keep4
 
 
-def inner_kernel(wave_ref, rows_ref, out_ref, flux_ref, run_ref, fluxy_ref):
+def inner_kernel(step, *refs):
+    if step is None:
+        wave_ref, rows_ref, out_ref, flux_ref, run_ref, fluxy_ref = refs
+    else:
+        (begun_ref, fluxz_ref, rows_ref, wave_ref, out_ref, flux_ref, run_ref,
+         fluxy_ref) = refs
+        order = jnp.broadcast_to(rows_ref[4:5, :], (NP, NE))
+        k = lax.broadcasted_iota(jnp.int32, (NP, NE), 0)
     rinv, lam, mu, speed = materials(rows_ref)
     keeps_x, keeps_y = lane_keeps()
     keep1, keep2, keep4, factor_z = mode_rows()
@@ -325,6 +332,14 @@
         i = NP - 1 - g
         parity = lax.rem(i, 2)
         factor_x = (2 * i + 1).astype(f32)
+
+        if step is not None:
+            at = pl.multiple_of(i * NP, NP)
+            scales = [factor_z * mask for mask in order_masks(order, k, i, step)]
+            for f in range(FIELDS):
+                for j in range(NP):
+                    lifted = lifted_row(fluxz_ref, f, at + j, k)
+                    wave_ref[f, at + j] = begun_ref[f, at + j] + scales[j] * lifted
 
         evens, odds = [], []
         for f in range(FIELDS):
@@ -389,32 +404,140 @@
 
 def inner(wave, rows):
     return call(
-        inner_kernel,
+        lambda *refs: inner_kernel(None, *refs),
         (wave, rows),
         [array(FIELDS, 64, NP, NE), array(2, FIELDS, NP, NP, NE)],
         [pltpu.VMEM((2, FIELDS, NP, NP, NE), f32), pltpu.VMEM((2, FIELDS, NP, NE), f32)],
     )
 
 
-def update_kernel(last, half, *refs):
+def complete(begun, fluxz, rows, step):
+    return call(
+        lambda *refs: inner_kernel(step, *refs),
+        (begun, fluxz, rows),
+        [
+            array(FIELDS, 64, NP, NE),
+            array(FIELDS, 64, NP, NE),
+            array(2, FIELDS, NP, NP, NE),
+        ],
+        [pltpu.VMEM((2, FIELDS, NP, NP, NE), f32), pltpu.VMEM((2, FIELDS, NP, NE), f32)],
+    )
+
+
+def order_masks(order, k, i, step):
+    highest = [jnp.maximum(k, jnp.maximum(i, j)).astype(f32) for j in range(NP)]
+    return [jnp.where(h <= order, step, 0.0) for h in highest]
+
+
+def lifted_row(fluxz_ref, f, at, k):
+    return jnp.where(
+        k % 2 == 0,
+        jnp.broadcast_to(fluxz_ref[0, f, pl.ds(at, 1), :], (NP, NE)),
+        jnp.broadcast_to(fluxz_ref[1, f, pl.ds(at, 1), :], (NP, NE)),
+    )
+
+
+def begin_kernel(half, *refs):
     refs = list(refs)
     base_ref = refs.pop(0) if half else None
-    (wave_ref, part_ref, flux_ref, cross_ref, paired_ref, got_cross_ref, got_paired_ref,
-     rows_ref, *rest) = refs
-    if last:
-        strain_ref, first_ref, out_ref, gradient_ref, fluxz_ref, sums_ref = rest
-        sums_ref[...] = jnp.zeros_like(sums_ref)
-    else:
-        out_ref, out_cross_ref, out_paired_ref, fluxz_ref = rest
+    wave_ref, part_ref, flux_ref, rows_ref, out_ref, cross_ref, paired_ref = refs
+    order = jnp.broadcast_to(rows_ref[4:5, :], (NP, NE))
+    odd = odd_device()
+    k = lax.broadcasted_iota(jnp.int32, (NP, NE), 0)
+
+    @pl.loop(0, NP)
+    def _(i):
+        parity = lax.rem(i, 2)
+        factor_x = (2 * i + 1).astype(f32)
+        at = pl.multiple_of(i * NP, NP)
+        rows = pl.ds(at, NP)
+        masks = order_masks(order, k, i, 0.5 * DT if half else DT)
+        for f in range(FIELDS):
+            fresh = []
+            for j in range(NP):
+                slope = part_ref[f, at + j] + factor_x * flux_ref[parity, f, j]
+                start = wave_ref[f, at + j]
+                if half:
+                    start = 0.5 * (base_ref[f, at + j] + start)
+                new = start + masks[j] * slope
+                out_ref[f, at + j] = new
+                fresh.append(new)
+            upper, lower = face_traces(fresh, k)
+            cross_ref[f, rows] = jnp.where(odd, upper, lower)
+            paired_ref[f, rows] = jnp.where(odd, lower, upper)
+
+
+def begin(base, wave, part, flux, rows):
+    half = base is not None
+    return call(
+        lambda *refs: begin_kernel(half, *refs),
+        ([base] if half else []) + [wave, part, flux, rows],
+        [array(FIELDS, 64, NP, NE), array(FIELDS, 64, NE), array(FIELDS, 64, NE)],
+    )
+
+
+def outer_kernel(
+    step, cross_ref, paired_ref, got_cross_ref, got_paired_ref, begun_cross_ref,
+    begun_paired_ref, rows_ref, fluxz_ref, out_cross_ref, out_paired_ref,
+):
+    rinv, lam, mu, speed = materials(rows_ref)
+    order = jnp.broadcast_to(rows_ref[4:5, :], (NP, NE))
+    side = jnp.where(odd_device(), 1.0, -1.0)
+    j = lax.broadcasted_iota(jnp.int32, (NP, NE), 0)
+
+    def factors(first):
+        total = jnp.zeros((NP, NE), f32)
+        for n in range(first, NP, 2):
+            total = total + jnp.where(order >= float(n), 2.0 * n + 1.0, 0.0)
+        return step * total
+
+    factor_even, factor_odd = factors(0), side * factors(1)
+
+    @pl.loop(0, NP)
+    def _(i):
+        rows = pl.ds(pl.multiple_of(i * NP, NP), NP)
+        total, difference = [], []
+        for f in range(FIELDS):
+            jump_cross = cross_ref[f, rows] - got_cross_ref[f, rows]
+            jump_paired = paired_ref[f, rows] - got_paired_ref[f, rows]
+            total.append(jump_cross + jump_paired)
+            difference.append(side * (jump_cross - jump_paired))
+        even, odds = face_flux(total, difference, 2, rinv, lam, mu, speed)
+        allowed = jnp.where(jnp.maximum(j, i).astype(f32) <= order, 1.0, 0.0)
+        scale_even, scale_odd = allowed * factor_even, allowed * factor_odd
+        for f in range(FIELDS):
+            fluxz_ref[0, f, rows] = even[f]
+            fluxz_ref[1, f, rows] = odds[f]
+            from_even, from_odd = scale_even * even[f], scale_odd * odds[f]
+            out_cross_ref[f, rows] = begun_cross_ref[f, rows] + (from_even + from_odd)
+            out_paired_ref[f, rows] = begun_paired_ref[f, rows] + (from_even - from_odd)
+
+
+def outer(traces, got, begun_traces, rows, step):
+    trace = array(FIELDS, 64, NE)
+    return call(
+        lambda *refs: outer_kernel(step, *refs),
+        [*traces, *got, *begun_traces, rows],
+        [array(2, FIELDS, 64, NE), trace, trace],
+    )
+
+
+def finish_kernel(
+    base_ref, wave_ref, part_ref, flux_ref, cross_ref, paired_ref, got_cross_ref,
+    got_paired_ref, rows_ref, strain_ref, first_ref, out_hbm, gradient_ref,
+    out_ref, fluxz_ref, sums_ref, out_sem,
+):
     rinv, lam, mu, speed = materials(rows_ref)
     order = jnp.broadcast_to(rows_ref[4:5, :], (NP, NE))
     orient = jnp.broadcast_to(rows_ref[5:6, :], (NP, NE))
-    odd = odd_device()
-    side = jnp.where(odd, 1.0, -1.0)
+    side = jnp.where(odd_device(), 1.0, -1.0)
     k = lax.broadcasted_iota(jnp.int32, (NP, NE), 0)
-    k_even = k % 2 == 0
     factor_z = (2 * k + 1).astype(f32)
-    step = 0.5 * DT if half else DT
+    sums_ref[...] = jnp.zeros_like(sums_ref)
+
+    def leave(i):
+        rows = pl.ds(pl.multiple_of(i * NP, NP), NP)
+        return pltpu.make_async_copy(out_ref.at[:, rows], out_hbm.at[:, rows], out_sem.at[i])
 
     @pl.loop(0, NP)
     def _(i):
@@ -433,64 +556,43 @@
             fluxz_ref[0, f] = even[f]
             fluxz_ref[1, f] = odds[f]
 
-        masks = []
+        masks = order_masks(order, k, i, 0.5 * DT)
+        flip_x = ((orient == 1.0) | (orient == 3.0)) & (parity == 1)
+        sign_x = jnp.where(flip_x, -1.0, 1.0)
+        sign_y = jnp.where(orient >= 2.0, -1.0, 1.0)
+        signs = [sign_x, sign_x * sign_y]
+        stresses = [[] for _ in range(NP)]
+        for f in range(FIELDS):
+            for j in range(NP):
+                lifted = lifted_row(fluxz_ref, f, j, k)
+                slope = part_ref[f, at + j] + factor_x * flux_ref[parity, f, j] + factor_z * lifted
+                start = 0.5 * (base_ref[f, at + j] + wave_ref[f, at + j])
+                new = start + masks[j] * slope
+                out_ref[f, at + j] = new * signs[j % 2]
+                if f >= 3:
+                    stresses[j].append(new)
+        leave(i).start()
         for j in range(NP):
-            highest = jnp.maximum(k, jnp.maximum(i, j)).astype(f32)
-            masks.append(jnp.where(highest <= order, step, 0.0))
-        if last:
-            flip_x = ((orient == 1.0) | (orient == 3.0)) & (parity == 1)
-            sign_x = jnp.where(flip_x, -1.0, 1.0)
-            sign_y = jnp.where(orient >= 2.0, -1.0, 1.0)
-            signs = [sign_x, sign_x * sign_y]
-            stresses = [[] for _ in range(NP)]
-
-        for f in range(FIELDS):
-            fresh = []
-            for j in range(NP):
-                lifted = jnp.where(
-                    k_even,
-                    jnp.broadcast_to(fluxz_ref[0, f, j : j + 1, :], (NP, NE)),
-                    jnp.broadcast_to(fluxz_ref[1, f, j : j + 1, :], (NP, NE)),
-                )
-                slope = part_ref[f, at + j] + factor_x * flux_ref[parity, f, j] + factor_z * lifted
-                start = wave_ref[f, at + j]
-                if half:
-                    start = 0.5 * (base_ref[f, at + j] + start)
-                new = start + masks[j] * slope
-                if last:
-                    out_ref[f, at + j] = new * signs[j % 2]
-                    if f >= 3:
-                        stresses[j].append(new)
-                else:
-                    out_ref[f, at + j] = new
-                fresh.append(new)
-            if not last:
-                upper, lower = face_traces(fresh, k)
-                out_cross_ref[f, rows] = jnp.where(odd, upper, lower)
-                out_paired_ref[f, rows] = jnp.where(odd, lower, upper)
-        if last:
-            for j in range(NP):
-                add_gradient(sums_ref, stresses[j], [strain_ref[f, at + j] for f in range(6)])
-
-    if last:
-        gradient_ref[...] = first_ref[...] + gradient_rows(sums_ref)
-
-
-def update(base, wave, part, flux, traces, got, rows, last=None):
-    half = base is not None
-    whole, trace = array(FIELDS, 64, NP, NE), array(FIELDS, 64, NE)
-    operands = ([base] if half else []) + [wave, part, flux, *traces, *got, rows]
-    scratch = [pltpu.VMEM((2, FIELDS, NP, NE), f32)]
-    out = [whole, trace, trace]
-    if last is not None:
-        operands += list(last)
-        scratch.append(pltpu.VMEM((2, NP, NE), f32))
-        out = [whole, array(2, NE)]
-
-    def kernel(*refs):
-        update_kernel(last is not None, half, *refs)
-
-    return call(kernel, operands, out, scratch)
+            add_gradient(sums_ref, stresses[j], [strain_ref[f, at + j] for f in range(6)])
+
+    gradient_ref[...] = first_ref[...] + gradient_rows(sums_ref)
+    for i in range(NP):
+        leave(i).wait()
+
+
+def finish(base, wave, part, flux, traces, got, rows, strain, first):
+    return call(
+        finish_kernel,
+        [base, wave, part, flux, *traces, *got, rows, strain, first],
+        [array(FIELDS, 64, NP, NE), array(2, NE)],
+        [
+            pltpu.VMEM((FIELDS, 64, NP, NE), f32),
+            pltpu.VMEM((2, FIELDS, NP, NE), f32),
+            pltpu.VMEM((2, NP, NE), f32),
+            pltpu.SemaphoreType.DMA((NP,)),
+        ],
+        hbm_out=(0,),
+    )
 
 
 def add_gradient(sums_ref, stress, strain):
@@ -617,24 +719,26 @@
     send, meta = pack(rows, adjoint, snaps)
     got = lax.all_to_all(send, "dom", split_axis=0, concat_axis=0, tiled=True)
     wave, *traces, rows, pick, frame = place(meta, got, adjoint)
-    stage = 0
-    for step in range(STEPS):
-        start = wave
-        for half in (False, True):
-            outer = swap_traces(*traces)
-            part, flux = inner(wave, rows)
-            base = start if half else None
-            if stage == 2:
-                strain = velocities(meta, pick, frame, None, snaps, got)
-                part, strain = lax.optimization_barrier((part, strain))
-            if stage == 3:
-                first = velocities(meta, pick, frame, start, snaps, got)
-                signed, gradients = update(
-                    base, wave, part, flux, traces, outer, rows, (strain, first)
-                )
-            else:
-                wave, *traces = update(base, wave, part, flux, traces, outer, rows)
-            stage += 1
+    part, flux = inner(wave, rows)
+    start, base = wave, None
+    for stage in range(2 * STEPS - 1):
+        got_traces = swap_traces(*traces)
+        step = DT if base is None else 0.5 * DT
+        begun, *begun_traces = begin(base, wave, part, flux, rows)
+        if stage == 2:
+            strain = velocities(meta, pick, frame, None, snaps, got)
+            begun_traces[0], strain = lax.optimization_barrier((begun_traces[0], strain))
+        fluxz, *traces = outer(traces, got_traces, begun_traces, rows, step)
+        wave, part, flux = complete(begun, fluxz, rows, step)
+        if base is None:
+            base = start
+        else:
+            start, base = wave, None
+    first = velocities(meta, pick, frame, start, snaps, got)
+    got_traces = swap_traces(*traces)
+    signed, gradients = finish(
+        base, wave, part, flux, traces, got_traces, rows, strain, first
+    )
     return signed.reshape(FIELDS, NM, NE), gradients
 
 

time: 173 us -> 170 us (0.983)
  waiting for transfers between devices: 26.5 us -> 21.9 us
    ppermute x4, waiting for transfers between devices: 26.5 us -> 21.9 us  [swap_traces(): lax.ppermute(cross, 'dom', both(ups))]
    pallas_call x12 -> x15, Pallas kernels: 34.4 us -> 34.3 us  [call(): pl.pallas_call(kernel, in_specs=[pl.BlockSpec(memory_space=space(n, x)) f...]
  transfers between devices with their start and end apart: 8 -> 8, of which waited for: 4 -> 4; matrix products, arithmetic and copies ran while one was open for 0% -> 0% of each run, Pallas kernels for 8% -> 10%
where the time goes in v4:
time: 170 us
  blocking collectives  102 us (60%)
  Pallas kernels  34.3 us (20%)
  waiting for transfers between devices  21.9 us (13%)
  starting transfers between devices  10.3 us (6%)
    all_to_all x1, blocking collectives, body(): got = lax.all_to_all(send, 'dom', split_axis=0, concat_axis=0, tiled=True)  102 us
    pallas_call x15, Pallas kernels, call(): pl.pallas_call(kernel, in_specs=[pl.BlockSpec(memory_space=space(n, x)) f...  34.3 us
    ppermute x4, waiting for transfers between devices, swap_traces(): lax.ppermute(cross, 'dom', both(ups))  21.9 us
    ppermute x4, starting transfers between devices, swap_traces(): lax.ppermute(cross, 'dom', both(ups))  9.78 us
  transfers between devices with their start and end apart: 8, of which 4 were waited for; matrix products, arithmetic and copies ran while one was open for 0% of the time, Pallas kernels for 10%

profile of v4, /device:TPU:32, one launch (start us, length us, event | category | flops | bytes accessed | tf_op | source)
XLA Modules:
  0.0 169.5 jit_solution(811982636338755142)
XLA Ops:
  0.6 9.2 %shard_map.104 = (f32[128,120,128]{2,1,0:T(8,128)}, f32[8,128]{1,0:T(8,128)}) custom-call(s32[1,128]{1,0:T(1,128)} %bitcast.12, f32[1,128]{1,0:T(1,128)} %bitcast.13, f32[1,128]{1,0:T(1,128)} %bitcast.14, f32[1,128]{1,0:T(1,128)} %bitcast.15, s32[1,128]{1,0:T(1,128)} %bitcast.16, s32[1,128]{1,0:T(1,128)} %bitcast.17, s32[1,128]{1,0:T(1,128)} %bitcast.18, ...), custom_call_target="tpu_custom_call" | custom-call | tf_op jit(solution)/shard_map/pallas_call | solution.py:37
  9.8 0.0 copy-start.1
  9.9 0.0 copy-start.2
  9.9 102.0 %all_to_all.5.got_ref.refs_4_.refs_5_ = f32[128,120,128]{2,1,0:T(8,128)S(1)} all-to-all(f32[128,120,128]{2,1,0:T(8,128)} %get-tuple-element.44), channel_id=1, replica_groups=mesh['dom'=128] {'dom'}, dimensions={0} | all-to-all | bytes 15728640 | tf_op jit(solution)/shard_map/all_to_all | solution.py:720
  111.9 0.0 copy-done.1
  111.9 0.0 copy-done.2
  111.9 4.6 %shard_map.105 = (f32[9,64,8,128]{3,2,1,0:T(8,128)S(1)}, f32[9,64,128]{2,1,0:T(8,128)S(1)}, f32[9,64,128]{2,1,0:T(8,128)S(1)}, f32[8,128]{1,0:T(8,128)S(1)}, bf1...) custom-call(f32[8,128]{1,0:T(8,128)S(1)} %copy-done.2, f32[128,120,128]{2,1,0:T(8,128)S(1)} %all_to_all.5.got_ref.refs_4_.refs_5_, ...), custom_call_target="tpu_custom_call" | custom-call | tf_op jit(solution)/shard_map/pallas_call | solution.py:37
  116.4 2.2 %collective-permute-start = (f32[9,64,128]{2,1,0:T(8,128)S(1)}, f32[9,64,128]{2,1,0:T(8,128)S(1)}, u32[]{:S(2)}, u32[]{:S(2)}) collective-permute-start(f32[9,64,128]{2,1,0:T(8,128)S(1)} %get-tuple-element.50.refs_0_), channel_id=1, source_target_pairs={{1,2},{3,4},{5,6},{7,8},{9,10},{11,12},{13,14},{15,16},{17,18},{19... | collective-permute-start | bytes 884744 | tf_op jit(solution)/shard_map/ppermute | solution.py:708
  118.7 0.1 collective-permute-start.1
  118.8 2.5 %shard_map.106 = (f32[9,64,8,128]{3,2,1,0:T(8,128)S(1)}, f32[2,9,8,8,128]{4,3,2,1,0:T(8,128)S(1)}) custom-call(f32[9,64,8,128]{3,2,1,0:T(8,128)S(1)} %get-tuple-element.45.refs_0_, f32[8,128]{1,0:T(8,128)S(1)} %get-tuple-element.46.refs_1_.refs_3_.refs_6_.refs_2_.refs_4_.rows_ref), custom_call_target="tpu_custom_call" | custom-call | tf_op jit(solution)/shard_map/pallas_call | solution.py:37
  121.3 0.9 shard_map.107
  122.1 6.6 %collective-permute-done.refs_2_ = f32[9,64,128]{2,1,0:T(8,128)S(1)} collective-permute-done((f32[9,64,128]{2,1,0:T(8,128)S(1)}, f32[9,64,128]{2,1,0:T(8,128)S(1)}, u32[]{:S(2)}, u32[]{:S(2)}) %collective-permute-start) | collective-permute-done | bytes 294944 | tf_op jit(solution)/shard_map/ppermute | solution.py:708
  128.7 0.0 collective-permute-done.1.refs_3_
  128.7 0.3 shard_map.108
  129.1 2.2 %collective-permute-start.2 = (f32[9,64,128]{2,1,0:T(8,128)S(1)}, f32[9,64,128]{2,1,0:T(8,128)S(1)}, u32[]{:S(2)}, u32[]{:S(2)}) collective-permute-start(f32[9,64,128]{2,1,0:T(8,128)S(1)} %get-tuple-element.59.refs_0_), channel_id=1, source_target_pairs={{1,2},{3,4},{5,6},{7,8},{9,10},{11,12},{13,14},{15,16},{17,18},{19... | collective-permute-start | bytes 884744 | tf_op jit(solution)/shard_map/ppermute | solution.py:708
  131.3 0.1 collective-permute-start.3
  131.4 2.7 %shard_map.109 = (f32[9,64,8,128]{3,2,1,0:T(8,128)S(1)}, f32[9,64,8,128]{3,2,1,0:T(8,128)S(1)}, f32[2,9,8,8,128]{4,3,2,1,0:T(8,128)S(1)}) custom-call(f32[9,64,8,128]{3,2,1,0:T(8,128)S(1)} %get-tuple-element.49.refs_0_, f32[2,9,64,128]{3,2,1,0:T(8,128)S(1)} %get-tuple-element.54.refs_1_, ...), custom_call_target="tpu_custom_call" | custom-call | tf_op jit(solution)/shard_map/pallas_call | solution.py:37
  134.1 1.0 shard_map.110
  135.1 0.0 copy-start
  135.2 6.2 %collective-permute-done.2.refs_2_ = f32[9,64,128]{2,1,0:T(8,128)S(1)} collective-permute-done((f32[9,64,128]{2,1,0:T(8,128)S(1)}, f32[9,64,128]{2,1,0:T(8,128)S(1)}, u32[]{:S(2)}, u32[]{:S(2)}) %collective-permute-start.2) | collective-permute-done | bytes 294944 | tf_op jit(solution)/shard_map/ppermute | solution.py:708
  141.3 0.0 collective-permute-done.3.refs_3_
  141.3 0.3 shard_map.111
  141.7 2.2 %collective-permute-start.4 = (f32[9,64,128]{2,1,0:T(8,128)S(1)}, f32[9,64,128]{2,1,0:T(8,128)S(1)}, u32[]{:S(2)}, u32[]{:S(2)}) collective-permute-start(f32[9,64,128]{2,1,0:T(8,128)S(1)} %get-tuple-element.68.refs_0_), channel_id=1, source_target_pairs={{1,2},{3,4},{5,6},{7,8},{9,10},{11,12},{13,14},{15,16},{17,18},{19... | collective-permute-start | bytes 884744 | tf_op jit(solution)/shard_map/ppermute | solution.py:708
  143.9 0.3 collective-permute-start.5
  144.2 0.0 copy-done
  144.2 1.7 shard_map.114.strain_ref
  145.9 2.7 %shard_map.112 = (f32[9,64,8,128]{3,2,1,0:T(8,128)S(1)}, f32[9,64,8,128]{3,2,1,0:T(8,128)S(1)}, f32[2,9,8,8,128]{4,3,2,1,0:T(8,128)S(1)}) custom-call(f32[9,64,8,128]{3,2,1,0:T(8,128)S(1)} %get-tuple-element.58.refs_0_, f32[2,9,64,128]{3,2,1,0:T(8,128)S(1)} %get-tuple-element.63.refs_1_, ...), custom_call_target="tpu_custom_call" | custom-call | tf_op jit(solution)/shard_map/pallas_call | solution.py:37
  148.6 0.8 shard_map.113
  149.5 4.5 %collective-permute-done.4.refs_2_ = f32[9,64,128]{2,1,0:T(8,128)S(1)} collective-permute-done((f32[9,64,128]{2,1,0:T(8,128)S(1)}, f32[9,64,128]{2,1,0:T(8,128)S(1)}, u32[]{:S(2)}, u32[]{:S(2)}) %collective-permute-start.4) | collective-permute-done | bytes 294944 | tf_op jit(solution)/shard_map/ppermute | solution.py:708
  153.9 0.0 collective-permute-done.5.refs_3_
  153.9 0.3 shard_map.115
  154.3 3.1 %collective-permute-start.6 = (f32[9,64,128]{2,1,0:T(8,128)S(1)}, f32[9,64,128]{2,1,0:T(8,128)S(1)}, u32[]{:S(2)}, u32[]{:S(2)}) collective-permute-start(f32[9,64,128]{2,1,0:T(8,128)S(1)} %get-tuple-element.79.cross_ref), channel_id=1, source_target_pairs={{1,2},{3,4},{5,6},{7,8},{9,10},{11,12},{13,14},{15,16},{17,18},{19... | collective-permute-start | bytes 884744 | tf_op jit(solution)/shard_map/ppermute | solution.py:708
  157.4 0.1 collective-permute-start.7
  157.5 1.7 shard_map.117.first_ref
  159.1 2.7 %shard_map.116 = (f32[9,64,8,128]{3,2,1,0:T(8,128)S(1)}, f32[9,64,8,128]{3,2,1,0:T(8,128)S(1)}, f32[2,9,8,8,128]{4,3,2,1,0:T(8,128)S(1)}) custom-call(f32[9,64,8,128]{3,2,1,0:T(8,128)S(1)} %get-tuple-element.67.refs_0_, f32[2,9,64,128]{3,2,1,0:T(8,128)S(1)} %get-tuple-element.75.refs_1_, ...), custom_call_target="tpu_custom_call" | custom-call | tf_op jit(solution)/shard_map/pallas_call | solution.py:37
  161.9 4.7 %collective-permute-done.6.got_cross_ref = f32[9,64,128]{2,1,0:T(8,128)S(1)} collective-permute-done((f32[9,64,128]{2,1,0:T(8,128)S(1)}, f32[9,64,128]{2,1,0:T(8,128)S(1)}, u32[]{:S(2)}, u32[]{:S(2)}) %collective-permute-start.6) | collective-permute-done | bytes 294944 | tf_op jit(solution)/shard_map/ppermute | solution.py:708
  166.5 0.0 collective-permute-done.7.got_paired_ref
  166.5 2.8 %shard_map.118 = (f32[9,64,8,128]{3,2,1,0:T(8,128)}, f32[2,128]{1,0:T(2,128)}) custom-call(f32[9,64,8,128]{3,2,1,0:T(8,128)S(1)} %get-tuple-element.64.refs_0_.refs_3_.base_ref, f32[9,64,8,128]{3,2,1,0:T(8,128)S(1)} %get-tuple-element.76.wave_ref, f32[9,64,8,128]{3,2,1,0:T(8,128)S(1)} %get-tuple-element.77.part_ref, ...), custom_call_target="tpu_custom_call" | custom-call | tf_op jit(solution)/shard_map/pallas_call | solution.py:37
Async XLA Ops:
  9.8 102.0 %copy-start.1 = (f32[9,512,128]{2,1,0:T(8,128)S(1)}, f32[9,512,128]{2,1,0:T(8,128)}, u32[]{:S(2)}) copy-start(f32[9,512,128]{2,1,0:T(8,128)} %adj_ref.1) | copy-start | bytes 7077892
  9.9 102.0 %copy-start.2 = (f32[8,128]{1,0:T(8,128)S(1)}, f32[8,128]{1,0:T(8,128)}, u32[]{:S(2)}) copy-start(f32[8,128]{1,0:T(8,128)} %get-tuple-element.43.meta_ref.refs_0_) | copy-start | bytes 12292
  116.4 12.3 %collective-permute-start = (f32[9,64,128]{2,1,0:T(8,128)S(1)}, f32[9,64,128]{2,1,0:T(8,128)S(1)}, u32[]{:S(2)}, u32[]{:S(2)}) collective-permute-start(f32[9,64,128]{2,1,0:T(8,128)S(1)} %get-tuple-element.50.refs_0_), channel_id=1, source_target_pairs={{1,2},{3,4},{5,6},{7,8},{9,10},{11,12},{13,14},{15,16},{17,18},{19... | collective-permute-start | bytes 884744 | tf_op jit(solution)/shard_map/ppermute | solution.py:708
  118.7 10.0 %collective-permute-start.1 = (f32[9,64,128]{2,1,0:T(8,128)S(1)}, f32[9,64,128]{2,1,0:T(8,128)S(1)}, u32[]{:S(2)}, u32[]{:S(2)}) collective-permute-start(f32[9,64,128]{2,1,0:T(8,128)S(1)} %get-tuple-element.51.refs_1_), channel_id=1, source_target_pairs={{0,1},{2,3},{4,5},{6,7},{8,9},{10,11},{12,13},{14,15},{16,17},{18,... | collective-permute-start | bytes 884744 | tf_op jit(solution)/shard_map/ppermute | solution.py:708
  129.1 12.3 %collective-permute-start.2 = (f32[9,64,128]{2,1,0:T(8,128)S(1)}, f32[9,64,128]{2,1,0:T(8,128)S(1)}, u32[]{:S(2)}, u32[]{:S(2)}) collective-permute-start(f32[9,64,128]{2,1,0:T(8,128)S(1)} %get-tuple-element.59.refs_0_), channel_id=1, source_target_pairs={{1,2},{3,4},{5,6},{7,8},{9,10},{11,12},{13,14},{15,16},{17,18},{19... | collective-permute-start | bytes 884744 | tf_op jit(solution)/shard_map/ppermute | solution.py:708
  131.3 10.0 %collective-permute-start.3 = (f32[9,64,128]{2,1,0:T(8,128)S(1)}, f32[9,64,128]{2,1,0:T(8,128)S(1)}, u32[]{:S(2)}, u32[]{:S(2)}) collective-permute-start(f32[9,64,128]{2,1,0:T(8,128)S(1)} %get-tuple-element.60.refs_1_), channel_id=1, source_target_pairs={{0,1},{2,3},{4,5},{6,7},{8,9},{10,11},{12,13},{14,15},{16,17},{18,... | collective-permute-start | bytes 884744 | tf_op jit(solution)/shard_map/ppermute | solution.py:708
  135.1 9.0 %copy-start = (f32[2,3,512,128]{3,2,1,0:T(8,128)S(1)}, f32[2,3,512,128]{3,2,1,0:T(8,128)}, u32[]{:S(2)}) copy-start(f32[2,3,512,128]{3,2,1,0:T(8,128)} %param.10) | copy-start | bytes 4718596
  141.7 12.3 %collective-permute-start.4 = (f32[9,64,128]{2,1,0:T(8,128)S(1)}, f32[9,64,128]{2,1,0:T(8,128)S(1)}, u32[]{:S(2)}, u32[]{:S(2)}) collective-permute-start(f32[9,64,128]{2,1,0:T(8,128)S(1)} %get-tuple-element.68.refs_0_), channel_id=1, source_target_pairs={{1,2},{3,4},{5,6},{7,8},{9,10},{11,12},{13,14},{15,16},{17,18},{19... | collective-permute-start | bytes 884744 | tf_op jit(solution)/shard_map/ppermute | solution.py:708
  143.9 10.0 %collective-permute-start.5 = (f32[9,64,128]{2,1,0:T(8,128)S(1)}, f32[9,64,128]{2,1,0:T(8,128)S(1)}, u32[]{:S(2)}, u32[]{:S(2)}) collective-permute-start(f32[9,64,128]{2,1,0:T(8,128)S(1)} %get-tuple-element.69.refs_1_), channel_id=1, source_target_pairs={{0,1},{2,3},{4,5},{6,7},{8,9},{10,11},{12,13},{14,15},{16,17},{18,... | collective-permute-start | bytes 884744 | tf_op jit(solution)/shard_map/ppermute | solution.py:708
  154.3 12.3 %collective-permute-start.6 = (f32[9,64,128]{2,1,0:T(8,128)S(1)}, f32[9,64,128]{2,1,0:T(8,128)S(1)}, u32[]{:S(2)}, u32[]{:S(2)}) collective-permute-start(f32[9,64,128]{2,1,0:T(8,128)S(1)} %get-tuple-element.79.cross_ref), channel_id=1, source_target_pairs={{1,2},{3,4},{5,6},{7,8},{9,10},{11,12},{13,14},{15,16},{17,18},{19... | collective-permute-start | bytes 884744 | tf_op jit(solution)/shard_map/ppermute | solution.py:708
  157.4 9.2 %collective-permute-start.7 = (f32[9,64,128]{2,1,0:T(8,128)S(1)}, f32[9,64,128]{2,1,0:T(8,128)S(1)}, u32[]{:S(2)}, u32[]{:S(2)}) collective-permute-start(f32[9,64,128]{2,1,0:T(8,128)S(1)} %get-tuple-element.80.paired_ref), channel_id=1, source_target_pairs={{0,1},{2,3},{4,5},{6,7},{8,9},{10,11},{12,13},{14,15},{16,17},{18,... | collective-permute-start | bytes 884744 | tf_op jit(solution)/shard_map/ppermute | solution.py:708

commit v5 on v4

--- a/solution.py
+++ b/solution.py
@@ -523,9 +523,8 @@
 
 
 def finish_kernel(
-    base_ref, wave_ref, part_ref, flux_ref, cross_ref, paired_ref, got_cross_ref,
-    got_paired_ref, rows_ref, strain_ref, first_ref, out_hbm, gradient_ref,
-    out_ref, fluxz_ref, sums_ref, out_sem,
+    begun_ref, cross_ref, paired_ref, got_cross_ref, got_paired_ref, rows_ref, strain_ref,
+    first_ref, out_hbm, gradient_ref, out_ref, fluxz_ref, sums_ref, out_sem,
 ):
     rinv, lam, mu, speed = materials(rows_ref)
     order = jnp.broadcast_to(rows_ref[4:5, :], (NP, NE))
@@ -541,8 +540,6 @@
 
     @pl.loop(0, NP)
     def _(i):
-        parity = lax.rem(i, 2)
-        factor_x = (2 * i + 1).astype(f32)
         at = pl.multiple_of(i * NP, NP)
         rows = pl.ds(at, NP)
         total, difference = [], []
@@ -556,8 +553,8 @@
             fluxz_ref[0, f] = even[f]
             fluxz_ref[1, f] = odds[f]
 
-        masks = order_masks(order, k, i, 0.5 * DT)
-        flip_x = ((orient == 1.0) | (orient == 3.0)) & (parity == 1)
+        scales = [factor_z * mask for mask in order_masks(order, k, i, 0.5 * DT)]
+        flip_x = ((orient == 1.0) | (orient == 3.0)) & (lax.rem(i, 2) == 1)
         sign_x = jnp.where(flip_x, -1.0, 1.0)
         sign_y = jnp.where(orient >= 2.0, -1.0, 1.0)
         signs = [sign_x, sign_x * sign_y]
@@ -565,9 +562,7 @@
         for f in range(FIELDS):
             for j in range(NP):
                 lifted = lifted_row(fluxz_ref, f, j, k)
-                slope = part_ref[f, at + j] + factor_x * flux_ref[parity, f, j] + factor_z * lifted
-                start = 0.5 * (base_ref[f, at + j] + wave_ref[f, at + j])
-                new = start + masks[j] * slope
+                new = begun_ref[f, at + j] + scales[j] * lifted
                 out_ref[f, at + j] = new * signs[j % 2]
                 if f >= 3:
                     stresses[j].append(new)
@@ -580,10 +575,10 @@
         leave(i).wait()
 
 
-def finish(base, wave, part, flux, traces, got, rows, strain, first):
+def finish(begun, traces, got, rows, strain, first):
     return call(
         finish_kernel,
-        [base, wave, part, flux, *traces, *got, rows, strain, first],
+        [begun, *traces, *got, rows, strain, first],
         [array(FIELDS, 64, NP, NE), array(2, NE)],
         [
             pltpu.VMEM((FIELDS, 64, NP, NE), f32),
@@ -736,9 +731,8 @@
             start, base = wave, None
     first = velocities(meta, pick, frame, start, snaps, got)
     got_traces = swap_traces(*traces)
-    signed, gradients = finish(
-        base, wave, part, flux, traces, got_traces, rows, strain, first
-    )
+    begun, *_ = begin(base, wave, part, flux, rows)
+    signed, gradients = finish(begun, traces, got_traces, rows, strain, first)
     return signed.reshape(FIELDS, NM, NE), gradients
 
 

time: 170 us -> 169 us (level)
  waiting for transfers between devices: 21.9 us -> 19.9 us
    ppermute x4, waiting for transfers between devices: 21.9 us -> 19.9 us  [swap_traces(): lax.ppermute(cross, 'dom', both(ups))]
    pallas_call x15 -> x16, Pallas kernels: 34.3 us -> 35.9 us  [call(): pl.pallas_call(kernel, in_specs=[pl.BlockSpec(memory_space=space(n, x)) f...]
  transfers between devices with their start and end apart: 8 -> 8, of which waited for: 4 -> 4; matrix products, arithmetic and copies ran while one was open for 0% -> 0% of each run, Pallas kernels for 10% -> 11%
where the time goes in v5:
time: 169 us
  blocking collectives  102 us (60%)
  Pallas kernels  35.9 us (21%)
  waiting for transfers between devices  19.9 us (12%)
  starting transfers between devices  10.3 us (6%)
    all_to_all x1, blocking collectives, body(): got = lax.all_to_all(send, 'dom', split_axis=0, concat_axis=0, tiled=True)  102 us
    pallas_call x16, Pallas kernels, call(): pl.pallas_call(kernel, in_specs=[pl.BlockSpec(memory_space=space(n, x)) f...  35.9 us
    ppermute x4, waiting for transfers between devices, swap_traces(): lax.ppermute(cross, 'dom', both(ups))  19.9 us
    ppermute x4, starting transfers between devices, swap_traces(): lax.ppermute(cross, 'dom', both(ups))  9.77 us
  transfers between devices with their start and end apart: 8, of which 4 were waited for; matrix products, arithmetic and copies ran while one was open for 0% of the time, Pallas kernels for 11%

profile of v5, /device:TPU:32, one launch (start us, length us, event | category | flops | bytes accessed | tf_op | source)
XLA Modules:
  0.0 169.1 jit_solution(8396825141765425040)
XLA Ops:
  0.6 9.2 %shard_map.104 = (f32[128,120,128]{2,1,0:T(8,128)}, f32[8,128]{1,0:T(8,128)}) custom-call(s32[1,128]{1,0:T(1,128)} %bitcast.12, f32[1,128]{1,0:T(1,128)} %bitcast.13, f32[1,128]{1,0:T(1,128)} %bitcast.14, f32[1,128]{1,0:T(1,128)} %bitcast.15, s32[1,128]{1,0:T(1,128)} %bitcast.16, s32[1,128]{1,0:T(1,128)} %bitcast.17, s32[1,128]{1,0:T(1,128)} %bitcast.18, ...), custom_call_target="tpu_custom_call" | custom-call | tf_op jit(solution)/shard_map/pallas_call | solution.py:37
  9.9 0.0 copy-start.1
  9.9 0.0 copy-start.2
  9.9 102.0 %all_to_all.5.got_ref.refs_4_.refs_5_ = f32[128,120,128]{2,1,0:T(8,128)S(1)} all-to-all(f32[128,120,128]{2,1,0:T(8,128)} %get-tuple-element.45), channel_id=1, replica_groups=mesh['dom'=128] {'dom'}, dimensions={0} | all-to-all | bytes 15728640 | tf_op jit(solution)/shard_map/all_to_all | solution.py:715
  111.9 0.0 copy-done.1
  111.9 0.0 copy-done.2
  111.9 4.6 %shard_map.105 = (f32[9,64,8,128]{3,2,1,0:T(8,128)S(1)}, f32[9,64,128]{2,1,0:T(8,128)S(1)}, f32[9,64,128]{2,1,0:T(8,128)S(1)}, f32[8,128]{1,0:T(8,128)S(1)}, bf1...) custom-call(f32[8,128]{1,0:T(8,128)S(1)} %copy-done.2, f32[128,120,128]{2,1,0:T(8,128)S(1)} %all_to_all.5.got_ref.refs_4_.refs_5_, ...), custom_call_target="tpu_custom_call" | custom-call | tf_op jit(solution)/shard_map/pallas_call | solution.py:37
  116.5 2.2 %collective-permute-start = (f32[9,64,128]{2,1,0:T(8,128)S(1)}, f32[9,64,128]{2,1,0:T(8,128)S(1)}, u32[]{:S(2)}, u32[]{:S(2)}) collective-permute-start(f32[9,64,128]{2,1,0:T(8,128)S(1)} %get-tuple-element.51.refs_0_), channel_id=1, source_target_pairs={{1,2},{3,4},{5,6},{7,8},{9,10},{11,12},{13,14},{15,16},{17,18},{19... | collective-permute-start | bytes 884744 | tf_op jit(solution)/shard_map/ppermute | solution.py:703
  118.7 0.1 collective-permute-start.1
  118.8 2.5 %shard_map.106 = (f32[9,64,8,128]{3,2,1,0:T(8,128)S(1)}, f32[2,9,8,8,128]{4,3,2,1,0:T(8,128)S(1)}) custom-call(f32[9,64,8,128]{3,2,1,0:T(8,128)S(1)} %get-tuple-element.46.refs_0_, f32[8,128]{1,0:T(8,128)S(1)} %get-tuple-element.47.refs_1_.refs_3_.refs_6_.refs_2_.refs_4_.rows_ref), custom_call_target="tpu_custom_call" | custom-call | tf_op jit(solution)/shard_map/pallas_call | solution.py:37
  121.3 0.9 shard_map.107
  122.2 6.6 %collective-permute-done.refs_2_ = f32[9,64,128]{2,1,0:T(8,128)S(1)} collective-permute-done((f32[9,64,128]{2,1,0:T(8,128)S(1)}, f32[9,64,128]{2,1,0:T(8,128)S(1)}, u32[]{:S(2)}, u32[]{:S(2)}) %collective-permute-start) | collective-permute-done | bytes 294944 | tf_op jit(solution)/shard_map/ppermute | solution.py:703
  128.7 0.0 collective-permute-done.1.refs_3_
  128.8 0.3 shard_map.108
  129.1 2.2 %collective-permute-start.2 = (f32[9,64,128]{2,1,0:T(8,128)S(1)}, f32[9,64,128]{2,1,0:T(8,128)S(1)}, u32[]{:S(2)}, u32[]{:S(2)}) collective-permute-start(f32[9,64,128]{2,1,0:T(8,128)S(1)} %get-tuple-element.60.refs_0_), channel_id=1, source_target_pairs={{1,2},{3,4},{5,6},{7,8},{9,10},{11,12},{13,14},{15,16},{17,18},{19... | collective-permute-start | bytes 884744 | tf_op jit(solution)/shard_map/ppermute | solution.py:703
  131.3 0.1 collective-permute-start.3
  131.4 2.7 %shard_map.109 = (f32[9,64,8,128]{3,2,1,0:T(8,128)S(1)}, f32[9,64,8,128]{3,2,1,0:T(8,128)S(1)}, f32[2,9,8,8,128]{4,3,2,1,0:T(8,128)S(1)}) custom-call(f32[9,64,8,128]{3,2,1,0:T(8,128)S(1)} %get-tuple-element.50.refs_0_, f32[2,9,64,128]{3,2,1,0:T(8,128)S(1)} %get-tuple-element.55.refs_1_, ...), custom_call_target="tpu_custom_call" | custom-call | tf_op jit(solution)/shard_map/pallas_call | solution.py:37
  134.2 1.1 shard_map.110
  135.2 0.0 copy-start
  135.2 6.1 %collective-permute-done.2.refs_2_ = f32[9,64,128]{2,1,0:T(8,128)S(1)} collective-permute-done((f32[9,64,128]{2,1,0:T(8,128)S(1)}, f32[9,64,128]{2,1,0:T(8,128)S(1)}, u32[]{:S(2)}, u32[]{:S(2)}) %collective-permute-start.2) | collective-permute-done | bytes 294944 | tf_op jit(solution)/shard_map/ppermute | solution.py:703
  141.4 0.0 collective-permute-done.3.refs_3_
  141.4 0.4 shard_map.111
  141.7 2.2 %collective-permute-start.4 = (f32[9,64,128]{2,1,0:T(8,128)S(1)}, f32[9,64,128]{2,1,0:T(8,128)S(1)}, u32[]{:S(2)}, u32[]{:S(2)}) collective-permute-start(f32[9,64,128]{2,1,0:T(8,128)S(1)} %get-tuple-element.69.refs_0_), channel_id=1, source_target_pairs={{1,2},{3,4},{5,6},{7,8},{9,10},{11,12},{13,14},{15,16},{17,18},{19... | collective-permute-start | bytes 884744 | tf_op jit(solution)/shard_map/ppermute | solution.py:703
  144.0 0.3 collective-permute-start.5
  144.3 0.0 copy-done
  144.3 1.7 shard_map.114.strain_ref
  145.9 2.7 %shard_map.112 = (f32[9,64,8,128]{3,2,1,0:T(8,128)S(1)}, f32[9,64,8,128]{3,2,1,0:T(8,128)S(1)}, f32[2,9,8,8,128]{4,3,2,1,0:T(8,128)S(1)}) custom-call(f32[9,64,8,128]{3,2,1,0:T(8,128)S(1)} %get-tuple-element.59.refs_0_, f32[2,9,64,128]{3,2,1,0:T(8,128)S(1)} %get-tuple-element.64.refs_1_, ...), custom_call_target="tpu_custom_call" | custom-call | tf_op jit(solution)/shard_map/pallas_call | solution.py:37
  148.7 0.8 shard_map.113
  149.5 4.5 %collective-permute-done.4.refs_2_ = f32[9,64,128]{2,1,0:T(8,128)S(1)} collective-permute-done((f32[9,64,128]{2,1,0:T(8,128)S(1)}, f32[9,64,128]{2,1,0:T(8,128)S(1)}, u32[]{:S(2)}, u32[]{:S(2)}) %collective-permute-start.4) | collective-permute-done | bytes 294944 | tf_op jit(solution)/shard_map/ppermute | solution.py:703
  154.0 0.0 collective-permute-done.5.refs_3_
  154.0 0.3 shard_map.115
  154.4 3.1 %collective-permute-start.6 = (f32[9,64,128]{2,1,0:T(8,128)S(1)}, f32[9,64,128]{2,1,0:T(8,128)S(1)}, u32[]{:S(2)}, u32[]{:S(2)}) collective-permute-start(f32[9,64,128]{2,1,0:T(8,128)S(1)} %get-tuple-element.81.cross_ref), channel_id=1, source_target_pairs={{1,2},{3,4},{5,6},{7,8},{9,10},{11,12},{13,14},{15,16},{17,18},{19... | collective-permute-start | bytes 884744 | tf_op jit(solution)/shard_map/ppermute | solution.py:703
  157.5 0.1 collective-permute-start.7
  157.6 1.7 shard_map.118.first_ref
  159.2 2.7 %shard_map.116 = (f32[9,64,8,128]{3,2,1,0:T(8,128)S(1)}, f32[9,64,8,128]{3,2,1,0:T(8,128)S(1)}, f32[2,9,8,8,128]{4,3,2,1,0:T(8,128)S(1)}) custom-call(f32[9,64,8,128]{3,2,1,0:T(8,128)S(1)} %get-tuple-element.68.refs_0_, f32[2,9,64,128]{3,2,1,0:T(8,128)S(1)} %get-tuple-element.76.refs_1_, ...), custom_call_target="tpu_custom_call" | custom-call | tf_op jit(solution)/shard_map/pallas_call | solution.py:37
  162.0 1.9 %shard_map.117 = (f32[9,64,8,128]{3,2,1,0:T(8,128)S(1)}, f32[9,64,128]{2,1,0:T(8,128)}, f32[9,64,128]{2,1,0:T(8,128)}) custom-call(f32[9,64,8,128]{3,2,1,0:T(8,128)S(1)} %get-tuple-element.65.refs_0_.refs_3_, f32[9,64,8,128]{3,2,1,0:T(8,128)S(1)} %get-tuple-element.77.refs_1_, f32[9,64,8,128]{3,2,1,0:T(8,128)S(1)} %get-tuple-element.78.refs_2_, ...), custom_call_target="tpu_custom_call" | custom-call | tf_op jit(solution)/shard_map/pallas_call | solution.py:37
  163.9 2.7 %collective-permute-done.6.got_cross_ref = f32[9,64,128]{2,1,0:T(8,128)S(1)} collective-permute-done((f32[9,64,128]{2,1,0:T(8,128)S(1)}, f32[9,64,128]{2,1,0:T(8,128)S(1)}, u32[]{:S(2)}, u32[]{:S(2)}) %collective-permute-start.6) | collective-permute-done | bytes 294944 | tf_op jit(solution)/shard_map/ppermute | solution.py:703
  166.6 0.0 collective-permute-done.7.got_paired_ref
  166.6 2.3 %shard_map.119 = (f32[9,64,8,128]{3,2,1,0:T(8,128)}, f32[2,128]{1,0:T(2,128)}) custom-call(f32[9,64,8,128]{3,2,1,0:T(8,128)S(1)} %get-tuple-element.80.begun_ref, f32[9,64,128]{2,1,0:T(8,128)S(1)} %get-tuple-element.81.cross_ref, f32[9,64,128]{2,1,0:T(8,128)S(1)} %get-tuple-element.82.paired_ref, f32[9,64,128]{2,1,0:T(8,128)S(1)} %collective-permute-done.6.got_cross_ref, ...), custom_call_target="tpu_custom_call" | custom-call | tf_op jit(solution)/shard_map/pallas_call | solution.py:37
Async XLA Ops:
  9.9 102.0 %copy-start.1 = (f32[9,512,128]{2,1,0:T(8,128)S(1)}, f32[9,512,128]{2,1,0:T(8,128)}, u32[]{:S(2)}) copy-start(f32[9,512,128]{2,1,0:T(8,128)} %adj_ref.1) | copy-start | bytes 7077892
  9.9 102.0 %copy-start.2 = (f32[8,128]{1,0:T(8,128)S(1)}, f32[8,128]{1,0:T(8,128)}, u32[]{:S(2)}) copy-start(f32[8,128]{1,0:T(8,128)} %get-tuple-element.44.meta_ref.refs_0_) | copy-start | bytes 12292
  116.5 12.3 %collective-permute-start = (f32[9,64,128]{2,1,0:T(8,128)S(1)}, f32[9,64,128]{2,1,0:T(8,128)S(1)}, u32[]{:S(2)}, u32[]{:S(2)}) collective-permute-start(f32[9,64,128]{2,1,0:T(8,128)S(1)} %get-tuple-element.51.refs_0_), channel_id=1, source_target_pairs={{1,2},{3,4},{5,6},{7,8},{9,10},{11,12},{13,14},{15,16},{17,18},{19... | collective-permute-start | bytes 884744 | tf_op jit(solution)/shard_map/ppermute | solution.py:703
  118.7 10.0 %collective-permute-start.1 = (f32[9,64,128]{2,1,0:T(8,128)S(1)}, f32[9,64,128]{2,1,0:T(8,128)S(1)}, u32[]{:S(2)}, u32[]{:S(2)}) collective-permute-start(f32[9,64,128]{2,1,0:T(8,128)S(1)} %get-tuple-element.52.refs_1_), channel_id=1, source_target_pairs={{0,1},{2,3},{4,5},{6,7},{8,9},{10,11},{12,13},{14,15},{16,17},{18,... | collective-permute-start | bytes 884744 | tf_op jit(solution)/shard_map/ppermute | solution.py:703
  129.1 12.3 %collective-permute-start.2 = (f32[9,64,128]{2,1,0:T(8,128)S(1)}, f32[9,64,128]{2,1,0:T(8,128)S(1)}, u32[]{:S(2)}, u32[]{:S(2)}) collective-permute-start(f32[9,64,128]{2,1,0:T(8,128)S(1)} %get-tuple-element.60.refs_0_), channel_id=1, source_target_pairs={{1,2},{3,4},{5,6},{7,8},{9,10},{11,12},{13,14},{15,16},{17,18},{19... | collective-permute-start | bytes 884744 | tf_op jit(solution)/shard_map/ppermute | solution.py:703
  131.3 10.0 %collective-permute-start.3 = (f32[9,64,128]{2,1,0:T(8,128)S(1)}, f32[9,64,128]{2,1,0:T(8,128)S(1)}, u32[]{:S(2)}, u32[]{:S(2)}) collective-permute-start(f32[9,64,128]{2,1,0:T(8,128)S(1)} %get-tuple-element.61.refs_1_), channel_id=1, source_target_pairs={{0,1},{2,3},{4,5},{6,7},{8,9},{10,11},{12,13},{14,15},{16,17},{18,... | collective-permute-start | bytes 884744 | tf_op jit(solution)/shard_map/ppermute | solution.py:703
  135.2 9.0 %copy-start = (f32[2,3,512,128]{3,2,1,0:T(8,128)S(1)}, f32[2,3,512,128]{3,2,1,0:T(8,128)}, u32[]{:S(2)}) copy-start(f32[2,3,512,128]{3,2,1,0:T(8,128)} %param.10) | copy-start | bytes 4718596
  141.7 12.3 %collective-permute-start.4 = (f32[9,64,128]{2,1,0:T(8,128)S(1)}, f32[9,64,128]{2,1,0:T(8,128)S(1)}, u32[]{:S(2)}, u32[]{:S(2)}) collective-permute-start(f32[9,64,128]{2,1,0:T(8,128)S(1)} %get-tuple-element.69.refs_0_), channel_id=1, source_target_pairs={{1,2},{3,4},{5,6},{7,8},{9,10},{11,12},{13,14},{15,16},{17,18},{19... | collective-permute-start | bytes 884744 | tf_op jit(solution)/shard_map/ppermute | solution.py:703
  144.0 10.0 %collective-permute-start.5 = (f32[9,64,128]{2,1,0:T(8,128)S(1)}, f32[9,64,128]{2,1,0:T(8,128)S(1)}, u32[]{:S(2)}, u32[]{:S(2)}) collective-permute-start(f32[9,64,128]{2,1,0:T(8,128)S(1)} %get-tuple-element.70.refs_1_), channel_id=1, source_target_pairs={{0,1},{2,3},{4,5},{6,7},{8,9},{10,11},{12,13},{14,15},{16,17},{18,... | collective-permute-start | bytes 884744 | tf_op jit(solution)/shard_map/ppermute | solution.py:703
  154.4 12.3 %collective-permute-start.6 = (f32[9,64,128]{2,1,0:T(8,128)S(1)}, f32[9,64,128]{2,1,0:T(8,128)S(1)}, u32[]{:S(2)}, u32[]{:S(2)}) collective-permute-start(f32[9,64,128]{2,1,0:T(8,128)S(1)} %get-tuple-element.81.cross_ref), channel_id=1, source_target_pairs={{1,2},{3,4},{5,6},{7,8},{9,10},{11,12},{13,14},{15,16},{17,18},{19... | collective-permute-start | bytes 884744 | tf_op jit(solution)/shard_map/ppermute | solution.py:703
  157.5 9.2 %collective-permute-start.7 = (f32[9,64,128]{2,1,0:T(8,128)S(1)}, f32[9,64,128]{2,1,0:T(8,128)S(1)}, u32[]{:S(2)}, u32[]{:S(2)}) collective-permute-start(f32[9,64,128]{2,1,0:T(8,128)S(1)} %get-tuple-element.82.paired_ref), channel_id=1, source_target_pairs={{0,1},{2,3},{4,5},{6,7},{8,9},{10,11},{12,13},{14,15},{16,17},{18,... | collective-permute-start | bytes 884744 | tf_op jit(solution)/shard_map/ppermute | solution.py:703

commit v6 on v4

--- a/solution.py
+++ b/solution.py
@@ -52,10 +52,15 @@
     return jax.ShapeDtypeStruct(shape, dtype)
 
 
-def scatter_rows(hot, x, out_ref, row):
-    parts = jnp.concatenate(split3(x), axis=1)
+def scatter_rows(hot, blocks, out_ref, row):
+    parts = jnp.concatenate(split3(jnp.concatenate(blocks, axis=0)), axis=1)
     hots = jnp.concatenate([hot, hot, hot], axis=1)
     rows = lax.dot_general(hots, parts, (((1,), (1,)), ((), ())), preferred_element_type=f32)
+    for b in range(len(blocks)):
+        store_block(rows[:, b * NM : (b + 1) * NM], out_ref, row + 8 * b)
+
+
+def store_block(rows, out_ref, row):
     groups = [
         rows[r * DEV : (r + 1) * DEV, q * 128 : (q + 1) * 128].reshape(DEV // 8, 8, 128)
         for r in range(2)
@@ -101,20 +106,24 @@
         hot_ref[r * DEV : (r + 1) * DEV, :] = jnp.where(chosen, 1.0, 0.0).astype(bf16)
 
     first_row = lax.broadcasted_iota(jnp.int32, (8, NE), 0) == 0
-    leave = []
-    for b in range(BLOCKS):
+    def load(b):
         arrive[b].wait()
         block = block_ref[b]
-        if b >= FIELDS:
-            n = b - FIELDS
-            row = jnp.broadcast_to(meta_ref[n : n + 1, :], (8, NE))
-            block = jnp.concatenate([jnp.where(first_row, row, block[0:8]), block[8:]], axis=0)
-        scatter_rows(hot_ref[...], block, out_ref, b * 8)
-        rows = pl.ds(b * 8, 8)
+        if b < FIELDS:
+            return block
+        n = b - FIELDS
+        row = jnp.broadcast_to(meta_ref[n : n + 1, :], (8, NE))
+        return jnp.concatenate([jnp.where(first_row, row, block[0:8]), block[8:]], axis=0)
+
+    leave, b = [], 0
+    for count in (3, 3, 3, 3, 2, 1):
+        scatter_rows(hot_ref[...], [load(b + n) for n in range(count)], out_ref, b * 8)
+        rows = pl.ds(b * 8, count * 8)
         leave.append(
             pltpu.make_async_copy(out_ref.at[:, rows, :], out_hbm.at[:, rows, :], out_sem.at[b])
         )
-        leave[b].start()
+        leave[-1].start()
+        b += count
     for copy in leave:
         copy.wait()
 

time: 170 us -> 168 us (0.988)
  no operation moved by 1% of the time
where the time goes in v6:
time: 168 us
  blocking collectives  102 us (61%)
  Pallas kernels  32.7 us (19%)
  waiting for transfers between devices  22.3 us (13%)
  starting transfers between devices  9.95 us (6%)
    all_to_all x1, blocking collectives, body(): got = lax.all_to_all(send, 'dom', split_axis=0, concat_axis=0, tiled=True)  102 us
    pallas_call x15, Pallas kernels, call(): pl.pallas_call(kernel, in_specs=[pl.BlockSpec(memory_space=space(n, x)) f...  32.7 us
    ppermute x4, waiting for transfers between devices, swap_traces(): lax.ppermute(cross, 'dom', both(ups))  22.3 us
    ppermute x4, starting transfers between devices, swap_traces(): lax.ppermute(cross, 'dom', both(ups))  9.61 us
  transfers between devices with their start and end apart: 8, of which 4 were waited for; matrix products, arithmetic and copies ran while one was open for 0% of the time, Pallas kernels for 10%

profile of v6, /device:TPU:32, one launch (start us, length us, event | category | flops | bytes accessed | tf_op | source)
XLA Modules:
  0.0 167.7 jit_solution(8342850424563863676)
XLA Ops:
  0.6 7.6 %shard_map.104 = (f32[128,120,128]{2,1,0:T(8,128)}, f32[8,128]{1,0:T(8,128)}) custom-call(s32[1,128]{1,0:T(1,128)} %bitcast.12, f32[1,128]{1,0:T(1,128)} %bitcast.13, f32[1,128]{1,0:T(1,128)} %bitcast.14, f32[1,128]{1,0:T(1,128)} %bitcast.15, s32[1,128]{1,0:T(1,128)} %bitcast.16, s32[1,128]{1,0:T(1,128)} %bitcast.17, s32[1,128]{1,0:T(1,128)} %bitcast.18, ...), custom_call_target="tpu_custom_call" | custom-call | tf_op jit(solution)/shard_map/pallas_call | solution.py:37
  8.2 0.0 copy-start.1
  8.2 0.0 copy-start.2
  8.2 102.0 %all_to_all.5.got_ref.refs_4_.refs_5_ = f32[128,120,128]{2,1,0:T(8,128)S(1)} all-to-all(f32[128,120,128]{2,1,0:T(8,128)} %get-tuple-element.44), channel_id=1, replica_groups=mesh['dom'=128] {'dom'}, dimensions={0} | all-to-all | bytes 15728640 | tf_op jit(solution)/shard_map/all_to_all | solution.py:729
  110.2 0.0 copy-done.1
  110.2 0.0 copy-done.2
  110.2 4.6 %shard_map.105 = (f32[9,64,8,128]{3,2,1,0:T(8,128)S(1)}, f32[9,64,128]{2,1,0:T(8,128)S(1)}, f32[9,64,128]{2,1,0:T(8,128)S(1)}, f32[8,128]{1,0:T(8,128)S(1)}, bf1...) custom-call(f32[8,128]{1,0:T(8,128)S(1)} %copy-done.2, f32[128,120,128]{2,1,0:T(8,128)S(1)} %all_to_all.5.got_ref.refs_4_.refs_5_, ...), custom_call_target="tpu_custom_call" | custom-call | tf_op jit(solution)/shard_map/pallas_call | solution.py:37
  114.8 2.2 %collective-permute-start = (f32[9,64,128]{2,1,0:T(8,128)S(1)}, f32[9,64,128]{2,1,0:T(8,128)S(1)}, u32[]{:S(2)}, u32[]{:S(2)}) collective-permute-start(f32[9,64,128]{2,1,0:T(8,128)S(1)} %get-tuple-element.50.refs_0_), channel_id=1, source_target_pairs={{1,2},{3,4},{5,6},{7,8},{9,10},{11,12},{13,14},{15,16},{17,18},{19... | collective-permute-start | bytes 884744 | tf_op jit(solution)/shard_map/ppermute | solution.py:717
  117.1 0.1 collective-permute-start.1
  117.1 2.5 %shard_map.106 = (f32[9,64,8,128]{3,2,1,0:T(8,128)S(1)}, f32[2,9,8,8,128]{4,3,2,1,0:T(8,128)S(1)}) custom-call(f32[9,64,8,128]{3,2,1,0:T(8,128)S(1)} %get-tuple-element.45.refs_0_, f32[8,128]{1,0:T(8,128)S(1)} %get-tuple-element.46.refs_1_.refs_3_.refs_6_.refs_2_.refs_4_.rows_ref), custom_call_target="tpu_custom_call" | custom-call | tf_op jit(solution)/shard_map/pallas_call | solution.py:37
  119.6 0.9 shard_map.107
  120.5 6.6 %collective-permute-done.refs_2_ = f32[9,64,128]{2,1,0:T(8,128)S(1)} collective-permute-done((f32[9,64,128]{2,1,0:T(8,128)S(1)}, f32[9,64,128]{2,1,0:T(8,128)S(1)}, u32[]{:S(2)}, u32[]{:S(2)}) %collective-permute-start) | collective-permute-done | bytes 294944 | tf_op jit(solution)/shard_map/ppermute | solution.py:717
  127.1 0.0 collective-permute-done.1.refs_3_
  127.1 0.3 shard_map.108
  127.4 2.2 %collective-permute-start.2 = (f32[9,64,128]{2,1,0:T(8,128)S(1)}, f32[9,64,128]{2,1,0:T(8,128)S(1)}, u32[]{:S(2)}, u32[]{:S(2)}) collective-permute-start(f32[9,64,128]{2,1,0:T(8,128)S(1)} %get-tuple-element.59.refs_0_), channel_id=1, source_target_pairs={{1,2},{3,4},{5,6},{7,8},{9,10},{11,12},{13,14},{15,16},{17,18},{19... | collective-permute-start | bytes 884744 | tf_op jit(solution)/shard_map/ppermute | solution.py:717
  129.7 0.1 collective-permute-start.3
  129.8 2.7 %shard_map.109 = (f32[9,64,8,128]{3,2,1,0:T(8,128)S(1)}, f32[9,64,8,128]{3,2,1,0:T(8,128)S(1)}, f32[2,9,8,8,128]{4,3,2,1,0:T(8,128)S(1)}) custom-call(f32[9,64,8,128]{3,2,1,0:T(8,128)S(1)} %get-tuple-element.49.refs_0_, f32[2,9,64,128]{3,2,1,0:T(8,128)S(1)} %get-tuple-element.54.refs_1_, ...), custom_call_target="tpu_custom_call" | custom-call | tf_op jit(solution)/shard_map/pallas_call | solution.py:37
  132.5 1.0 shard_map.110
  133.5 0.0 copy-start
  133.5 6.2 %collective-permute-done.2.refs_2_ = f32[9,64,128]{2,1,0:T(8,128)S(1)} collective-permute-done((f32[9,64,128]{2,1,0:T(8,128)S(1)}, f32[9,64,128]{2,1,0:T(8,128)S(1)}, u32[]{:S(2)}, u32[]{:S(2)}) %collective-permute-start.2) | collective-permute-done | bytes 294944 | tf_op jit(solution)/shard_map/ppermute | solution.py:717
  139.7 0.0 collective-permute-done.3.refs_3_
  139.7 0.3 shard_map.111
  140.0 2.2 %collective-permute-start.4 = (f32[9,64,128]{2,1,0:T(8,128)S(1)}, f32[9,64,128]{2,1,0:T(8,128)S(1)}, u32[]{:S(2)}, u32[]{:S(2)}) collective-permute-start(f32[9,64,128]{2,1,0:T(8,128)S(1)} %get-tuple-element.68.refs_0_), channel_id=1, source_target_pairs={{1,2},{3,4},{5,6},{7,8},{9,10},{11,12},{13,14},{15,16},{17,18},{19... | collective-permute-start | bytes 884744 | tf_op jit(solution)/shard_map/ppermute | solution.py:717
  142.3 0.1 collective-permute-start.5
  142.4 0.0 copy-done
  142.4 1.7 shard_map.114.strain_ref
  144.0 2.7 %shard_map.112 = (f32[9,64,8,128]{3,2,1,0:T(8,128)S(1)}, f32[9,64,8,128]{3,2,1,0:T(8,128)S(1)}, f32[2,9,8,8,128]{4,3,2,1,0:T(8,128)S(1)}) custom-call(f32[9,64,8,128]{3,2,1,0:T(8,128)S(1)} %get-tuple-element.58.refs_0_, f32[2,9,64,128]{3,2,1,0:T(8,128)S(1)} %get-tuple-element.63.refs_1_, ...), custom_call_target="tpu_custom_call" | custom-call | tf_op jit(solution)/shard_map/pallas_call | solution.py:37
  146.8 0.8 shard_map.113
  147.6 4.7 %collective-permute-done.4.refs_2_ = f32[9,64,128]{2,1,0:T(8,128)S(1)} collective-permute-done((f32[9,64,128]{2,1,0:T(8,128)S(1)}, f32[9,64,128]{2,1,0:T(8,128)S(1)}, u32[]{:S(2)}, u32[]{:S(2)}) %collective-permute-start.4) | collective-permute-done | bytes 294944 | tf_op jit(solution)/shard_map/ppermute | solution.py:717
  152.3 0.0 collective-permute-done.5.refs_3_
  152.3 0.3 shard_map.115
  152.6 2.9 %collective-permute-start.6 = (f32[9,64,128]{2,1,0:T(8,128)S(1)}, f32[9,64,128]{2,1,0:T(8,128)S(1)}, u32[]{:S(2)}, u32[]{:S(2)}) collective-permute-start(f32[9,64,128]{2,1,0:T(8,128)S(1)} %get-tuple-element.79.cross_ref), channel_id=1, source_target_pairs={{1,2},{3,4},{5,6},{7,8},{9,10},{11,12},{13,14},{15,16},{17,18},{19... | collective-permute-start | bytes 884744 | tf_op jit(solution)/shard_map/ppermute | solution.py:717
  155.6 0.1 collective-permute-start.7
  155.7 1.7 shard_map.117.first_ref
  157.3 2.7 %shard_map.116 = (f32[9,64,8,128]{3,2,1,0:T(8,128)S(1)}, f32[9,64,8,128]{3,2,1,0:T(8,128)S(1)}, f32[2,9,8,8,128]{4,3,2,1,0:T(8,128)S(1)}) custom-call(f32[9,64,8,128]{3,2,1,0:T(8,128)S(1)} %get-tuple-element.67.refs_0_, f32[2,9,64,128]{3,2,1,0:T(8,128)S(1)} %get-tuple-element.75.refs_1_, ...), custom_call_target="tpu_custom_call" | custom-call | tf_op jit(solution)/shard_map/pallas_call | solution.py:37
  160.1 4.8 %collective-permute-done.6.got_cross_ref = f32[9,64,128]{2,1,0:T(8,128)S(1)} collective-permute-done((f32[9,64,128]{2,1,0:T(8,128)S(1)}, f32[9,64,128]{2,1,0:T(8,128)S(1)}, u32[]{:S(2)}, u32[]{:S(2)}) %collective-permute-start.6) | collective-permute-done | bytes 294944 | tf_op jit(solution)/shard_map/ppermute | solution.py:717
  164.9 0.0 collective-permute-done.7.got_paired_ref
  164.9 2.8 %shard_map.118 = (f32[9,64,8,128]{3,2,1,0:T(8,128)}, f32[2,128]{1,0:T(2,128)}) custom-call(f32[9,64,8,128]{3,2,1,0:T(8,128)S(1)} %get-tuple-element.64.refs_0_.refs_3_.base_ref, f32[9,64,8,128]{3,2,1,0:T(8,128)S(1)} %get-tuple-element.76.wave_ref, f32[9,64,8,128]{3,2,1,0:T(8,128)S(1)} %get-tuple-element.77.part_ref, ...), custom_call_target="tpu_custom_call" | custom-call | tf_op jit(solution)/shard_map/pallas_call | solution.py:37
Async XLA Ops:
  8.2 102.0 %copy-start.1 = (f32[9,512,128]{2,1,0:T(8,128)S(1)}, f32[9,512,128]{2,1,0:T(8,128)}, u32[]{:S(2)}) copy-start(f32[9,512,128]{2,1,0:T(8,128)} %adj_ref.1) | copy-start | bytes 7077892
  8.2 102.0 %copy-start.2 = (f32[8,128]{1,0:T(8,128)S(1)}, f32[8,128]{1,0:T(8,128)}, u32[]{:S(2)}) copy-start(f32[8,128]{1,0:T(8,128)} %get-tuple-element.43.meta_ref.refs_0_) | copy-start | bytes 12292
  114.8 12.3 %collective-permute-start = (f32[9,64,128]{2,1,0:T(8,128)S(1)}, f32[9,64,128]{2,1,0:T(8,128)S(1)}, u32[]{:S(2)}, u32[]{:S(2)}) collective-permute-start(f32[9,64,128]{2,1,0:T(8,128)S(1)} %get-tuple-element.50.refs_0_), channel_id=1, source_target_pairs={{1,2},{3,4},{5,6},{7,8},{9,10},{11,12},{13,14},{15,16},{17,18},{19... | collective-permute-start | bytes 884744 | tf_op jit(solution)/shard_map/ppermute | solution.py:717
  117.1 10.0 %collective-permute-start.1 = (f32[9,64,128]{2,1,0:T(8,128)S(1)}, f32[9,64,128]{2,1,0:T(8,128)S(1)}, u32[]{:S(2)}, u32[]{:S(2)}) collective-permute-start(f32[9,64,128]{2,1,0:T(8,128)S(1)} %get-tuple-element.51.refs_1_), channel_id=1, source_target_pairs={{0,1},{2,3},{4,5},{6,7},{8,9},{10,11},{12,13},{14,15},{16,17},{18,... | collective-permute-start | bytes 884744 | tf_op jit(solution)/shard_map/ppermute | solution.py:717
  127.4 12.3 %collective-permute-start.2 = (f32[9,64,128]{2,1,0:T(8,128)S(1)}, f32[9,64,128]{2,1,0:T(8,128)S(1)}, u32[]{:S(2)}, u32[]{:S(2)}) collective-permute-start(f32[9,64,128]{2,1,0:T(8,128)S(1)} %get-tuple-element.59.refs_0_), channel_id=1, source_target_pairs={{1,2},{3,4},{5,6},{7,8},{9,10},{11,12},{13,14},{15,16},{17,18},{19... | collective-permute-start | bytes 884744 | tf_op jit(solution)/shard_map/ppermute | solution.py:717
  129.7 10.0 %collective-permute-start.3 = (f32[9,64,128]{2,1,0:T(8,128)S(1)}, f32[9,64,128]{2,1,0:T(8,128)S(1)}, u32[]{:S(2)}, u32[]{:S(2)}) collective-permute-start(f32[9,64,128]{2,1,0:T(8,128)S(1)} %get-tuple-element.60.refs_1_), channel_id=1, source_target_pairs={{0,1},{2,3},{4,5},{6,7},{8,9},{10,11},{12,13},{14,15},{16,17},{18,... | collective-permute-start | bytes 884744 | tf_op jit(solution)/shard_map/ppermute | solution.py:717
  133.5 8.9 %copy-start = (f32[2,3,512,128]{3,2,1,0:T(8,128)S(1)}, f32[2,3,512,128]{3,2,1,0:T(8,128)}, u32[]{:S(2)}) copy-start(f32[2,3,512,128]{3,2,1,0:T(8,128)} %param.10) | copy-start | bytes 4718596
  140.0 12.3 %collective-permute-start.4 = (f32[9,64,128]{2,1,0:T(8,128)S(1)}, f32[9,64,128]{2,1,0:T(8,128)S(1)}, u32[]{:S(2)}, u32[]{:S(2)}) collective-permute-start(f32[9,64,128]{2,1,0:T(8,128)S(1)} %get-tuple-element.68.refs_0_), channel_id=1, source_target_pairs={{1,2},{3,4},{5,6},{7,8},{9,10},{11,12},{13,14},{15,16},{17,18},{19... | collective-permute-start | bytes 884744 | tf_op jit(solution)/shard_map/ppermute | solution.py:717
  142.3 10.0 %collective-permute-start.5 = (f32[9,64,128]{2,1,0:T(8,128)S(1)}, f32[9,64,128]{2,1,0:T(8,128)S(1)}, u32[]{:S(2)}, u32[]{:S(2)}) collective-permute-start(f32[9,64,128]{2,1,0:T(8,128)S(1)} %get-tuple-element.69.refs_1_), channel_id=1, source_target_pairs={{0,1},{2,3},{4,5},{6,7},{8,9},{10,11},{12,13},{14,15},{16,17},{18,... | collective-permute-start | bytes 884744 | tf_op jit(solution)/shard_map/ppermute | solution.py:717
  152.6 12.3 %collective-permute-start.6 = (f32[9,64,128]{2,1,0:T(8,128)S(1)}, f32[9,64,128]{2,1,0:T(8,128)S(1)}, u32[]{:S(2)}, u32[]{:S(2)}) collective-permute-start(f32[9,64,128]{2,1,0:T(8,128)S(1)} %get-tuple-element.79.cross_ref), channel_id=1, source_target_pairs={{1,2},{3,4},{5,6},{7,8},{9,10},{11,12},{13,14},{15,16},{17,18},{19... | collective-permute-start | bytes 884744 | tf_op jit(solution)/shard_map/ppermute | solution.py:717
  155.6 9.3 %collective-permute-start.7 = (f32[9,64,128]{2,1,0:T(8,128)S(1)}, f32[9,64,128]{2,1,0:T(8,128)S(1)}, u32[]{:S(2)}, u32[]{:S(2)}) collective-permute-start(f32[9,64,128]{2,1,0:T(8,128)S(1)} %get-tuple-element.80.paired_ref), channel_id=1, source_target_pairs={{0,1},{2,3},{4,5},{6,7},{8,9},{10,11},{12,13},{14,15},{16,17},{18,... | collective-permute-start | bytes 884744 | tf_op jit(solution)/shard_map/ppermute | solution.py:717

commit v7 on v6

--- a/solution.py
+++ b/solution.py
@@ -116,7 +116,7 @@
         return jnp.concatenate([jnp.where(first_row, row, block[0:8]), block[8:]], axis=0)
 
     leave, b = [], 0
-    for count in (3, 3, 3, 3, 2, 1):
+    for count in (3, 5, 4, 2, 1):
         scatter_rows(hot_ref[...], [load(b + n) for n in range(count)], out_ref, b * 8)
         rows = pl.ds(b * 8, count * 8)
         leave.append(
@@ -532,9 +532,8 @@
 
 
 def finish_kernel(
-    base_ref, wave_ref, part_ref, flux_ref, cross_ref, paired_ref, got_cross_ref,
-    got_paired_ref, rows_ref, strain_ref, first_ref, out_hbm, gradient_ref,
-    out_ref, fluxz_ref, sums_ref, out_sem,
+    begun_ref, cross_ref, paired_ref, got_cross_ref, got_paired_ref, rows_ref, strain_ref,
+    first_ref, out_hbm, gradient_ref, out_ref, fluxz_ref, sums_ref, out_sem,
 ):
     rinv, lam, mu, speed = materials(rows_ref)
     order = jnp.broadcast_to(rows_ref[4:5, :], (NP, NE))
@@ -550,8 +549,6 @@
 
     @pl.loop(0, NP)
     def _(i):
-        parity = lax.rem(i, 2)
-        factor_x = (2 * i + 1).astype(f32)
         at = pl.multiple_of(i * NP, NP)
         rows = pl.ds(at, NP)
         total, difference = [], []
@@ -565,8 +562,8 @@
             fluxz_ref[0, f] = even[f]
             fluxz_ref[1, f] = odds[f]
 
-        masks = order_masks(order, k, i, 0.5 * DT)
-        flip_x = ((orient == 1.0) | (orient == 3.0)) & (parity == 1)
+        scales = [factor_z * mask for mask in order_masks(order, k, i, 0.5 * DT)]
+        flip_x = ((orient == 1.0) | (orient == 3.0)) & (lax.rem(i, 2) == 1)
         sign_x = jnp.where(flip_x, -1.0, 1.0)
         sign_y = jnp.where(orient >= 2.0, -1.0, 1.0)
         signs = [sign_x, sign_x * sign_y]
@@ -574,9 +571,7 @@
         for f in range(FIELDS):
             for j in range(NP):
                 lifted = lifted_row(fluxz_ref, f, j, k)
-                slope = part_ref[f, at + j] + factor_x * flux_ref[parity, f, j] + factor_z * lifted
-                start = 0.5 * (base_ref[f, at + j] + wave_ref[f, at + j])
-                new = start + masks[j] * slope
+                new = begun_ref[f, at + j] + scales[j] * lifted
                 out_ref[f, at + j] = new * signs[j % 2]
                 if f >= 3:
                     stresses[j].append(new)
@@ -589,10 +584,10 @@
         leave(i).wait()
 
 
-def finish(base, wave, part, flux, traces, got, rows, strain, first):
+def finish(begun, traces, got, rows, strain, first):
     return call(
         finish_kernel,
-        [base, wave, part, flux, *traces, *got, rows, strain, first],
+        [begun, *traces, *got, rows, strain, first],
         [array(FIELDS, 64, NP, NE), array(2, NE)],
         [
             pltpu.VMEM((FIELDS, 64, NP, NE), f32),
@@ -745,9 +740,8 @@
             start, base = wave, None
     first = velocities(meta, pick, frame, start, snaps, got)
     got_traces = swap_traces(*traces)
-    signed, gradients = finish(
-        base, wave, part, flux, traces, got_traces, rows, strain, first
-    )
+    begun, *_ = begin(base, wave, part, flux, rows)
+    signed, gradients = finish(begun, traces, got_traces, rows, strain, first)
     return signed.reshape(FIELDS, NM, NE), gradients
 
 

time: 168 us -> 168 us (level)
  waiting for transfers between devices: 22.3 us -> 20.3 us
    ppermute x4, waiting for transfers between devices: 22.3 us -> 20.3 us  [swap_traces(): lax.ppermute(cross, 'dom', both(ups))]
    pallas_call x15 -> x16, Pallas kernels: 32.7 us -> 34.2 us  [call(): pl.pallas_call(kernel, in_specs=[pl.BlockSpec(memory_space=space(n, x)) f...]
  transfers between devices with their start and end apart: 8 -> 8, of which waited for: 4 -> 4; matrix products, arithmetic and copies ran while one was open for 0% -> 0% of each run, Pallas kernels for 10% -> 11%
where the time goes in v7:
time: 168 us; the launch traced here: 167 us
  blocking collectives  102 us (61%)
  Pallas kernels  34.2 us (20%)
  waiting for transfers between devices  20.3 us (12%)
  starting transfers between devices  9.93 us (6%)
    all_to_all x1, blocking collectives, body(): got = lax.all_to_all(send, 'dom', split_axis=0, concat_axis=0, tiled=True)  102 us
    pallas_call x16, Pallas kernels, call(): pl.pallas_call(kernel, in_specs=[pl.BlockSpec(memory_space=space(n, x)) f...  34.2 us
    ppermute x4, waiting for transfers between devices, swap_traces(): lax.ppermute(cross, 'dom', both(ups))  20.3 us
    ppermute x4, starting transfers between devices, swap_traces(): lax.ppermute(cross, 'dom', both(ups))  9.59 us
  transfers between devices with their start and end apart: 8, of which 4 were waited for; matrix products, arithmetic and copies ran while one was open for 0% of the time, Pallas kernels for 11%

profile of v7, /device:TPU:32, one launch (start us, length us, event | category | flops | bytes accessed | tf_op | source)
XLA Modules:
  0.0 167.3 jit_solution(8327486302464265139)
XLA Ops:
  0.6 7.6 %shard_map.104 = (f32[128,120,128]{2,1,0:T(8,128)}, f32[8,128]{1,0:T(8,128)}) custom-call(s32[1,128]{1,0:T(1,128)} %bitcast.12, f32[1,128]{1,0:T(1,128)} %bitcast.13, f32[1,128]{1,0:T(1,128)} %bitcast.14, f32[1,128]{1,0:T(1,128)} %bitcast.15, s32[1,128]{1,0:T(1,128)} %bitcast.16, s32[1,128]{1,0:T(1,128)} %bitcast.17, s32[1,128]{1,0:T(1,128)} %bitcast.18, ...), custom_call_target="tpu_custom_call" | custom-call | tf_op jit(solution)/shard_map/pallas_call | solution.py:37
  8.2 0.0 copy-start.1
  8.2 0.0 copy-start.2
  8.2 102.0 %all_to_all.5.got_ref.refs_4_.refs_5_ = f32[128,120,128]{2,1,0:T(8,128)S(1)} all-to-all(f32[128,120,128]{2,1,0:T(8,128)} %get-tuple-element.45), channel_id=1, replica_groups=mesh['dom'=128] {'dom'}, dimensions={0} | all-to-all | bytes 15728640 | tf_op jit(solution)/shard_map/all_to_all | solution.py:724
  110.2 0.0 copy-done.1
  110.2 0.0 copy-done.2
  110.2 4.6 %shard_map.105 = (f32[9,64,8,128]{3,2,1,0:T(8,128)S(1)}, f32[9,64,128]{2,1,0:T(8,128)S(1)}, f32[9,64,128]{2,1,0:T(8,128)S(1)}, f32[8,128]{1,0:T(8,128)S(1)}, bf1...) custom-call(f32[8,128]{1,0:T(8,128)S(1)} %copy-done.2, f32[128,120,128]{2,1,0:T(8,128)S(1)} %all_to_all.5.got_ref.refs_4_.refs_5_, ...), custom_call_target="tpu_custom_call" | custom-call | tf_op jit(solution)/shard_map/pallas_call | solution.py:37
  114.8 2.2 %collective-permute-start = (f32[9,64,128]{2,1,0:T(8,128)S(1)}, f32[9,64,128]{2,1,0:T(8,128)S(1)}, u32[]{:S(2)}, u32[]{:S(2)}) collective-permute-start(f32[9,64,128]{2,1,0:T(8,128)S(1)} %get-tuple-element.51.refs_0_), channel_id=1, source_target_pairs={{1,2},{3,4},{5,6},{7,8},{9,10},{11,12},{13,14},{15,16},{17,18},{19... | collective-permute-start | bytes 884744 | tf_op jit(solution)/shard_map/ppermute | solution.py:712
  117.1 0.1 collective-permute-start.1
  117.2 2.5 %shard_map.106 = (f32[9,64,8,128]{3,2,1,0:T(8,128)S(1)}, f32[2,9,8,8,128]{4,3,2,1,0:T(8,128)S(1)}) custom-call(f32[9,64,8,128]{3,2,1,0:T(8,128)S(1)} %get-tuple-element.46.refs_0_, f32[8,128]{1,0:T(8,128)S(1)} %get-tuple-element.47.refs_1_.refs_3_.refs_6_.refs_2_.refs_4_.rows_ref), custom_call_target="tpu_custom_call" | custom-call | tf_op jit(solution)/shard_map/pallas_call | solution.py:37
  119.6 0.9 shard_map.107
  120.5 6.6 %collective-permute-done.refs_2_ = f32[9,64,128]{2,1,0:T(8,128)S(1)} collective-permute-done((f32[9,64,128]{2,1,0:T(8,128)S(1)}, f32[9,64,128]{2,1,0:T(8,128)S(1)}, u32[]{:S(2)}, u32[]{:S(2)}) %collective-permute-start) | collective-permute-done | bytes 294944 | tf_op jit(solution)/shard_map/ppermute | solution.py:712
  127.1 0.0 collective-permute-done.1.refs_3_
  127.1 0.3 shard_map.108
  127.5 2.2 %collective-permute-start.2 = (f32[9,64,128]{2,1,0:T(8,128)S(1)}, f32[9,64,128]{2,1,0:T(8,128)S(1)}, u32[]{:S(2)}, u32[]{:S(2)}) collective-permute-start(f32[9,64,128]{2,1,0:T(8,128)S(1)} %get-tuple-element.60.refs_0_), channel_id=1, source_target_pairs={{1,2},{3,4},{5,6},{7,8},{9,10},{11,12},{13,14},{15,16},{17,18},{19... | collective-permute-start | bytes 884744 | tf_op jit(solution)/shard_map/ppermute | solution.py:712
  129.7 0.1 collective-permute-start.3
  129.8 2.7 %shard_map.109 = (f32[9,64,8,128]{3,2,1,0:T(8,128)S(1)}, f32[9,64,8,128]{3,2,1,0:T(8,128)S(1)}, f32[2,9,8,8,128]{4,3,2,1,0:T(8,128)S(1)}) custom-call(f32[9,64,8,128]{3,2,1,0:T(8,128)S(1)} %get-tuple-element.50.refs_0_, f32[2,9,64,128]{3,2,1,0:T(8,128)S(1)} %get-tuple-element.55.refs_1_, ...), custom_call_target="tpu_custom_call" | custom-call | tf_op jit(solution)/shard_map/pallas_call | solution.py:37
  132.5 1.1 shard_map.110
  133.6 0.0 copy-start
  133.6 6.1 %collective-permute-done.2.refs_2_ = f32[9,64,128]{2,1,0:T(8,128)S(1)} collective-permute-done((f32[9,64,128]{2,1,0:T(8,128)S(1)}, f32[9,64,128]{2,1,0:T(8,128)S(1)}, u32[]{:S(2)}, u32[]{:S(2)}) %collective-permute-start.2) | collective-permute-done | bytes 294944 | tf_op jit(solution)/shard_map/ppermute | solution.py:712
  139.7 0.0 collective-permute-done.3.refs_3_
  139.7 0.4 shard_map.111
  140.1 2.2 %collective-permute-start.4 = (f32[9,64,128]{2,1,0:T(8,128)S(1)}, f32[9,64,128]{2,1,0:T(8,128)S(1)}, u32[]{:S(2)}, u32[]{:S(2)}) collective-permute-start(f32[9,64,128]{2,1,0:T(8,128)S(1)} %get-tuple-element.69.refs_0_), channel_id=1, source_target_pairs={{1,2},{3,4},{5,6},{7,8},{9,10},{11,12},{13,14},{15,16},{17,18},{19... | collective-permute-start | bytes 884744 | tf_op jit(solution)/shard_map/ppermute | solution.py:712
  142.3 0.1 collective-permute-start.5
  142.4 0.0 copy-done
  142.4 1.7 shard_map.114.strain_ref
  144.1 2.7 %shard_map.112 = (f32[9,64,8,128]{3,2,1,0:T(8,128)S(1)}, f32[9,64,8,128]{3,2,1,0:T(8,128)S(1)}, f32[2,9,8,8,128]{4,3,2,1,0:T(8,128)S(1)}) custom-call(f32[9,64,8,128]{3,2,1,0:T(8,128)S(1)} %get-tuple-element.59.refs_0_, f32[2,9,64,128]{3,2,1,0:T(8,128)S(1)} %get-tuple-element.64.refs_1_, ...), custom_call_target="tpu_custom_call" | custom-call | tf_op jit(solution)/shard_map/pallas_call | solution.py:37
  146.8 0.8 shard_map.113
  147.7 4.7 %collective-permute-done.4.refs_2_ = f32[9,64,128]{2,1,0:T(8,128)S(1)} collective-permute-done((f32[9,64,128]{2,1,0:T(8,128)S(1)}, f32[9,64,128]{2,1,0:T(8,128)S(1)}, u32[]{:S(2)}, u32[]{:S(2)}) %collective-permute-start.4) | collective-permute-done | bytes 294944 | tf_op jit(solution)/shard_map/ppermute | solution.py:712
  152.4 0.0 collective-permute-done.5.refs_3_
  152.4 0.3 shard_map.115
  152.7 2.9 %collective-permute-start.6 = (f32[9,64,128]{2,1,0:T(8,128)S(1)}, f32[9,64,128]{2,1,0:T(8,128)S(1)}, u32[]{:S(2)}, u32[]{:S(2)}) collective-permute-start(f32[9,64,128]{2,1,0:T(8,128)S(1)} %get-tuple-element.81.cross_ref), channel_id=1, source_target_pairs={{1,2},{3,4},{5,6},{7,8},{9,10},{11,12},{13,14},{15,16},{17,18},{19... | collective-permute-start | bytes 884744 | tf_op jit(solution)/shard_map/ppermute | solution.py:712
  155.6 0.1 collective-permute-start.7
  155.7 1.7 shard_map.118.first_ref
  157.4 2.7 %shard_map.116 = (f32[9,64,8,128]{3,2,1,0:T(8,128)S(1)}, f32[9,64,8,128]{3,2,1,0:T(8,128)S(1)}, f32[2,9,8,8,128]{4,3,2,1,0:T(8,128)S(1)}) custom-call(f32[9,64,8,128]{3,2,1,0:T(8,128)S(1)} %get-tuple-element.68.refs_0_, f32[2,9,64,128]{3,2,1,0:T(8,128)S(1)} %get-tuple-element.76.refs_1_, ...), custom_call_target="tpu_custom_call" | custom-call | tf_op jit(solution)/shard_map/pallas_call | solution.py:37
  160.1 1.9 %shard_map.117 = (f32[9,64,8,128]{3,2,1,0:T(8,128)S(1)}, f32[9,64,128]{2,1,0:T(8,128)}, f32[9,64,128]{2,1,0:T(8,128)}) custom-call(f32[9,64,8,128]{3,2,1,0:T(8,128)S(1)} %get-tuple-element.65.refs_0_.refs_3_, f32[9,64,8,128]{3,2,1,0:T(8,128)S(1)} %get-tuple-element.77.refs_1_, f32[9,64,8,128]{3,2,1,0:T(8,128)S(1)} %get-tuple-element.78.refs_2_, ...), custom_call_target="tpu_custom_call" | custom-call | tf_op jit(solution)/shard_map/pallas_call | solution.py:37
  162.1 2.9 %collective-permute-done.6.got_cross_ref = f32[9,64,128]{2,1,0:T(8,128)S(1)} collective-permute-done((f32[9,64,128]{2,1,0:T(8,128)S(1)}, f32[9,64,128]{2,1,0:T(8,128)S(1)}, u32[]{:S(2)}, u32[]{:S(2)}) %collective-permute-start.6) | collective-permute-done | bytes 294944 | tf_op jit(solution)/shard_map/ppermute | solution.py:712
  165.0 0.0 collective-permute-done.7.got_paired_ref
  165.0 2.3 %shard_map.119 = (f32[9,64,8,128]{3,2,1,0:T(8,128)}, f32[2,128]{1,0:T(2,128)}) custom-call(f32[9,64,8,128]{3,2,1,0:T(8,128)S(1)} %get-tuple-element.80.begun_ref, f32[9,64,128]{2,1,0:T(8,128)S(1)} %get-tuple-element.81.cross_ref, f32[9,64,128]{2,1,0:T(8,128)S(1)} %get-tuple-element.82.paired_ref, f32[9,64,128]{2,1,0:T(8,128)S(1)} %collective-permute-done.6.got_cross_ref, ...), custom_call_target="tpu_custom_call" | custom-call | tf_op jit(solution)/shard_map/pallas_call | solution.py:37
Async XLA Ops:
  8.2 102.0 %copy-start.1 = (f32[9,512,128]{2,1,0:T(8,128)S(1)}, f32[9,512,128]{2,1,0:T(8,128)}, u32[]{:S(2)}) copy-start(f32[9,512,128]{2,1,0:T(8,128)} %adj_ref.1) | copy-start | bytes 7077892
  8.2 102.0 %copy-start.2 = (f32[8,128]{1,0:T(8,128)S(1)}, f32[8,128]{1,0:T(8,128)}, u32[]{:S(2)}) copy-start(f32[8,128]{1,0:T(8,128)} %get-tuple-element.44.meta_ref.refs_0_) | copy-start | bytes 12292
  114.8 12.3 %collective-permute-start = (f32[9,64,128]{2,1,0:T(8,128)S(1)}, f32[9,64,128]{2,1,0:T(8,128)S(1)}, u32[]{:S(2)}, u32[]{:S(2)}) collective-permute-start(f32[9,64,128]{2,1,0:T(8,128)S(1)} %get-tuple-element.51.refs_0_), channel_id=1, source_target_pairs={{1,2},{3,4},{5,6},{7,8},{9,10},{11,12},{13,14},{15,16},{17,18},{19... | collective-permute-start | bytes 884744 | tf_op jit(solution)/shard_map/ppermute | solution.py:712
  117.1 10.0 %collective-permute-start.1 = (f32[9,64,128]{2,1,0:T(8,128)S(1)}, f32[9,64,128]{2,1,0:T(8,128)S(1)}, u32[]{:S(2)}, u32[]{:S(2)}) collective-permute-start(f32[9,64,128]{2,1,0:T(8,128)S(1)} %get-tuple-element.52.refs_1_), channel_id=1, source_target_pairs={{0,1},{2,3},{4,5},{6,7},{8,9},{10,11},{12,13},{14,15},{16,17},{18,... | collective-permute-start | bytes 884744 | tf_op jit(solution)/shard_map/ppermute | solution.py:712
  127.5 12.3 %collective-permute-start.2 = (f32[9,64,128]{2,1,0:T(8,128)S(1)}, f32[9,64,128]{2,1,0:T(8,128)S(1)}, u32[]{:S(2)}, u32[]{:S(2)}) collective-permute-start(f32[9,64,128]{2,1,0:T(8,128)S(1)} %get-tuple-element.60.refs_0_), channel_id=1, source_target_pairs={{1,2},{3,4},{5,6},{7,8},{9,10},{11,12},{13,14},{15,16},{17,18},{19... | collective-permute-start | bytes 884744 | tf_op jit(solution)/shard_map/ppermute | solution.py:712
  129.7 10.0 %collective-permute-start.3 = (f32[9,64,128]{2,1,0:T(8,128)S(1)}, f32[9,64,128]{2,1,0:T(8,128)S(1)}, u32[]{:S(2)}, u32[]{:S(2)}) collective-permute-start(f32[9,64,128]{2,1,0:T(8,128)S(1)} %get-tuple-element.61.refs_1_), channel_id=1, source_target_pairs={{0,1},{2,3},{4,5},{6,7},{8,9},{10,11},{12,13},{14,15},{16,17},{18,... | collective-permute-start | bytes 884744 | tf_op jit(solution)/shard_map/ppermute | solution.py:712
  133.6 8.8 %copy-start = (f32[2,3,512,128]{3,2,1,0:T(8,128)S(1)}, f32[2,3,512,128]{3,2,1,0:T(8,128)}, u32[]{:S(2)}) copy-start(f32[2,3,512,128]{3,2,1,0:T(8,128)} %param.10) | copy-start | bytes 4718596
  140.1 12.3 %collective-permute-start.4 = (f32[9,64,128]{2,1,0:T(8,128)S(1)}, f32[9,64,128]{2,1,0:T(8,128)S(1)}, u32[]{:S(2)}, u32[]{:S(2)}) collective-permute-start(f32[9,64,128]{2,1,0:T(8,128)S(1)} %get-tuple-element.69.refs_0_), channel_id=1, source_target_pairs={{1,2},{3,4},{5,6},{7,8},{9,10},{11,12},{13,14},{15,16},{17,18},{19... | collective-permute-start | bytes 884744 | tf_op jit(solution)/shard_map/ppermute | solution.py:712
  142.3 10.0 %collective-permute-start.5 = (f32[9,64,128]{2,1,0:T(8,128)S(1)}, f32[9,64,128]{2,1,0:T(8,128)S(1)}, u32[]{:S(2)}, u32[]{:S(2)}) collective-permute-start(f32[9,64,128]{2,1,0:T(8,128)S(1)} %get-tuple-element.70.refs_1_), channel_id=1, source_target_pairs={{0,1},{2,3},{4,5},{6,7},{8,9},{10,11},{12,13},{14,15},{16,17},{18,... | collective-permute-start | bytes 884744 | tf_op jit(solution)/shard_map/ppermute | solution.py:712
  152.7 12.3 %collective-permute-start.6 = (f32[9,64,128]{2,1,0:T(8,128)S(1)}, f32[9,64,128]{2,1,0:T(8,128)S(1)}, u32[]{:S(2)}, u32[]{:S(2)}) collective-permute-start(f32[9,64,128]{2,1,0:T(8,128)S(1)} %get-tuple-element.81.cross_ref), channel_id=1, source_target_pairs={{1,2},{3,4},{5,6},{7,8},{9,10},{11,12},{13,14},{15,16},{17,18},{19... | collective-permute-start | bytes 884744 | tf_op jit(solution)/shard_map/ppermute | solution.py:712
  155.6 9.3 %collective-permute-start.7 = (f32[9,64,128]{2,1,0:T(8,128)S(1)}, f32[9,64,128]{2,1,0:T(8,128)S(1)}, u32[]{:S(2)}, u32[]{:S(2)}) collective-permute-start(f32[9,64,128]{2,1,0:T(8,128)S(1)} %get-tuple-element.82.paired_ref), channel_id=1, source_target_pairs={{0,1},{2,3},{4,5},{6,7},{8,9},{10,11},{12,13},{14,15},{16,17},{18,... | collective-permute-start | bytes 884744 | tf_op jit(solution)/shard_map/ppermute | solution.py:712
